TPU v7x, 32 devices: a whole 2x2x4 slice. The times are simulated.
32 devices in a mesh: row: 8 (over z, core), pair: 4 (over y, x).
Axes of the slice: x: 2, y: 2, z: 4, core: 2. Of those that a mesh axis runs over, the one named last changes fastest.
Arguments:
- slab: float32 [2048, 2048], P(('row', 'pair'))
- plan: int32 [2, 8], replicated, may hold values from 0 to 7, as said below
Outputs:
- rotated: float32 [2048, 2048], P(('row', 'pair'))
- sing_vals: float32 [2048], replicated
Inputs may be any that keep to these rules, and one draw needn't show every extreme that they name: Each row of plan is a permutation of the block ids; no two blocks form a pair in two rounds, and the two blocks of a pair in round r sit in two different pairs in round r + 1.
All inputs are finite; a program needn't handle non-finite values.
Results may differ from a plain program's by a relative error of at most 0.00017.
Values sent between devices are 32-bit elements; how exact they have to be, the bound alone decides.
No kernel may reach another device: no remote copies, remote signals or barrier semaphores. Data moves between devices by JAX's collectives and lax.ppermute only.
A program may use at most 64 MiB of HBM per device.

v0:
```python
import jax
import jax.numpy as jnp
from jax import lax
from jax.sharding import PartitionSpec as P

ROUNDS = 2
NS_STEPS = 4


HIGH = lax.Precision.HIGHEST


def position(order):
    count = order.shape[0]
    slots = jnp.arange(count, dtype=jnp.int32)
    return jnp.sum(jnp.where(order[None, :] == slots[:, None], slots[None, :], 0), axis=1)


def build_turn(cross, diag_vals, width):
    coupling = cross / (diag_vals[:width, None] + diag_vals[None, width:] + 1e-06)
    zero_part = jnp.zeros((width, width), jnp.float32)
    skew = jnp.concatenate(
        [jnp.concatenate([zero_part, coupling], 1), jnp.concatenate([-coupling.T, zero_part], 1)], 0
    )
    scale_c = jnp.sqrt(1.0 + jnp.sum(coupling * coupling))
    ident = jnp.eye(2 * width, dtype=jnp.float32)
    turn = (ident + skew) / scale_c
    for step in range(NS_STEPS):
        inner = jnp.dot(turn.T, turn, precision=HIGH, preferred_element_type=jnp.float32)
        turn = 0.5 * jnp.dot(
            turn, 3.0 * ident - inner, precision=HIGH, preferred_element_type=jnp.float32
        )
    return turn


def on_device(slab, plan):
    piece_rows, ncols = slab.shape
    pair_count = lax.axis_size("pair")
    nblocks = 2 * pair_count
    width = ncols // nblocks
    mine_index = lax.axis_index("pair")
    pieces = slab.reshape(piece_rows, nblocks, width)
    ordered = jnp.take(pieces, plan[0], axis=1)
    local = lax.all_to_all(ordered, "pair", split_axis=1, concat_axis=0, tiled=True)
    group_rows = local.shape[0]
    local = local.reshape(group_rows, 2 * width)
    for rnd in range(ROUNDS):
        if rnd > 0:
            prev_order = plan[rnd - 1]
            next_order = plan[rnd]
            prev_pos = position(prev_order)
            halves = local.reshape(group_rows, 2, width)
            held = lax.dynamic_slice(prev_order, (2 * mine_index,), (2,))
            target = position(next_order)[held] // 2
            owners = jnp.arange(pair_count, dtype=jnp.int32)[:, None, None]
            outgoing = jnp.where(owners == target[0], halves[None, :, 0, :], 0.0) + jnp.where(
                owners == target[1], halves[None, :, 1, :], 0.0
            )
            arrived = lax.all_to_all(outgoing, "pair", split_axis=0, concat_axis=0, tiled=True)
            wanted = lax.dynamic_slice(next_order, (2 * mine_index,), (2,))
            sources = prev_pos[wanted] // 2
            chosen = jnp.take(arrived, sources, axis=0)
            local = jnp.moveaxis(chosen, 0, 1).reshape(group_rows, 2 * width)
        partial_cross = jnp.dot(
            local[:, :width].T, local[:, width:], precision=HIGH, preferred_element_type=jnp.float32
        )
        partial_diag = jnp.sum(local * local, axis=0)
        cross, diag_vals = lax.psum((partial_cross, partial_diag), "row")
        turn = build_turn(cross, diag_vals, width)
        local = jnp.dot(local, turn, precision=HIGH, preferred_element_type=jnp.float32)
    last_pos = position(plan[ROUNDS - 1])
    back_rows = lax.all_to_all(
        local.reshape(group_rows, 2, width), "pair", split_axis=0, concat_axis=1, tiled=True
    )
    rotated = jnp.take(back_rows, last_pos, axis=1).reshape(piece_rows, ncols)
    squares = lax.psum(jnp.sum(local * local, axis=0), "row")
    scaled = jnp.sqrt(squares / (lax.axis_size("row") * group_rows))
    every = lax.all_gather(scaled, "pair", axis=0, tiled=True)
    sing_vals = jnp.take(every.reshape(nblocks, width), last_pos, axis=0).reshape(ncols)
    return (rotated, sing_vals)


def solution(mesh):
    in_specs = (P(("row", "pair"), None), P())
    out_specs = (P(("row", "pair"), None), P())
    return jax.shard_map(
        on_device, mesh=mesh, in_specs=in_specs, out_specs=out_specs, check_vma=False
    )
```

profile of v0, /device:TPU:0, one launch (start us, length us, event | category | flops | bytes accessed | tf_op | source)
XLA Modules:
  0.0 233.1 jit_solution(6092032281203585838)
XLA Ops:
  7.2 0.8 fusion.30
  7.9 0.1 select_reduce_fusion
  8.0 0.6 copy-done
  8.6 1.1 copy.73
  9.7 0.6 gather_fusion.4
  10.3 0.9 select_bitcast_fusion.1
  11.2 5.2 %all-to-all-start = ((f32[64,8,256]{2,0,1:T(8,128)}), f32[64,8,256]{2,0,1:T(8,128)S(1)}, u32[]{:S(2)}, u32[]{:S(2)}) async-start(f32[64,8,256]{2,0,1:T(8,128)} %select_bitcast_fusion.1), calls=%async_computation | async-start | bytes 1048576 | tf_op jit(solution)/shard_map/all_to_all | solution.py:44
  16.4 0.1 fusion.12
  16.5 0.6 gather_fusion.1
  17.1 0.7 fusion.31
  17.8 0.1 select_reduce_fusion.1
  17.9 0.6 gather_fusion
  18.5 0.7 iota_compare_fusion.5
  19.2 0.7 iota_compare_fusion.6
  19.9 4.5 %all-to-all-done = f32[64,8,256]{2,0,1:T(8,128)S(1)} async-done(((f32[64,8,256]{2,0,1:T(8,128)}), f32[64,8,256]{2,0,1:T(8,128)S(1)}, u32[]{:S(2)}, u32[]{:S(2)}) %all-to-all-start) | async-done | bytes 524320 | tf_op jit(solution)/shard_map/all_to_all | solution.py:44
  24.4 0.4 copy.42
  24.8 0.1 multiply_reduce_fusion.2
  24.9 0.4 reshape.255
  25.3 1.3 fusion.5
  26.6 0.0 all-reduce.7.cloned.1.call-update
  26.7 16.0 %psum.36 = f32[512]{0:T(512)S(1)} all-reduce(f32[512]{0:T(512)S(1)} %bitcast.119), channel_id=1, replica_groups=mesh['row'=8,'pair'=4] {'row'}, use_global_device_ids=true, to_apply=%region_4.6 | all-reduce | flops 512 | bytes 4096 | tf_op jit(solution)/shard_map/psum | solution.py:68
  42.7 39.3 %all-reduce.7.cloned.1.call-done = f32[256,256]{1,0:T(8,128)} async-done(((f32[256,256]{1,0:T(8,128)}), f32[256,256]{1,0:T(8,128)}) %all-reduce.7.cloned.1.call-update) | async-done | bytes 262160 | tf_op jit(solution)/shard_map/psum | solution.py:68
  82.0 1.7 multiply_reduce_fusion.4
  83.8 0.1 copy.43
  84.6 1.9 select_subtract_fusion.7
  86.5 3.5 %convolution_multiply_fusion.7 = f32[512,512]{1,0:T(8,128)S(1)} fusion(f32[512,512]{0,1:T(8,128)S(1)} %select_subtract_fusion.7, f32[256,256]{0,1:T(8,128)S(1)} %negate_bitcast_fusion.1, f32[256,256]{0,1:T(8,128)S(1)} %copy.43, f32[]{:T(128)S(6)} %sqrt.9), kind=kOutput, calls=%fused_computation.23 | convolution fusion | flops 1613234176 | bytes 2621444 | tf_op jit(solution)/shard_map/dot_general | solution.py:30
  90.0 1.9 select_subtract_fusion.6
  91.9 1.9 convolution_multiply_fusion.6
  93.7 1.9 select_subtract_fusion.5
  95.6 2.1 convolution_multiply_fusion.5
  97.7 1.9 select_subtract_fusion.4
  99.6 1.9 convolution_multiply_fusion.4
  101.4 1.1 fusion.32
  102.6 1.2 select_add_fusion
  103.7 3.6 %all-to-all-start.1 = ((f32[4,256,256]{2,1,0:T(8,128)}), f32[4,256,256]{2,1,0:T(8,128)S(1)}, u32[]{:S(2)}, u32[]{:S(2)}) async-start(f32[4,256,256]{2,1,0:T(8,128)} %select_add_fusion), calls=%async_computation.1 | async-start | bytes 2097152 | tf_op jit(solution)/shard_map/all_to_all | solution.py:59
  107.5 12.0 %all-to-all-done.1 = f32[4,256,256]{2,1,0:T(8,128)S(1)} async-done(((f32[4,256,256]{2,1,0:T(8,128)}), f32[4,256,256]{2,1,0:T(8,128)S(1)}, u32[]{:S(2)}, u32[]{:S(2)}) %all-to-all-start.1) | async-done | bytes 1048608 | tf_op jit(solution)/shard_map/all_to_all | solution.py:59
  119.4 0.6 gather_fusion.2
  120.0 0.1 multiply_reduce_fusion.1
  120.2 0.2 copy.48
  120.4 1.1 fusion.2
  121.5 0.0 all-reduce.9.cloned.1.call-update
  121.5 14.7 %psum.38 = f32[512]{0:T(512)S(1)} all-reduce(f32[512]{0:T(512)S(1)} %bitcast.120), channel_id=1, replica_groups=mesh['row'=8,'pair'=4] {'row'}, use_global_device_ids=true, to_apply=%region_8.10 | all-reduce | flops 512 | bytes 4096 | tf_op jit(solution)/shard_map/psum | solution.py:68
  136.3 39.4 %all-reduce.9.cloned.1.call-done = f32[256,256]{1,0:T(8,128)} async-done(((f32[256,256]{1,0:T(8,128)}), f32[256,256]{1,0:T(8,128)}) %all-reduce.9.cloned.1.call-update) | async-done | bytes 262160 | tf_op jit(solution)/shard_map/psum | solution.py:68
  175.6 1.7 multiply_reduce_fusion.3
  177.3 0.1 copy.65
  178.2 1.9 select_subtract_fusion.3
  180.1 3.5 %convolution_multiply_fusion.3 = f32[512,512]{1,0:T(8,128)S(1)} fusion(f32[512,512]{0,1:T(8,128)S(1)} %select_subtract_fusion.3, f32[256,256]{0,1:T(8,128)S(1)} %negate_bitcast_fusion, f32[256,256]{0,1:T(8,128)S(1)} %copy.65, f32[]{:T(128)S(6)} %sqrt.10), kind=kOutput, calls=%fused_computation.19 | convolution fusion | flops 1613234176 | bytes 2621444 | tf_op jit(solution)/shard_map/dot_general | solution.py:30
  183.6 1.9 select_subtract_fusion.2
  185.4 1.9 convolution_multiply_fusion.2
  187.3 1.9 select_subtract_fusion.1
  189.2 2.1 convolution_multiply_fusion.1
  191.3 1.9 select_subtract_fusion
  193.2 1.9 convolution_multiply_fusion
  195.1 1.1 multiply_reduce_fusion
  196.2 1.1 reshape.195
  197.3 3.6 %all-to-all-start.2 = ((f32[256,2,256]{2,1,0:T(2,128)}), f32[256,2,256]{2,1,0:T(2,128)S(1)}, u32[]{:S(2)}, u32[]{:S(2)}) async-start(f32[256,2,256]{2,1,0:T(2,128)} %reshape.195), calls=%async_computation.2 | async-start | bytes 1048576 | tf_op jit(solution)/shard_map/all_to_all | solution.py:72
  200.9 13.6 %psum.39 = f32[512]{0:T(512)S(1)} all-reduce(f32[512]{0:T(512)S(1)} %get-tuple-element.23), channel_id=1, replica_groups=mesh['row'=8,'pair'=4] {'row'}, use_global_device_ids=true, to_apply=%region_11.13 | all-reduce | flops 512 | bytes 4096 | tf_op jit(solution)/shard_map/psum | solution.py:76
  214.5 8.6 %all-gather = f32[4,1,512]{2,1,0:T(1,128)S(1)} all-gather(f32[1,1,512]{2,1,0:T(1,128)S(1)} %bitcast.117), channel_id=1, replica_groups=mesh['row'=8,'pair'=4] {'pair'}, dimensions={0}, use_global_device_ids=true | all-gather | bytes 10240 | tf_op jit(solution)/shard_map/all_gather | solution.py:78
  223.1 0.6 gather_fusion.3
  223.7 0.1 select_bitcast_fusion.3
  223.8 0.6 copy.71
  224.5 0.6 gather_fusion.5
  225.1 0.1 select_bitcast_fusion
  225.2 0.8 copy.67
  (29 shorter events, 0.3 us)
Async XLA Ops:
  7.9 0.7 copy-start
  11.2 13.2 %all-to-all-start = ((f32[64,8,256]{2,0,1:T(8,128)}), f32[64,8,256]{2,0,1:T(8,128)S(1)}, u32[]{:S(2)}, u32[]{:S(2)}) async-start(f32[64,8,256]{2,0,1:T(8,128)} %select_bitcast_fusion.1), calls=%async_computation | async-start | bytes 1048576 | tf_op jit(solution)/shard_map/all_to_all | solution.py:44
  16.4 65.7 %all-reduce.7.cloned.1.call-start = ((), (), s32[]{:S(2)}) async-start(), calls=%async_computation.3 | async-start | bytes 524288 | tf_op jit(solution)/shard_map/psum | solution.py:68
  103.7 15.7 %all-to-all-start.1 = ((f32[4,256,256]{2,1,0:T(8,128)}), f32[4,256,256]{2,1,0:T(8,128)S(1)}, u32[]{:S(2)}, u32[]{:S(2)}) async-start(f32[4,256,256]{2,1,0:T(8,128)} %select_add_fusion), calls=%async_computation.1 | async-start | bytes 2097152 | tf_op jit(solution)/shard_map/all_to_all | solution.py:59
  107.4 68.3 %all-reduce.9.cloned.1.call-start = ((), (), s32[]{:S(2)}) async-start(), calls=%async_computation.4 | async-start | bytes 524288 | tf_op jit(solution)/shard_map/psum | solution.py:68
  197.3 27.1 %all-to-all-start.2 = ((f32[256,2,256]{2,1,0:T(2,128)}), f32[256,2,256]{2,1,0:T(2,128)S(1)}, u32[]{:S(2)}, u32[]{:S(2)}) async-start(f32[256,2,256]{2,1,0:T(2,128)} %reshape.195), calls=%async_computation.2 | async-start | bytes 1048576 | tf_op jit(solution)/shard_map/all_to_all | solution.py:72
Sparse Core Ops, SparseCore 0:
  26.8 55.2 all-reduce.6
  121.6 53.9 all-reduce.8
where the time goes:
time: 236 us; the launch traced here: 233 us
  waiting for transfers between devices  95.2 us (40%)
  blocking collectives  52.9 us (22%)
  matrix products  38.2 us (16%)
  between operations  16.1 us (7%)
  starting transfers between devices  12.5 us (5%)
  local copies, waits for them, and re-layouts  10.7 us (5%)
  other arithmetic  7.68 us (3%)
    psum x2, waiting for transfers between devices, on_device(): cross, diag_vals = lax.psum((partial_cross, partial_diag), 'row')  78.7 us
    psum x2, blocking collectives, on_device(): cross, diag_vals = lax.psum((partial_cross, partial_diag), 'row')  30.8 us
    dot_general x8, matrix products, build_turn(): jnp.dot(turn, 3.0 * ident - inner, precision=HIGH, preferred_element_type...  18.6 us
    dot_general x8, matrix products, build_turn(): jnp.dot(turn.T, turn, precision=HIGH, preferred_element_type=jnp.float32)  15 us
    psum x1, blocking collectives, on_device(): squares = lax.psum(jnp.sum(local * local, axis=0), 'row')  13.6 us
    all_to_all x1, waiting for transfers between devices, on_device(): lax.all_to_all(outgoing, 'pair', split_axis=0, concat_axis=0, tiled=True)  12 us
    all_gather x1, blocking collectives, on_device(): every = lax.all_gather(scaled, 'pair', axis=0, tiled=True)  8.57 us
    all_to_all x1, starting transfers between devices, on_device(): lax.all_to_all(ordered, 'pair', split_axis=1, concat_axis=0, tiled=True)  5.16 us
  transfers between devices with their start and end apart: 5, of which 4 were waited for; matrix products, arithmetic and copies ran while one was open for 2% of the time, Pallas kernels for 0%

commit v1 on v0

v1 whole, which is shorter than its diff:
```python
import functools

import jax
import jax.numpy as jnp
from jax import lax
from jax.experimental import pallas as pl
from jax.experimental.pallas import tpu as pltpu
from jax.sharding import PartitionSpec as P

NS_STEPS = 4
PAD = 8

VMEM = pl.BlockSpec(memory_space=pltpu.VMEM)
SMEM = pl.BlockSpec(memory_space=pltpu.SMEM)
ROWS_BY_COLS = (((1,), (0,)), ((), ()))
COLS_BY_COLS = (((0,), (0,)), ((), ()))


def split(x):
    high = x.astype(jnp.bfloat16)
    return high, (x - high.astype(jnp.float32)).astype(jnp.bfloat16)


def mul(a, b, dims=ROWS_BY_COLS):
    dot = functools.partial(lax.dot_general, dimension_numbers=dims, preferred_element_type=jnp.float32)
    return dot(a[0], b[0]) + (dot(a[0], b[1]) + dot(a[1], b[0]))


def where_is(plan_ref, rnd, block, count):
    found = jnp.int32(0)
    for slot in range(count):
        found = jnp.where(plan_ref[rnd, slot] == block, slot // 2, found)
    return found


def deal_kernel(plan_ref, slab_ref, *outs):
    me = lax.axis_index("pair")
    width = outs[0].shape[1] // 2
    for mask, out in enumerate(outs):
        to = me ^ mask
        for half in range(2):
            block = plan_ref[0, 2 * to + half]
            start = pl.multiple_of(block * width, width)
            out[:, half * width : (half + 1) * width] = slab_ref[:, pl.ds(start, width)]


def cross_of(first, second, keep_ref, send_ref, scratch):
    width = first.shape[1]
    scratch[...] = mul(split(first), split(second), COLS_BY_COLS)
    diag = jnp.concatenate(
        [
            jnp.sum(first * first, axis=0, keepdims=True),
            jnp.sum(second * second, axis=0, keepdims=True),
            jnp.zeros((PAD - 2, width), jnp.float32),
        ],
        axis=0,
    )
    core = lax.axis_index("row") & 1
    part = width // 2
    for ref, which in ((keep_ref, core), (send_ref, 1 - core)):
        ref[:part, :] = scratch[pl.ds(pl.multiple_of(which * part, part), part), :]
        ref[part:, :] = diag


def first_cross_kernel(*refs):
    *ins, local_ref, keep_ref, send_ref, scratch = refs
    me = lax.axis_index("pair")
    rows = ins[0].shape[0]
    width = ins[0].shape[1] // 2
    for mask, ref in enumerate(ins):
        local_ref[pl.ds(pl.multiple_of((me ^ mask) * rows, rows), rows), :] = ref[...]
    cross_of(local_ref[:, :width], local_ref[:, width:], keep_ref, send_ref, scratch)


def next_cross_kernel(plan_ref, *refs, rnd):
    *ins, local_ref, keep_ref, send_ref, scratch = refs
    width = ins[0].shape[1]
    count = 2 * len(ins)
    me = lax.axis_index("pair")
    halves = []
    for half in range(2):
        source = where_is(plan_ref, rnd - 1, plan_ref[rnd, 2 * me + half], count)
        block = ins[0][...]
        for mask in range(1, len(ins)):
            block = jnp.where(source == (me ^ mask), ins[mask][...], block)
        local_ref[:, half * width : (half + 1) * width] = block
        halves.append(block)
    cross_of(halves[0], halves[1], keep_ref, send_ref, scratch)


def rotate(mine, other, first, second):
    part, width = mine.shape[0] - PAD, mine.shape[1]
    core = lax.axis_index("row") & 1
    cross = jnp.concatenate(
        [jnp.where(core == 0, mine[:part], other[:part]), jnp.where(core == 0, other[:part], mine[:part])], axis=0
    )
    diag_first = jnp.transpose(jnp.broadcast_to(mine[part : part + 1], (width, width)))
    diag_second = mine[part + 1 : part + 2]
    coupling = cross / (diag_first + diag_second + 1e-06)
    k = split(coupling)
    kt = split(jnp.transpose(coupling))
    inv_sq = 1.0 / (1.0 + jnp.sum(coupling * coupling))
    row_id = lax.broadcasted_iota(jnp.int32, (width, width), 0)
    col_id = lax.broadcasted_iota(jnp.int32, (width, width), 1)
    ident = jnp.where(row_id == col_id, 1.0, 0.0)
    squares = [(ident + mul(k, kt)) * inv_sq, (ident + mul(kt, k)) * inv_sq]
    moved = [first - mul(split(second), kt), second + mul(split(first), k)]
    factors = [None, None]
    for step in range(NS_STEPS):
        for side in range(2):
            near = split(1.5 * ident - 0.5 * squares[side])
            if step == 0:
                factors[side] = 1.5 * ident - 0.5 * squares[side]
            else:
                factors[side] = mul(split(factors[side]), near)
            if step < NS_STEPS - 1:
                squares[side] = mul(split(mul(split(squares[side]), near)), near)
    scale = jnp.sqrt(inv_sq)
    return [mul(split(moved[side]), split(factors[side])) * scale for side in range(2)]


def turn_kernel(plan_ref, mine_ref, other_ref, local_ref, *outs, rnd):
    width = local_ref.shape[1] // 2
    new = rotate(mine_ref[...], other_ref[...], local_ref[:, :width], local_ref[:, width:])
    me = lax.axis_index("pair")
    to = where_is(plan_ref, rnd + 1, plan_ref[rnd, 2 * me], 2 * len(outs))
    for mask, out in enumerate(outs):
        out[...] = jnp.where(to == (me ^ mask), new[0], new[1])


def last_turn_kernel(mine_ref, other_ref, local_ref, *refs):
    *outs, squares_ref, scratch = refs
    width = local_ref.shape[1] // 2
    new = rotate(mine_ref[...], other_ref[...], local_ref[:, :width], local_ref[:, width:])
    scratch[:, :width] = new[0]
    scratch[:, width:] = new[1]
    squares_ref[...] = jnp.concatenate(
        [jnp.sum(part * part, axis=0, keepdims=True) for part in new] + [jnp.zeros((PAD - 2, width), jnp.float32)],
        axis=0,
    )
    me = lax.axis_index("pair")
    rows = outs[0].shape[0]
    for mask, out in enumerate(outs):
        out[...] = scratch[pl.ds(pl.multiple_of((me ^ mask) * rows, rows), rows), :]


def place_kernel(plan_ref, *refs, rnd):
    *ins, out_ref = refs
    width = ins[0].shape[1] // 2
    me = lax.axis_index("pair")
    for mask, ref in enumerate(ins):
        for half in range(2):
            block = plan_ref[rnd, 2 * (me ^ mask) + half]
            start = pl.multiple_of(block * width, width)
            out_ref[:, pl.ds(start, width)] = ref[:, half * width : (half + 1) * width]


def norms_kernel(plan_ref, *refs, rnd, total_rows):
    *ins, out_ref = refs
    width = ins[0].shape[1]
    me = lax.axis_index("pair")
    for mask, ref in enumerate(ins):
        for half in range(2):
            block = plan_ref[rnd, 2 * (me ^ mask) + half]
            start = pl.multiple_of(block * width, width)
            out_ref[:, pl.ds(start, width)] = jnp.sqrt(ref[half : half + 1, :] / total_rows)


def swap(x, axis, mask):
    return lax.ppermute(x, axis, [(i, i ^ mask) for i in range(lax.axis_size(axis))])


def spread(parts):
    return [parts[0]] + [swap(parts[mask], "pair", mask) for mask in range(1, len(parts))]


def tree_sum(parts):
    while len(parts) > 1:
        parts = [a + b for a, b in zip(parts[::2], parts[1::2])]
    return parts[0]


def over_chips(x):
    return tree_sum([x] + [swap(x, "row", mask) for mask in range(2, lax.axis_size("row"), 2)])


def call(kernel, ins, outs, scratch=(), smem=0):
    shapes = [jax.ShapeDtypeStruct(shape, jnp.float32) for shape in outs]
    return pl.pallas_call(
        kernel,
        out_shape=shapes,
        in_specs=[SMEM] * smem + [VMEM] * (len(ins) - smem),
        out_specs=[VMEM] * len(outs),
        scratch_shapes=[pltpu.VMEM(shape, jnp.float32) for shape in scratch],
        compiler_params=pltpu.CompilerParams(vmem_limit_bytes=24 * 2**20),
    )(*ins)


def on_device(slab, plan):
    piece_rows, ncols = slab.shape
    rounds = plan.shape[0]
    pair_count = lax.axis_size("pair")
    width = ncols // (2 * pair_count)
    group_rows = piece_rows * pair_count
    total_rows = group_rows * lax.axis_size("row")
    part = (width // 2 + PAD, width)
    square = (width, width)

    dealt = call(deal_kernel, [plan, slab], [(piece_rows, 2 * width)] * pair_count, smem=1)
    held = spread(dealt)
    for rnd in range(rounds):
        if rnd == 0:
            local, keep, send = call(first_cross_kernel, held, [(group_rows, 2 * width), part, part], [square])
        else:
            local, keep, send = call(
                functools.partial(next_cross_kernel, rnd=rnd),
                [plan] + held,
                [(group_rows, 2 * width), part, part],
                [square],
                smem=1,
            )
        mine = over_chips(keep + swap(send, "row", 1))
        other = swap(mine, "row", 1)
        if rnd < rounds - 1:
            sent = call(
                functools.partial(turn_kernel, rnd=rnd),
                [plan, mine, other, local],
                [(group_rows, width)] * pair_count,
                smem=1,
            )
            held = spread(sent)
    *sent, squares = call(
        last_turn_kernel,
        [mine, other, local],
        [(piece_rows, 2 * width)] * pair_count + [(PAD, width)],
        [(group_rows, 2 * width)],
    )
    back = spread(sent)
    squares = squares + swap(squares, "row", 1)
    squares = spread([over_chips(squares)] * pair_count)
    (rotated,) = call(functools.partial(place_kernel, rnd=rounds - 1), [plan] + back, [(piece_rows, ncols)], smem=1)
    (norms,) = call(
        functools.partial(norms_kernel, rnd=rounds - 1, total_rows=total_rows), [plan] + squares, [(1, ncols)], smem=1
    )
    return rotated, norms.reshape(ncols)


def solution(mesh):
    specs = (P(("row", "pair"), None), P())
    return jax.shard_map(on_device, mesh=mesh, in_specs=specs, out_specs=specs, check_vma=False)
```

time: 236 us -> 94.6 us (0.40); the launches traced: 233 us -> 94.4 us
  blocking collectives: 52.9 us -> 0 us
  waiting for transfers between devices: 95.2 us -> 49.7 us
  matrix products: 38.2 us -> 0 us
  starting transfers between devices: 12.5 us -> 29 us
  between operations: 16.1 us -> 0.75 us
  Pallas kernels: 0 us -> 13.2 us
  local copies, waits for them, and re-layouts: 10.7 us -> 1.72 us
  other arithmetic: 7.68 us -> 0.12 us
    psum x2 -> x0, waiting for transfers between devices: 78.7 us -> none  [on_device(): cross, diag_vals = lax.psum((partial_cross, partial_diag), 'row')]
    ppermute x0 -> x26, waiting for transfers between devices: none -> 49.7 us  [swap(): lax.ppermute(x, axis, [(i, i ^ mask) for i in range(lax.axis_size(axis))])]
    psum x3 -> x0, blocking collectives: 44.3 us -> none  [the longest x2 30.8 us: on_device(): cross, diag_vals = lax.psum((partial_cross, partial_diag), 'row')]
    dot_general x20 -> x0, matrix products: 38.2 us -> none  [the longest x8 18.6 us: build_turn(): jnp.dot(turn, 3.0 * ident - inner, precision=HIGH, preferred_element_type...]
    ppermute x0 -> x26, starting transfers between devices: none -> 29 us  [swap(): lax.ppermute(x, axis, [(i, i ^ mask) for i in range(lax.axis_size(axis))])]
    all_to_all x3 -> x0, waiting for transfers between devices: 16.5 us -> none  [the longest x1 12 us: on_device(): lax.all_to_all(outgoing, 'pair', split_axis=0, concat_axis=0, tiled=True)]
    pallas_call x0 -> x7, Pallas kernels: none -> 13.2 us  [call(): pl.pallas_call(kernel, out_shape=shapes, in_specs=[SMEM] * smem + [VMEM]...]
    all_to_all x3 -> x0, starting transfers between devices: 12.5 us -> none  [the longest x1 5.16 us: on_device(): lax.all_to_all(ordered, 'pair', split_axis=1, concat_axis=0, tiled=True)]
  transfers between devices with their start and end apart: 5 -> 26, of which waited for: 4 -> 16; matrix products, arithmetic and copies ran while one was open for 2% -> 0% of each run, Pallas kernels for 0% -> 1%
where the time goes in v1:
time: 94.6 us; the launch traced here: 94.4 us
  waiting for transfers between devices  49.7 us (53%)
  starting transfers between devices  29 us (31%)
  Pallas kernels  13.2 us (14%)
  local copies, waits for them, and re-layouts  1.72 us (2%)
    ppermute x26, waiting for transfers between devices, swap(): lax.ppermute(x, axis, [(i, i ^ mask) for i in range(lax.axis_size(axis))])  49.7 us
    ppermute x26, starting transfers between devices, swap(): lax.ppermute(x, axis, [(i, i ^ mask) for i in range(lax.axis_size(axis))])  29 us
    pallas_call x7, Pallas kernels, call(): pl.pallas_call(kernel, out_shape=shapes, in_specs=[SMEM] * smem + [VMEM]...  13.2 us
  transfers between devices with their start and end apart: 26, of which 16 were waited for; matrix products, arithmetic and copies ran while one was open for 0% of the time, Pallas kernels for 1%

profile of v1, /device:TPU:0, one launch (start us, length us, event | category | flops | bytes accessed | tf_op | source)
XLA Modules:
  0.0 94.4 jit_solution(21067526850391373)
XLA Ops:
  0.6 0.0 copy-start
  0.6 1.0 %copy-done = f32[64,2048]{1,0:T(8,128)S(1)} copy-done((f32[64,2048]{1,0:T(8,128)S(1)}, f32[64,2048]{1,0:T(8,128)}, u32[]{:S(2)}) %copy-start) | copy-done | bytes 524312
  1.7 0.7 copy-done.1
  2.4 0.6 shard_map.41
  3.0 3.0 %collective-permute-start = (f32[64,512]{1,0:T(8,128)S(1)}, f32[64,512]{1,0:T(8,128)S(1)}, u32[]{:S(2)}, u32[]{:S(2)}) collective-permute-start(f32[64,512]{1,0:T(8,128)S(1)} %get-tuple-element.22), channel_id=1, source_target_pairs={{0,1},{1,0},{2,3},{3,2},{4,5},{5,4},{6,7},{7,6},{8,9},{9,8},{10,11... | collective-permute-start | bytes 393224 | tf_op jit(solution)/shard_map/ppermute | solution.py:170
  6.0 1.5 %collective-permute-start.1 = (f32[64,512]{1,0:T(8,128)S(1)}, f32[64,512]{1,0:T(8,128)S(1)}, u32[]{:S(2)}, u32[]{:S(2)}) collective-permute-start(f32[64,512]{1,0:T(8,128)S(1)} %get-tuple-element.23), channel_id=1, source_target_pairs={{0,2},{1,3},{2,0},{3,1},{4,6},{5,7},{6,4},{7,5},{8,10},{9,11},{10,... | collective-permute-start | bytes 393224 | tf_op jit(solution)/shard_map/ppermute | solution.py:170
  7.5 0.0 collective-permute-start.2
  7.5 2.4 %collective-permute-done.refs_1_ = f32[64,512]{1,0:T(8,128)S(1)} collective-permute-done((f32[64,512]{1,0:T(8,128)S(1)}, f32[64,512]{1,0:T(8,128)S(1)}, u32[]{:S(2)}, u32[]{:S(2)}) %collective-permute-start) | collective-permute-done | bytes 131104 | tf_op jit(solution)/shard_map/ppermute | solution.py:170
  9.9 3.9 %collective-permute-done.1.refs_2_ = f32[64,512]{1,0:T(8,128)S(1)} collective-permute-done((f32[64,512]{1,0:T(8,128)S(1)}, f32[64,512]{1,0:T(8,128)S(1)}, u32[]{:S(2)}, u32[]{:S(2)}) %collective-permute-start.1) | collective-permute-done | bytes 131104 | tf_op jit(solution)/shard_map/ppermute | solution.py:170
  13.7 0.0 collective-permute-done.2.refs_3_
  13.7 0.4 shard_map.42
  14.1 0.1 collective-permute-start.3
  14.2 1.3 %collective-permute-done.3 = f32[136,256]{1,0:T(8,128)S(1)} collective-permute-done((f32[136,256]{1,0:T(8,128)S(1)}, f32[136,256]{1,0:T(8,128)S(1)}, u32[]{:S(2)}, u32[]{:S(2)}) %collective-permute-start.3) | collective-permute-done | bytes 139296 | tf_op jit(solution)/shard_map/ppermute | solution.py:170
  15.6 3.7 %collective-permute-start.6 = (f32[136,256]{1,0:T(8,128)S(1)}, f32[136,256]{1,0:T(8,128)S(1)}, u32[]{:S(2)}, u32[]{:S(2)}) collective-permute-start(f32[136,256]{1,0:T(8,128)S(1)} %add.36), channel_id=1, source_target_pairs={{0,24},{4,28},{8,16},{12,20},{16,8},{20,12},{24,0},{28,4},{1,25},{... | collective-permute-start | bytes 417800 | tf_op jit(solution)/shard_map/ppermute | solution.py:170
  19.3 0.0 collective-permute-start.5
  19.3 0.8 collective-permute-start.4
  20.0 4.0 %collective-permute-done.6 = f32[136,256]{1,0:T(8,128)S(1)} collective-permute-done((f32[136,256]{1,0:T(8,128)S(1)}, f32[136,256]{1,0:T(8,128)S(1)}, u32[]{:S(2)}, u32[]{:S(2)}) %collective-permute-start.6) | collective-permute-done | bytes 139296 | tf_op jit(solution)/shard_map/ppermute | solution.py:170
  24.1 7.3 %collective-permute-done.5 = f32[136,256]{1,0:T(8,128)S(1)} collective-permute-done((f32[136,256]{1,0:T(8,128)S(1)}, f32[136,256]{1,0:T(8,128)S(1)}, u32[]{:S(2)}, u32[]{:S(2)}) %collective-permute-start.5) | collective-permute-done | bytes 139296 | tf_op jit(solution)/shard_map/ppermute | solution.py:170
  31.4 0.0 collective-permute-done.4
  31.4 0.0 copy-start.2
  31.4 0.1 collective-permute-start.7
  31.5 1.3 %collective-permute-done.7.other_ref = f32[136,256]{1,0:T(8,128)S(1)} collective-permute-done((f32[136,256]{1,0:T(8,128)S(1)}, f32[136,256]{1,0:T(8,128)S(1)}, u32[]{:S(2)}, u32[]{:S(2)}) %collective-permute-start.7) | collective-permute-done | bytes 139296 | tf_op jit(solution)/shard_map/ppermute | solution.py:170
  32.8 0.0 copy-done.2
  32.8 4.6 %shard_map.43 = (f32[256,256]{1,0:T(8,128)S(1)}, f32[256,256]{1,0:T(8,128)S(1)}, f32[256,256]{1,0:T(8,128)S(1)}, f32[256,256]{1,0:T(8,128)S(1)}) custom-call(s32[2,8]{1,0:T(2,128)S(1)} %copy-done.2, f32[136,256]{1,0:T(8,128)S(1)} %add_add_fusion.1.mine_ref, f32[136,256]{1,0:T(8,128)S(1)} %collective-permute-done.7.other_ref, ...), custom_call_target="tpu_custom_call" | custom-call | tf_op jit(solution)/shard_map/pallas_call | solution.py:189
  37.4 1.3 %collective-permute-start.8 = (f32[256,256]{1,0:T(8,128)S(1)}, f32[256,256]{1,0:T(8,128)S(1)}, u32[]{:S(2)}, u32[]{:S(2)}) collective-permute-start(f32[256,256]{1,0:T(8,128)S(1)} %get-tuple-element.29), channel_id=1, source_target_pairs={{0,1},{1,0},{2,3},{3,2},{4,5},{5,4},{6,7},{7,6},{8,9},{9,8},{10,11... | collective-permute-start | bytes 786440 | tf_op jit(solution)/shard_map/ppermute | solution.py:170
  38.7 0.8 collective-permute-start.9
  39.5 1.4 %collective-permute-start.10 = (f32[256,256]{1,0:T(8,128)S(1)}, f32[256,256]{1,0:T(8,128)S(1)}, u32[]{:S(2)}, u32[]{:S(2)}) collective-permute-start(f32[256,256]{1,0:T(8,128)S(1)} %get-tuple-element.31), channel_id=1, source_target_pairs={{0,3},{1,2},{2,1},{3,0},{4,7},{5,6},{6,5},{7,4},{8,11},{9,10},{10,... | collective-permute-start | bytes 786440 | tf_op jit(solution)/shard_map/ppermute | solution.py:170
  40.9 5.7 %collective-permute-done.8.refs_1_ = f32[256,256]{1,0:T(8,128)S(1)} collective-permute-done((f32[256,256]{1,0:T(8,128)S(1)}, f32[256,256]{1,0:T(8,128)S(1)}, u32[]{:S(2)}, u32[]{:S(2)}) %collective-permute-start.8) | collective-permute-done | bytes 262176 | tf_op jit(solution)/shard_map/ppermute | solution.py:170
  46.6 4.1 %collective-permute-done.9.refs_2_ = f32[256,256]{1,0:T(8,128)S(1)} collective-permute-done((f32[256,256]{1,0:T(8,128)S(1)}, f32[256,256]{1,0:T(8,128)S(1)}, u32[]{:S(2)}, u32[]{:S(2)}) %collective-permute-start.9) | collective-permute-done | bytes 262176 | tf_op jit(solution)/shard_map/ppermute | solution.py:170
  50.7 1.6 %collective-permute-done.10.refs_3_ = f32[256,256]{1,0:T(8,128)S(1)} collective-permute-done((f32[256,256]{1,0:T(8,128)S(1)}, f32[256,256]{1,0:T(8,128)S(1)}, u32[]{:S(2)}, u32[]{:S(2)}) %collective-permute-start.10) | collective-permute-done | bytes 262176 | tf_op jit(solution)/shard_map/ppermute | solution.py:170
  52.4 1.0 %shard_map.44 = (f32[256,512]{1,0:T(8,128)S(1)}, f32[136,256]{1,0:T(8,128)S(1)}, f32[136,256]{1,0:T(8,128)S(1)}) custom-call(s32[2,8]{1,0:T(2,128)S(1)} %copy-done.2, f32[256,256]{1,0:T(8,128)S(1)} %get-tuple-element.28.refs_0_, f32[256,256]{1,0:T(8,128)S(1)} %collective-permute-done.8.refs_1_, f32[256,256]{1,0:T(8,128)S(1)} %collective-permute-done.9.refs_2_, ...), custom_call_target="tpu_custom_call" | custom-call | tf_op jit(solution)/shard_map/pallas_call | solution.py:189
  53.4 0.1 collective-permute-start.11
  53.5 1.3 %collective-permute-done.11 = f32[136,256]{1,0:T(8,128)S(1)} collective-permute-done((f32[136,256]{1,0:T(8,128)S(1)}, f32[136,256]{1,0:T(8,128)S(1)}, u32[]{:S(2)}, u32[]{:S(2)}) %collective-permute-start.11) | collective-permute-done | bytes 139296 | tf_op jit(solution)/shard_map/ppermute | solution.py:170
  54.8 2.5 %collective-permute-start.14 = (f32[136,256]{1,0:T(8,128)S(1)}, f32[136,256]{1,0:T(8,128)S(1)}, u32[]{:S(2)}, u32[]{:S(2)}) collective-permute-start(f32[136,256]{1,0:T(8,128)S(1)} %add.40), channel_id=1, source_target_pairs={{0,24},{4,28},{8,16},{12,20},{16,8},{20,12},{24,0},{28,4},{1,25},{... | collective-permute-start | bytes 417800 | tf_op jit(solution)/shard_map/ppermute | solution.py:170
  57.4 0.0 collective-permute-start.13
  57.4 1.9 %collective-permute-start.12 = (f32[136,256]{1,0:T(8,128)S(1)}, f32[136,256]{1,0:T(8,128)S(1)}, u32[]{:S(2)}, u32[]{:S(2)}) collective-permute-start(f32[136,256]{1,0:T(8,128)S(1)} %add.40), channel_id=1, source_target_pairs={{0,8},{4,12},{8,0},{12,4},{16,24},{20,28},{24,16},{28,20},{1,9},{5... | collective-permute-start | bytes 417800 | tf_op jit(solution)/shard_map/ppermute | solution.py:170
  59.3 4.1 %collective-permute-done.14 = f32[136,256]{1,0:T(8,128)S(1)} collective-permute-done((f32[136,256]{1,0:T(8,128)S(1)}, f32[136,256]{1,0:T(8,128)S(1)}, u32[]{:S(2)}, u32[]{:S(2)}) %collective-permute-start.14) | collective-permute-done | bytes 139296 | tf_op jit(solution)/shard_map/ppermute | solution.py:170
  63.4 5.3 %collective-permute-done.13 = f32[136,256]{1,0:T(8,128)S(1)} collective-permute-done((f32[136,256]{1,0:T(8,128)S(1)}, f32[136,256]{1,0:T(8,128)S(1)}, u32[]{:S(2)}, u32[]{:S(2)}) %collective-permute-start.13) | collective-permute-done | bytes 139296 | tf_op jit(solution)/shard_map/ppermute | solution.py:170
  68.7 0.0 collective-permute-done.12
  68.7 0.1 collective-permute-start.15
  68.8 1.3 %collective-permute-done.15.other_ref = f32[136,256]{1,0:T(8,128)S(1)} collective-permute-done((f32[136,256]{1,0:T(8,128)S(1)}, f32[136,256]{1,0:T(8,128)S(1)}, u32[]{:S(2)}, u32[]{:S(2)}) %collective-permute-start.15) | collective-permute-done | bytes 139296 | tf_op jit(solution)/shard_map/ppermute | solution.py:170
  70.2 4.0 %shard_map.45 = (f32[64,512]{1,0:T(8,128)S(1)}, f32[64,512]{1,0:T(8,128)S(1)}, f32[64,512]{1,0:T(8,128)S(1)}, f32[64,512]{1,0:T(8,128)S(1)}, f32[8,256]{1,0:T(8,128)S(1)}) custom-call(f32[136,256]{1,0:T(8,128)S(1)} %add_add_fusion.mine_ref, f32[136,256]{1,0:T(8,128)S(1)} %collective-permute-done.15.other_ref, f32[256,512]{1,0:T(8,128)S(1)} %get-tuple-element.34.local_ref), custom_call_target="tpu_custom_call" | custom-call | tf_op jit(solution)/shard_map/pallas_call | solution.py:189
  74.2 0.2 collective-permute-start.19
  74.4 1.0 %collective-permute-done.19 = f32[8,256]{1,0:T(8,128)S(1)} collective-permute-done((f32[8,256]{1,0:T(8,128)S(1)}, f32[8,256]{1,0:T(8,128)S(1)}, u32[]{:S(2)}, u32[]{:S(2)}) %collective-permute-start.19) | collective-permute-done | bytes 8224 | tf_op jit(solution)/shard_map/ppermute | solution.py:170
  75.5 2.2 %collective-permute-start.22 = (f32[8,256]{1,0:T(8,128)S(1)}, f32[8,256]{1,0:T(8,128)S(1)}, u32[]{:S(2)}, u32[]{:S(2)}) collective-permute-start(f32[8,256]{1,0:T(8,128)S(1)} %add.44), channel_id=1, source_target_pairs={{0,24},{4,28},{8,16},{12,20},{16,8},{20,12},{24,0},{28,4},{1,25},{... | collective-permute-start | bytes 24584 | tf_op jit(solution)/shard_map/ppermute | solution.py:170
  77.7 0.0 collective-permute-start.21
  77.7 2.2 %collective-permute-start.20 = (f32[8,256]{1,0:T(8,128)S(1)}, f32[8,256]{1,0:T(8,128)S(1)}, u32[]{:S(2)}, u32[]{:S(2)}) collective-permute-start(f32[8,256]{1,0:T(8,128)S(1)} %add.44), channel_id=1, source_target_pairs={{0,8},{4,12},{8,0},{12,4},{16,24},{20,28},{24,16},{28,20},{1,9},{5... | collective-permute-start | bytes 24584 | tf_op jit(solution)/shard_map/ppermute | solution.py:170
  79.8 0.8 collective-permute-start.16
  80.7 1.5 %collective-permute-start.17 = (f32[64,512]{1,0:T(8,128)S(1)}, f32[64,512]{1,0:T(8,128)S(1)}, u32[]{:S(2)}, u32[]{:S(2)}) collective-permute-start(f32[64,512]{1,0:T(8,128)S(1)} %get-tuple-element.37), channel_id=1, source_target_pairs={{0,2},{1,3},{2,0},{3,1},{4,6},{5,7},{6,4},{7,5},{8,10},{9,11},{10,... | collective-permute-start | bytes 393224 | tf_op jit(solution)/shard_map/ppermute | solution.py:170
  82.2 0.0 collective-permute-done.22
  82.2 1.2 %collective-permute-start.18 = (f32[64,512]{1,0:T(8,128)S(1)}, f32[64,512]{1,0:T(8,128)S(1)}, u32[]{:S(2)}, u32[]{:S(2)}) collective-permute-start(f32[64,512]{1,0:T(8,128)S(1)} %get-tuple-element.38), channel_id=1, source_target_pairs={{0,3},{1,2},{2,1},{3,0},{4,7},{5,6},{6,5},{7,4},{8,11},{9,10},{10,... | collective-permute-start | bytes 393224 | tf_op jit(solution)/shard_map/ppermute | solution.py:170
  83.3 0.0 collective-permute-done.21
  83.3 0.0 collective-permute-done.20
  83.4 1.8 %collective-permute-start.25 = (f32[8,256]{1,0:T(8,128)S(1)}, f32[8,256]{1,0:T(8,128)S(1)}, u32[]{:S(2)}, u32[]{:S(2)}) collective-permute-start(f32[8,256]{1,0:T(8,128)S(1)} %add_add_fusion.2.refs_0_), channel_id=1, source_target_pairs={{0,3},{1,2},{2,1},{3,0},{4,7},{5,6},{6,5},{7,4},{8,11},{9,10},{10,... | collective-permute-start | bytes 24584 | tf_op jit(solution)/shard_map/ppermute | solution.py:170
  85.2 0.5 collective-permute-start.24
  85.7 2.5 %collective-permute-done.25.refs_3_ = f32[8,256]{1,0:T(8,128)S(1)} collective-permute-done((f32[8,256]{1,0:T(8,128)S(1)}, f32[8,256]{1,0:T(8,128)S(1)}, u32[]{:S(2)}, u32[]{:S(2)}) %collective-permute-start.25) | collective-permute-done | bytes 8224 | tf_op jit(solution)/shard_map/ppermute | solution.py:170
  88.2 1.3 %collective-permute-start.23 = (f32[8,256]{1,0:T(8,128)S(1)}, f32[8,256]{1,0:T(8,128)S(1)}, u32[]{:S(2)}, u32[]{:S(2)}) collective-permute-start(f32[8,256]{1,0:T(8,128)S(1)} %add_add_fusion.2.refs_0_), channel_id=1, source_target_pairs={{0,1},{1,0},{2,3},{3,2},{4,5},{5,4},{6,7},{7,6},{8,9},{9,8},{10,11... | collective-permute-start | bytes 24584 | tf_op jit(solution)/shard_map/ppermute | solution.py:170
  89.5 0.0 collective-permute-done.24.refs_2_
  89.5 2.4 %collective-permute-done.23.refs_1_ = f32[8,256]{1,0:T(8,128)S(1)} collective-permute-done((f32[8,256]{1,0:T(8,128)S(1)}, f32[8,256]{1,0:T(8,128)S(1)}, u32[]{:S(2)}, u32[]{:S(2)}) %collective-permute-start.23) | collective-permute-done | bytes 8224 | tf_op jit(solution)/shard_map/ppermute | solution.py:170
  91.8 1.2 %shard_map.47 = f32[1,2048]{1,0:T(1,128)} custom-call(s32[2,8]{1,0:T(2,128)S(1)} %copy-done.2, f32[8,256]{1,0:T(8,128)S(1)} %add_add_fusion.2.refs_0_, f32[8,256]{1,0:T(8,128)S(1)} %collective-permute-done.23.refs_1_, f32[8,256]{1,0:T(8,128)S(1)} %collective-permute-done.24.refs_2_, f32[8,256]{1,0:T(8,128)S(1)} %collective-permute-done.25.refs_3_), custom_call_target="tpu_custom_call" | custom-call | tf_op jit(solution)/shard_map/pallas_call | solution.py:189
  93.0 0.0 collective-permute-done.16.refs_1_
  93.0 0.0 collective-permute-done.17.refs_2_
  93.0 0.0 collective-permute-done.18.refs_3_
  93.0 1.4 %shard_map.46 = f32[64,2048]{1,0:T(8,128)} custom-call(s32[2,8]{1,0:T(2,128)S(1)} %copy-done.2, f32[64,512]{1,0:T(8,128)S(1)} %get-tuple-element.35.refs_0_, f32[64,512]{1,0:T(8,128)S(1)} %collective-permute-done.16.refs_1_, f32[64,512]{1,0:T(8,128)S(1)} %collective-permute-done.17.refs_2_, f32[64,512]{1,0:T(8,128)S(1)} %collective-permute-done.18.refs_3_), custom_call_target="tpu_custom_call" | custom-call | tf_op jit(solution)/shard_map/pallas_call | solution.py:189
  (7 shorter events, 0.1 us)
Async XLA Ops:
  0.6 1.0 %copy-start = (f32[64,2048]{1,0:T(8,128)S(1)}, f32[64,2048]{1,0:T(8,128)}, u32[]{:S(2)}) copy-start(f32[64,2048]{1,0:T(8,128)} %slab_ref.1) | copy-start | bytes 1572868
  1.7 0.7 copy-start.1
  3.0 6.9 %collective-permute-start = (f32[64,512]{1,0:T(8,128)S(1)}, f32[64,512]{1,0:T(8,128)S(1)}, u32[]{:S(2)}, u32[]{:S(2)}) collective-permute-start(f32[64,512]{1,0:T(8,128)S(1)} %get-tuple-element.22), channel_id=1, source_target_pairs={{0,1},{1,0},{2,3},{3,2},{4,5},{5,4},{6,7},{7,6},{8,9},{9,8},{10,11... | collective-permute-start | bytes 393224 | tf_op jit(solution)/shard_map/ppermute | solution.py:170
  6.0 7.8 %collective-permute-start.1 = (f32[64,512]{1,0:T(8,128)S(1)}, f32[64,512]{1,0:T(8,128)S(1)}, u32[]{:S(2)}, u32[]{:S(2)}) collective-permute-start(f32[64,512]{1,0:T(8,128)S(1)} %get-tuple-element.23), channel_id=1, source_target_pairs={{0,2},{1,3},{2,0},{3,1},{4,6},{5,7},{6,4},{7,5},{8,10},{9,11},{10,... | collective-permute-start | bytes 393224 | tf_op jit(solution)/shard_map/ppermute | solution.py:170
  7.5 6.3 %collective-permute-start.2 = (f32[64,512]{1,0:T(8,128)S(1)}, f32[64,512]{1,0:T(8,128)S(1)}, u32[]{:S(2)}, u32[]{:S(2)}) collective-permute-start(f32[64,512]{1,0:T(8,128)S(1)} %get-tuple-element.24), channel_id=1, source_target_pairs={{0,3},{1,2},{2,1},{3,0},{4,7},{5,6},{6,5},{7,4},{8,11},{9,10},{10,... | collective-permute-start | bytes 393224 | tf_op jit(solution)/shard_map/ppermute | solution.py:170
  14.1 1.4 %collective-permute-start.3 = (f32[136,256]{1,0:T(8,128)S(1)}, f32[136,256]{1,0:T(8,128)S(1)}, u32[]{:S(2)}, u32[]{:S(2)}) collective-permute-start(f32[136,256]{1,0:T(8,128)S(1)} %get-tuple-element.26), channel_id=1, source_target_pairs={{0,4},{4,0},{8,12},{12,8},{16,20},{20,16},{24,28},{28,24},{1,5},{5... | collective-permute-start | bytes 417800 | tf_op jit(solution)/shard_map/ppermute | solution.py:170
  15.6 8.5 %collective-permute-start.6 = (f32[136,256]{1,0:T(8,128)S(1)}, f32[136,256]{1,0:T(8,128)S(1)}, u32[]{:S(2)}, u32[]{:S(2)}) collective-permute-start(f32[136,256]{1,0:T(8,128)S(1)} %add.36), channel_id=1, source_target_pairs={{0,24},{4,28},{8,16},{12,20},{16,8},{20,12},{24,0},{28,4},{1,25},{... | collective-permute-start | bytes 417800 | tf_op jit(solution)/shard_map/ppermute | solution.py:170
  19.3 12.1 %collective-permute-start.5 = (f32[136,256]{1,0:T(8,128)S(1)}, f32[136,256]{1,0:T(8,128)S(1)}, u32[]{:S(2)}, u32[]{:S(2)}) collective-permute-start(f32[136,256]{1,0:T(8,128)S(1)} %add.36), channel_id=1, source_target_pairs={{0,16},{4,20},{8,24},{12,28},{16,0},{20,4},{24,8},{28,12},{1,17},{... | collective-permute-start | bytes 417800 | tf_op jit(solution)/shard_map/ppermute | solution.py:170
  19.3 12.1 %collective-permute-start.4 = (f32[136,256]{1,0:T(8,128)S(1)}, f32[136,256]{1,0:T(8,128)S(1)}, u32[]{:S(2)}, u32[]{:S(2)}) collective-permute-start(f32[136,256]{1,0:T(8,128)S(1)} %add.36), channel_id=1, source_target_pairs={{0,8},{4,12},{8,0},{12,4},{16,24},{20,28},{24,16},{28,20},{1,9},{5... | collective-permute-start | bytes 417800 | tf_op jit(solution)/shard_map/ppermute | solution.py:170
  31.4 1.4 %copy-start.2 = (s32[2,8]{1,0:T(2,128)S(1)}, s32[2,8]{1,0:T(2,128)}, u32[]{:S(2)}) copy-start(s32[2,8]{1,0:T(2,128)} %plan_ref.9) | copy-start | bytes 196
  31.4 1.4 %collective-permute-start.7 = (f32[136,256]{1,0:T(8,128)S(1)}, f32[136,256]{1,0:T(8,128)S(1)}, u32[]{:S(2)}, u32[]{:S(2)}) collective-permute-start(f32[136,256]{1,0:T(8,128)S(1)} %add_add_fusion.1.mine_ref), channel_id=1, source_target_pairs={{0,4},{4,0},{8,12},{12,8},{16,20},{20,16},{24,28},{28,24},{1,5},{5... | collective-permute-start | bytes 417800 | tf_op jit(solution)/shard_map/ppermute | solution.py:170
  37.4 9.2 %collective-permute-start.8 = (f32[256,256]{1,0:T(8,128)S(1)}, f32[256,256]{1,0:T(8,128)S(1)}, u32[]{:S(2)}, u32[]{:S(2)}) collective-permute-start(f32[256,256]{1,0:T(8,128)S(1)} %get-tuple-element.29), channel_id=1, source_target_pairs={{0,1},{1,0},{2,3},{3,2},{4,5},{5,4},{6,7},{7,6},{8,9},{9,8},{10,11... | collective-permute-start | bytes 786440 | tf_op jit(solution)/shard_map/ppermute | solution.py:170
  38.7 12.1 %collective-permute-start.9 = (f32[256,256]{1,0:T(8,128)S(1)}, f32[256,256]{1,0:T(8,128)S(1)}, u32[]{:S(2)}, u32[]{:S(2)}) collective-permute-start(f32[256,256]{1,0:T(8,128)S(1)} %get-tuple-element.30), channel_id=1, source_target_pairs={{0,2},{1,3},{2,0},{3,1},{4,6},{5,7},{6,4},{7,5},{8,10},{9,11},{10,... | collective-permute-start | bytes 786440 | tf_op jit(solution)/shard_map/ppermute | solution.py:170
  39.5 12.9 %collective-permute-start.10 = (f32[256,256]{1,0:T(8,128)S(1)}, f32[256,256]{1,0:T(8,128)S(1)}, u32[]{:S(2)}, u32[]{:S(2)}) collective-permute-start(f32[256,256]{1,0:T(8,128)S(1)} %get-tuple-element.31), channel_id=1, source_target_pairs={{0,3},{1,2},{2,1},{3,0},{4,7},{5,6},{6,5},{7,4},{8,11},{9,10},{10,... | collective-permute-start | bytes 786440 | tf_op jit(solution)/shard_map/ppermute | solution.py:170
  53.4 1.4 %collective-permute-start.11 = (f32[136,256]{1,0:T(8,128)S(1)}, f32[136,256]{1,0:T(8,128)S(1)}, u32[]{:S(2)}, u32[]{:S(2)}) collective-permute-start(f32[136,256]{1,0:T(8,128)S(1)} %get-tuple-element.33), channel_id=1, source_target_pairs={{0,4},{4,0},{8,12},{12,8},{16,20},{20,16},{24,28},{28,24},{1,5},{5... | collective-permute-start | bytes 417800 | tf_op jit(solution)/shard_map/ppermute | solution.py:170
  54.8 8.5 %collective-permute-start.14 = (f32[136,256]{1,0:T(8,128)S(1)}, f32[136,256]{1,0:T(8,128)S(1)}, u32[]{:S(2)}, u32[]{:S(2)}) collective-permute-start(f32[136,256]{1,0:T(8,128)S(1)} %add.40), channel_id=1, source_target_pairs={{0,24},{4,28},{8,16},{12,20},{16,8},{20,12},{24,0},{28,4},{1,25},{... | collective-permute-start | bytes 417800 | tf_op jit(solution)/shard_map/ppermute | solution.py:170
  57.4 11.3 %collective-permute-start.13 = (f32[136,256]{1,0:T(8,128)S(1)}, f32[136,256]{1,0:T(8,128)S(1)}, u32[]{:S(2)}, u32[]{:S(2)}) collective-permute-start(f32[136,256]{1,0:T(8,128)S(1)} %add.40), channel_id=1, source_target_pairs={{0,16},{4,20},{8,24},{12,28},{16,0},{20,4},{24,8},{28,12},{1,17},{... | collective-permute-start | bytes 417800 | tf_op jit(solution)/shard_map/ppermute | solution.py:170
  57.4 11.3 %collective-permute-start.12 = (f32[136,256]{1,0:T(8,128)S(1)}, f32[136,256]{1,0:T(8,128)S(1)}, u32[]{:S(2)}, u32[]{:S(2)}) collective-permute-start(f32[136,256]{1,0:T(8,128)S(1)} %add.40), channel_id=1, source_target_pairs={{0,8},{4,12},{8,0},{12,4},{16,24},{20,28},{24,16},{28,20},{1,9},{5... | collective-permute-start | bytes 417800 | tf_op jit(solution)/shard_map/ppermute | solution.py:170
  68.7 1.4 %collective-permute-start.15 = (f32[136,256]{1,0:T(8,128)S(1)}, f32[136,256]{1,0:T(8,128)S(1)}, u32[]{:S(2)}, u32[]{:S(2)}) collective-permute-start(f32[136,256]{1,0:T(8,128)S(1)} %add_add_fusion.mine_ref), channel_id=1, source_target_pairs={{0,4},{4,0},{8,12},{12,8},{16,20},{20,16},{24,28},{28,24},{1,5},{5... | collective-permute-start | bytes 417800 | tf_op jit(solution)/shard_map/ppermute | solution.py:170
  74.2 1.2 %collective-permute-start.19 = (f32[8,256]{1,0:T(8,128)S(1)}, f32[8,256]{1,0:T(8,128)S(1)}, u32[]{:S(2)}, u32[]{:S(2)}) collective-permute-start(f32[8,256]{1,0:T(8,128)S(1)} %get-tuple-element.39), channel_id=1, source_target_pairs={{0,4},{4,0},{8,12},{12,8},{16,20},{20,16},{24,28},{28,24},{1,5},{5... | collective-permute-start | bytes 24584 | tf_op jit(solution)/shard_map/ppermute | solution.py:170
  75.5 6.7 %collective-permute-start.22 = (f32[8,256]{1,0:T(8,128)S(1)}, f32[8,256]{1,0:T(8,128)S(1)}, u32[]{:S(2)}, u32[]{:S(2)}) collective-permute-start(f32[8,256]{1,0:T(8,128)S(1)} %add.44), channel_id=1, source_target_pairs={{0,24},{4,28},{8,16},{12,20},{16,8},{20,12},{24,0},{28,4},{1,25},{... | collective-permute-start | bytes 24584 | tf_op jit(solution)/shard_map/ppermute | solution.py:170
  77.7 5.7 %collective-permute-start.21 = (f32[8,256]{1,0:T(8,128)S(1)}, f32[8,256]{1,0:T(8,128)S(1)}, u32[]{:S(2)}, u32[]{:S(2)}) collective-permute-start(f32[8,256]{1,0:T(8,128)S(1)} %add.44), channel_id=1, source_target_pairs={{0,16},{4,20},{8,24},{12,28},{16,0},{20,4},{24,8},{28,12},{1,17},{... | collective-permute-start | bytes 24584 | tf_op jit(solution)/shard_map/ppermute | solution.py:170
  77.7 5.7 %collective-permute-start.20 = (f32[8,256]{1,0:T(8,128)S(1)}, f32[8,256]{1,0:T(8,128)S(1)}, u32[]{:S(2)}, u32[]{:S(2)}) collective-permute-start(f32[8,256]{1,0:T(8,128)S(1)} %add.44), channel_id=1, source_target_pairs={{0,8},{4,12},{8,0},{12,4},{16,24},{20,28},{24,16},{28,20},{1,9},{5... | collective-permute-start | bytes 24584 | tf_op jit(solution)/shard_map/ppermute | solution.py:170
  79.8 13.2 %collective-permute-start.16 = (f32[64,512]{1,0:T(8,128)S(1)}, f32[64,512]{1,0:T(8,128)S(1)}, u32[]{:S(2)}, u32[]{:S(2)}) collective-permute-start(f32[64,512]{1,0:T(8,128)S(1)} %get-tuple-element.36), channel_id=1, source_target_pairs={{0,1},{1,0},{2,3},{3,2},{4,5},{5,4},{6,7},{7,6},{8,9},{9,8},{10,11... | collective-permute-start | bytes 393224 | tf_op jit(solution)/shard_map/ppermute | solution.py:170
  80.7 12.4 %collective-permute-start.17 = (f32[64,512]{1,0:T(8,128)S(1)}, f32[64,512]{1,0:T(8,128)S(1)}, u32[]{:S(2)}, u32[]{:S(2)}) collective-permute-start(f32[64,512]{1,0:T(8,128)S(1)} %get-tuple-element.37), channel_id=1, source_target_pairs={{0,2},{1,3},{2,0},{3,1},{4,6},{5,7},{6,4},{7,5},{8,10},{9,11},{10,... | collective-permute-start | bytes 393224 | tf_op jit(solution)/shard_map/ppermute | solution.py:170
  82.2 10.9 %collective-permute-start.18 = (f32[64,512]{1,0:T(8,128)S(1)}, f32[64,512]{1,0:T(8,128)S(1)}, u32[]{:S(2)}, u32[]{:S(2)}) collective-permute-start(f32[64,512]{1,0:T(8,128)S(1)} %get-tuple-element.38), channel_id=1, source_target_pairs={{0,3},{1,2},{2,1},{3,0},{4,7},{5,6},{6,5},{7,4},{8,11},{9,10},{10,... | collective-permute-start | bytes 393224 | tf_op jit(solution)/shard_map/ppermute | solution.py:170
  83.4 4.8 %collective-permute-start.25 = (f32[8,256]{1,0:T(8,128)S(1)}, f32[8,256]{1,0:T(8,128)S(1)}, u32[]{:S(2)}, u32[]{:S(2)}) collective-permute-start(f32[8,256]{1,0:T(8,128)S(1)} %add_add_fusion.2.refs_0_), channel_id=1, source_target_pairs={{0,3},{1,2},{2,1},{3,0},{4,7},{5,6},{6,5},{7,4},{8,11},{9,10},{10,... | collective-permute-start | bytes 24584 | tf_op jit(solution)/shard_map/ppermute | solution.py:170
  85.2 4.3 %collective-permute-start.24 = (f32[8,256]{1,0:T(8,128)S(1)}, f32[8,256]{1,0:T(8,128)S(1)}, u32[]{:S(2)}, u32[]{:S(2)}) collective-permute-start(f32[8,256]{1,0:T(8,128)S(1)} %add_add_fusion.2.refs_0_), channel_id=1, source_target_pairs={{0,2},{1,3},{2,0},{3,1},{4,6},{5,7},{6,4},{7,5},{8,10},{9,11},{10,... | collective-permute-start | bytes 24584 | tf_op jit(solution)/shard_map/ppermute | solution.py:170
  88.2 3.7 %collective-permute-start.23 = (f32[8,256]{1,0:T(8,128)S(1)}, f32[8,256]{1,0:T(8,128)S(1)}, u32[]{:S(2)}, u32[]{:S(2)}) collective-permute-start(f32[8,256]{1,0:T(8,128)S(1)} %add_add_fusion.2.refs_0_), channel_id=1, source_target_pairs={{0,1},{1,0},{2,3},{3,2},{4,5},{5,4},{6,7},{7,6},{8,9},{9,8},{10,11... | collective-permute-start | bytes 24584 | tf_op jit(solution)/shard_map/ppermute | solution.py:170

commit v2 on v1

v2 whole, which is shorter than its diff:
```python
import functools
import itertools
import math

import jax
import jax.numpy as jnp
from jax import lax
from jax.experimental import pallas as pl
from jax.experimental.pallas import tpu as pltpu
from jax.sharding import PartitionSpec as P

NS_STEPS = 4
PAD = 8
MOST_MOVES = 16

VMEM = pl.BlockSpec(memory_space=pltpu.VMEM)
SMEM = pl.BlockSpec(memory_space=pltpu.SMEM)
ROWS_BY_COLS = (((1,), (0,)), ((), ()))
COLS_BY_COLS = (((0,), (0,)), ((), ()))


def split(x):
    high = x.astype(jnp.bfloat16)
    return high, (x - high.astype(jnp.float32)).astype(jnp.bfloat16)


def mul(a, b, dims=ROWS_BY_COLS):
    dot = functools.partial(lax.dot_general, dimension_numbers=dims, preferred_element_type=jnp.float32)
    return dot(a[0], b[0]) + (dot(a[0], b[1]) + dot(a[1], b[0]))


def slot_of(plan_ref, rnd, block, count):
    found = jnp.int32(0)
    for slot in range(1, count):
        found = jnp.where(plan_ref[rnd, slot] == block, slot, found)
    return found


def route_kernel(plan_ref, table_ref, case_ref, *, rnd, moves):
    slots = plan_ref.shape[1]
    count = slots // 2
    now, half, seen = jnp.int32(0), jnp.int32(0), jnp.int32(0)
    for _ in range(count):
        seen = seen | (jnp.int32(1) << now)
        leaves = plan_ref[rnd, 2 * now + 1 - half]
        slot = slot_of(plan_ref, rnd + 1, leaves, slots)
        joins = slot_of(plan_ref, rnd, plan_ref[rnd + 1, slot ^ 1], slots)
        table_ref[0, now] = half
        table_ref[1, now] = slot_of(plan_ref, rnd + 1, plan_ref[rnd, 2 * now + half], slots) // 2
        table_ref[2, now] = joins // 2
        now, half = joins // 2, joins % 2
        closed = ((seen >> now) & 1) == 1
        unseen = jnp.int32(0)
        for device in reversed(range(count)):
            unseen = jnp.where(((seen >> device) & 1) == 0, device, unseen)
        now, half = jnp.where(closed, unseen, now), jnp.where(closed, 0, half)
    code = jnp.int32(0)
    for device in range(count):
        code = code * count + table_ref[2, device]
    case = jnp.int32(0)
    for index, move in enumerate(moves):
        case = jnp.where(code == functools.reduce(lambda total, to: total * count + to, move), index, case)
    case_ref[0, 0] = case


def deal_kernel(plan_ref, slab_ref, *outs):
    me = lax.axis_index("pair")
    width = outs[0].shape[1] // 2
    for mask, out in enumerate(outs):
        to = me ^ mask
        for half in range(2):
            block = plan_ref[0, 2 * to + half]
            start = pl.multiple_of(block * width, width)
            out[:, half * width : (half + 1) * width] = slab_ref[:, pl.ds(start, width)]


def cross_of(first, second, keep_ref, send_ref, scratch):
    width = first.shape[1]
    scratch[...] = mul(split(first), split(second), COLS_BY_COLS)
    diag = jnp.concatenate(
        [
            jnp.sum(first * first, axis=0, keepdims=True),
            jnp.sum(second * second, axis=0, keepdims=True),
            jnp.zeros((PAD - 2, width), jnp.float32),
        ],
        axis=0,
    )
    core = lax.axis_index("row") & 1
    part = width // 2
    for ref, which in ((keep_ref, core), (send_ref, 1 - core)):
        ref[:part, :] = scratch[pl.ds(pl.multiple_of(which * part, part), part), :]
        ref[part:, :] = diag


def first_cross_kernel(*refs):
    *ins, local_ref, keep_ref, send_ref, scratch = refs
    me = lax.axis_index("pair")
    rows = ins[0].shape[0]
    width = ins[0].shape[1] // 2
    for mask, ref in enumerate(ins):
        local_ref[pl.ds(pl.multiple_of((me ^ mask) * rows, rows), rows), :] = ref[...]
    cross_of(local_ref[:, :width], local_ref[:, width:], keep_ref, send_ref, scratch)


def next_cross_kernel(plan_ref, table_ref, kept_ref, *refs, rnd):
    *ins, local_ref, keep_ref, send_ref, scratch = refs
    width = kept_ref.shape[1]
    count = plan_ref.shape[1] // 2
    me = lax.axis_index("pair")
    came = ins[0][...]
    for mask in range(2, len(ins) + 1):
        came = jnp.where(table_ref[2, me ^ mask] == me, ins[mask - 1][...], came)
    kept_first = plan_ref[rnd - 1, 2 * me + table_ref[0, me]] == plan_ref[rnd, 2 * table_ref[1, me]]
    first = jnp.where(kept_first, kept_ref[...], came)
    second = jnp.where(kept_first, came, kept_ref[...])
    local_ref[:, :width] = first
    local_ref[:, width:] = second
    cross_of(first, second, keep_ref, send_ref, scratch)


def rotate(mine, other, first, second):
    part, width = mine.shape[0] - PAD, mine.shape[1]
    core = lax.axis_index("row") & 1
    cross = jnp.concatenate(
        [jnp.where(core == 0, mine[:part], other[:part]), jnp.where(core == 0, other[:part], mine[:part])], axis=0
    )
    diag_first = jnp.transpose(jnp.broadcast_to(mine[part : part + 1], (width, width)))
    diag_second = mine[part + 1 : part + 2]
    coupling = cross / (diag_first + diag_second + 1e-06)
    k = split(coupling)
    kt = split(jnp.transpose(coupling))
    inv_sq = 1.0 / (1.0 + jnp.sum(coupling * coupling))
    row_id = lax.broadcasted_iota(jnp.int32, (width, width), 0)
    col_id = lax.broadcasted_iota(jnp.int32, (width, width), 1)
    ident = jnp.where(row_id == col_id, 1.0, 0.0)
    squares = [(ident + mul(k, kt)) * inv_sq, (ident + mul(kt, k)) * inv_sq]
    moved = [first - mul(split(second), kt), second + mul(split(first), k)]
    factors = [None, None]
    for step in range(NS_STEPS):
        for side in range(2):
            near = split(1.5 * ident - 0.5 * squares[side])
            if step == 0:
                factors[side] = 1.5 * ident - 0.5 * squares[side]
            else:
                factors[side] = mul(split(factors[side]), near)
            if step < NS_STEPS - 1:
                squares[side] = mul(split(mul(split(squares[side]), near)), near)
    scale = jnp.sqrt(inv_sq)
    return [mul(split(moved[side]), split(factors[side])) * scale for side in range(2)]


def turn_kernel(table_ref, mine_ref, other_ref, local_ref, kept_ref, leaves_ref):
    width = local_ref.shape[1] // 2
    new = rotate(mine_ref[...], other_ref[...], local_ref[:, :width], local_ref[:, width:])
    keeps_first = table_ref[0, lax.axis_index("pair")] == 0
    kept_ref[...] = jnp.where(keeps_first, new[0], new[1])
    leaves_ref[...] = jnp.where(keeps_first, new[1], new[0])


def last_turn_kernel(plan_ref, table_ref, mine_ref, other_ref, local_ref, *refs, rnd):
    *outs, squares_ref, scratch = refs
    width = local_ref.shape[1] // 2
    new = rotate(mine_ref[...], other_ref[...], local_ref[:, :width], local_ref[:, width:])
    me = lax.axis_index("pair")
    squares_ref[...] = jnp.zeros_like(squares_ref)
    for half in range(2):
        scratch[:, half * width : (half + 1) * width] = new[half]
        block = plan_ref[rnd, 2 * table_ref[1, me] + half]
        squares_ref[pl.ds(block, 1), :] = jnp.sum(new[half] * new[half], axis=0, keepdims=True)
    rows = outs[0].shape[0]
    for mask, out in enumerate(outs):
        out[...] = scratch[pl.ds(pl.multiple_of((me ^ mask) * rows, rows), rows), :]


def place_kernel(plan_ref, table_ref, *refs, rnd):
    *ins, out_ref = refs
    width = ins[0].shape[1] // 2
    me = lax.axis_index("pair")
    for mask, ref in enumerate(ins):
        for half in range(2):
            block = plan_ref[rnd, 2 * table_ref[1, me ^ mask] + half]
            start = pl.multiple_of(block * width, width)
            out_ref[:, pl.ds(start, width)] = ref[:, half * width : (half + 1) * width]


def swap(x, axis, mask):
    return lax.ppermute(x, axis, [(i, i ^ mask) for i in range(lax.axis_size(axis))])


def spread(parts):
    return [parts[0]] + [swap(parts[mask], "pair", mask) for mask in range(1, len(parts))]


def tree_sum(parts):
    while len(parts) > 1:
        parts = [a + b for a, b in zip(parts[::2], parts[1::2])]
    return parts[0]


def over_chips(x):
    return tree_sum([x] + [swap(x, "row", mask) for mask in range(2, lax.axis_size("row"), 2)])


def powers(size):
    return [1 << bit for bit in range(size.bit_length() - 1)]


def hand_on(x, case, moves):
    if moves:
        ways = [lambda x, move=move: lax.ppermute(x, "pair", list(enumerate(move))) for move in moves]
        return [lax.switch(case, ways, x)]
    return [swap(x, "pair", mask) for mask in range(1, lax.axis_size("pair"))]


def call(kernel, ins, outs, scratch=(), smem=0, smem_outs=(), cost=None):
    shapes = [jax.ShapeDtypeStruct(shape, jnp.int32) for shape in smem_outs]
    shapes += [jax.ShapeDtypeStruct(shape, jnp.float32) for shape in outs]
    return pl.pallas_call(
        kernel,
        out_shape=shapes,
        in_specs=[SMEM] * smem + [VMEM] * (len(ins) - smem),
        out_specs=[SMEM] * len(smem_outs) + [VMEM] * len(outs),
        scratch_shapes=[pltpu.VMEM(shape, jnp.float32) for shape in scratch],
        compiler_params=pltpu.CompilerParams(vmem_limit_bytes=24 * 2**20),
        cost_estimate=cost,
    )(*ins)


def on_device(slab, plan):
    piece_rows, ncols = slab.shape
    pair_count = lax.axis_size("pair")
    blocks = 2 * pair_count
    width = ncols // blocks
    group_rows = piece_rows * pair_count
    total_rows = group_rows * lax.axis_size("row")
    part = (width // 2 + PAD, width)
    square = (width, width)
    block = (group_rows, width)
    local_shape = (group_rows, 2 * width)
    piece = (piece_rows, 2 * width)
    moves = []
    if math.factorial(pair_count) <= 3 * MOST_MOVES:
        moves = [m for m in itertools.permutations(range(pair_count)) if all(to != i for i, to in enumerate(m))]

    dealt = call(deal_kernel, [plan, slab], [piece] * pair_count, smem=1)
    held = spread(dealt)
    table, case = call(
        functools.partial(route_kernel, rnd=0, moves=moves), [plan], [], smem=1, smem_outs=[(3, pair_count), (1, 1)]
    )
    local, keep, send = call(first_cross_kernel, held, [local_shape, part, part], [square])
    mine = over_chips(keep + swap(send, "row", 1))
    other = swap(mine, "row", 1)
    kept, leaves = call(turn_kernel, [table, mine, other, local], [block, block], smem=1)
    came = hand_on(leaves, case[0, 0], moves)
    local, keep, send = call(
        functools.partial(next_cross_kernel, rnd=1),
        [plan, table, kept] + came,
        [local_shape, part, part],
        [square],
        smem=2,
    )
    mine = over_chips(keep + swap(send, "row", 1))
    other = swap(mine, "row", 1)
    *sent, squares = call(
        functools.partial(last_turn_kernel, rnd=1),
        [plan, table, mine, other, local],
        [piece] * pair_count + [(blocks, width)],
        [local_shape],
        smem=2,
    )
    back = [sent[0]]
    hops = [("row", mask) for mask in powers(lax.axis_size("row"))] + [("pair", mask) for mask in powers(pair_count)]
    for hop, (axis, mask) in enumerate(hops[:-1]):
        if hop + 1 < pair_count:
            squares, piece_out = lax.optimization_barrier((squares, sent[hop + 1]))
            back.append(swap(piece_out, "pair", hop + 1))
        squares = squares + swap(squares, axis, mask)
    back += [swap(sent[mask], "pair", mask) for mask in range(len(hops), pair_count)]
    squares, back = lax.optimization_barrier((squares, back))
    squares = squares + swap(squares, *hops[-1])
    (rotated,) = call(
        functools.partial(place_kernel, rnd=1),
        [plan, table] + back,
        [(piece_rows, ncols)],
        smem=2,
        cost=pl.CostEstimate(flops=0, bytes_accessed=8 * slab.size, transcendentals=0),
    )
    return rotated, jnp.sqrt(squares / total_rows).reshape(ncols)


def solution(mesh):
    specs = (P(("row", "pair"), None), P())
    return jax.shard_map(on_device, mesh=mesh, in_specs=specs, out_specs=specs, check_vma=False)
```

time: 94.6 us -> 89 us (0.941)
  starting transfers between devices: 29 us -> 23.1 us
  waiting for transfers between devices: 49.7 us -> 47.7 us
  Pallas kernels: 13.2 us -> 14.3 us
    ppermute x26 -> x21, waiting for transfers between devices: 49.7 us -> 39.3 us  [swap(): lax.ppermute(x, axis, [(i, i ^ mask) for i in range(lax.axis_size(axis))])]
    ppermute x0 -> x1, waiting for transfers between devices: none -> 8.49 us  [hand_on(): lax.ppermute(x, 'pair', list(enumerate(move)))]
    ppermute x26 -> x21, starting transfers between devices: 29 us -> 21.8 us  [swap(): lax.ppermute(x, axis, [(i, i ^ mask) for i in range(lax.axis_size(axis))])]
    ppermute x0 -> x1, starting transfers between devices: none -> 1.27 us  [hand_on(): lax.ppermute(x, 'pair', list(enumerate(move)))]
    pallas_call x7, Pallas kernels: 13.2 us -> 14.3 us  [call(): pl.pallas_call(kernel, out_shape=shapes, in_specs=[SMEM] * smem + [VMEM]...]
    unnamed x6 -> x7, local copies, waits for them, and re-layouts: 1.72 us -> 2.33 us
  transfers between devices with their start and end apart: 26 -> 22, of which waited for: 16 -> 15; matrix products, arithmetic and copies ran while one was open for 0% -> 0% of each run, Pallas kernels for 1% -> 3%
where the time goes in v2:
time: 89 us
  waiting for transfers between devices  47.7 us (54%)
  starting transfers between devices  23.1 us (26%)
  Pallas kernels  14.3 us (16%)
  local copies, waits for them, and re-layouts  2.33 us (3%)
  between operations  1.43 us (2%)
    ppermute x21, waiting for transfers between devices, swap(): lax.ppermute(x, axis, [(i, i ^ mask) for i in range(lax.axis_size(axis))])  39.3 us
    ppermute x21, starting transfers between devices, swap(): lax.ppermute(x, axis, [(i, i ^ mask) for i in range(lax.axis_size(axis))])  21.8 us
    pallas_call x7, Pallas kernels, call(): pl.pallas_call(kernel, out_shape=shapes, in_specs=[SMEM] * smem + [VMEM]...  14.3 us
    ppermute x1, waiting for transfers between devices, hand_on(): lax.ppermute(x, 'pair', list(enumerate(move)))  8.49 us
    unnamed x7, local copies, waits for them, and re-layouts  2.33 us
  transfers between devices with their start and end apart: 22, of which 15 were waited for; matrix products, arithmetic and copies ran while one was open for 0% of the time, Pallas kernels for 3%

profile of v2, /device:TPU:0, one launch (start us, length us, event | category | flops | bytes accessed | tf_op | source)
XLA Modules:
  0.0 89.0 jit_solution(809383901254824507)
XLA Ops:
  0.6 0.0 copy-start
  0.6 1.0 %copy-done = f32[64,2048]{1,0:T(8,128)S(1)} copy-done((f32[64,2048]{1,0:T(8,128)S(1)}, f32[64,2048]{1,0:T(8,128)}, u32[]{:S(2)}) %copy-start) | copy-done | bytes 524312
  1.7 0.0 copy-start.1
  1.7 0.7 copy-done.1
  2.4 0.6 shard_map.42
  3.0 3.0 %collective-permute-start.9 = (f32[64,512]{1,0:T(8,128)S(1)}, f32[64,512]{1,0:T(8,128)S(1)}, u32[]{:S(2)}, u32[]{:S(2)}) collective-permute-start(f32[64,512]{1,0:T(8,128)S(1)} %get-tuple-element.53), channel_id=1, source_target_pairs={{0,1},{1,0},{2,3},{3,2},{4,5},{5,4},{6,7},{7,6},{8,9},{9,8},{10,11... | collective-permute-start | bytes 393224 | tf_op jit(solution)/shard_map/ppermute | solution.py:187
  6.0 1.5 %collective-permute-start.10 = (f32[64,512]{1,0:T(8,128)S(1)}, f32[64,512]{1,0:T(8,128)S(1)}, u32[]{:S(2)}, u32[]{:S(2)}) collective-permute-start(f32[64,512]{1,0:T(8,128)S(1)} %get-tuple-element.54), channel_id=1, source_target_pairs={{0,2},{1,3},{2,0},{3,1},{4,6},{5,7},{6,4},{7,5},{8,10},{9,11},{10,... | collective-permute-start | bytes 393224 | tf_op jit(solution)/shard_map/ppermute | solution.py:187
  7.5 0.0 collective-permute-start.11
  7.5 2.4 %collective-permute-done.9.refs_1_ = f32[64,512]{1,0:T(8,128)S(1)} collective-permute-done((f32[64,512]{1,0:T(8,128)S(1)}, f32[64,512]{1,0:T(8,128)S(1)}, u32[]{:S(2)}, u32[]{:S(2)}) %collective-permute-start.9) | collective-permute-done | bytes 131104 | tf_op jit(solution)/shard_map/ppermute | solution.py:187
  9.9 3.9 %collective-permute-done.10.refs_2_ = f32[64,512]{1,0:T(8,128)S(1)} collective-permute-done((f32[64,512]{1,0:T(8,128)S(1)}, f32[64,512]{1,0:T(8,128)S(1)}, u32[]{:S(2)}, u32[]{:S(2)}) %collective-permute-start.10) | collective-permute-done | bytes 131104 | tf_op jit(solution)/shard_map/ppermute | solution.py:187
  13.7 0.0 collective-permute-done.11.refs_3_
  13.7 0.4 shard_map.43
  14.1 0.1 collective-permute-start.12
  14.2 1.3 %collective-permute-done.12 = f32[136,256]{1,0:T(8,128)S(1)} collective-permute-done((f32[136,256]{1,0:T(8,128)S(1)}, f32[136,256]{1,0:T(8,128)S(1)}, u32[]{:S(2)}, u32[]{:S(2)}) %collective-permute-start.12) | collective-permute-done | bytes 139296 | tf_op jit(solution)/shard_map/ppermute | solution.py:187
  15.6 0.0 copy-start.2
  15.6 3.7 %collective-permute-start.15 = (f32[136,256]{1,0:T(8,128)S(1)}, f32[136,256]{1,0:T(8,128)S(1)}, u32[]{:S(2)}, u32[]{:S(2)}) collective-permute-start(f32[136,256]{1,0:T(8,128)S(1)} %add.39), channel_id=1, source_target_pairs={{0,24},{4,28},{8,16},{12,20},{16,8},{20,12},{24,0},{28,4},{1,25},{... | collective-permute-start | bytes 417800 | tf_op jit(solution)/shard_map/ppermute | solution.py:187
  19.3 0.0 collective-permute-start.14
  19.3 0.8 collective-permute-start.13
  20.1 4.0 %collective-permute-done.15 = f32[136,256]{1,0:T(8,128)S(1)} collective-permute-done((f32[136,256]{1,0:T(8,128)S(1)}, f32[136,256]{1,0:T(8,128)S(1)}, u32[]{:S(2)}, u32[]{:S(2)}) %collective-permute-start.15) | collective-permute-done | bytes 139296 | tf_op jit(solution)/shard_map/ppermute | solution.py:187
  24.1 7.3 %collective-permute-done.14 = f32[136,256]{1,0:T(8,128)S(1)} collective-permute-done((f32[136,256]{1,0:T(8,128)S(1)}, f32[136,256]{1,0:T(8,128)S(1)}, u32[]{:S(2)}, u32[]{:S(2)}) %collective-permute-start.14) | collective-permute-done | bytes 139296 | tf_op jit(solution)/shard_map/ppermute | solution.py:187
  31.4 0.0 collective-permute-done.13
  31.4 0.1 collective-permute-start.16
  31.5 0.0 copy-done.2
  31.5 1.3 %shard_map.41 = (s32[3,4]{1,0:T(4,128)S(1)}, s32[1,1]{1,0:T(1,128)}) custom-call(s32[2,8]{1,0:T(2,128)S(1)} %copy-done.2), custom_call_target="tpu_custom_call" | custom-call | tf_op jit(solution)/shard_map/pallas_call | solution.py:218
  33.4 0.0 collective-permute-done.16.other_ref
  33.5 4.6 %shard_map.44 = (f32[256,256]{1,0:T(8,128)S(1)}, f32[256,256]{1,0:T(8,128)S(1)}) custom-call(s32[3,4]{1,0:T(4,128)S(1)} %get-tuple-element.51.table_ref, f32[136,256]{1,0:T(8,128)S(1)} %add_add_fusion.1.mine_ref, f32[136,256]{1,0:T(8,128)S(1)} %collective-permute-done.16.other_ref, f32[256,512]{1,0:T(8,128)S(1)} %get-tuple-element.58.local_ref), custom_call_target="tpu_custom_call" | custom-call | tf_op jit(solution)/shard_map/pallas_call | solution.py:218
  38.0 9.8 %conditional.1 = (f32[256,256]{1,0:T(8,128)}) conditional(s32[]{:T(128)} %bitcast, f32[256,256]{1,0:T(8,128)S(1)} %get-tuple-element.61, f32[256,256]{1,0:T(8,128)S(1)} %get-tuple-element.61, f32[256,256]{1,0:T(8,128)S(1)} %get-tuple-element.61, f32[256,256]{1,0:T(8,128)S(1)} %get-tuple-element.61, ...), branch_computations={%region_0.0_spmd, %region_1.0_spmd, %region_2.0_spmd, %region_3.0_... | conditional | bytes 1048624 | solution.py:211
  38.1 1.3 %collective-permute-start.1 = (f32[256,256]{1,0:T(8,128)S(1)}, f32[256,256]{1,0:T(8,128)}, u32[]{:S(2)}, u32[]{:S(2)}) collective-permute-start(f32[256,256]{1,0:T(8,128)S(1)} %param.1), channel_id=1, source_target_pairs={{0,1},{1,2},{2,3},{3,0},{4,5},{5,6},{6,7},{7,4},{8,9},{9,10},{10,1... | collective-permute-start | bytes 786440 | tf_op jit(solution)/shard_map/cond/branch_1_fun/ppermute | solution.py:210
  39.3 8.5 %collective-permute-done.1 = f32[256,256]{1,0:T(8,128)} collective-permute-done((f32[256,256]{1,0:T(8,128)S(1)}, f32[256,256]{1,0:T(8,128)}, u32[]{:S(2)}, u32[]{:S(2)}) %collective-permute-start.1) | collective-permute-done | bytes 262176 | tf_op jit(solution)/shard_map/cond/branch_1_fun/ppermute | solution.py:210
  47.8 1.4 %shard_map.45 = (f32[256,512]{1,0:T(8,128)S(1)}, f32[136,256]{1,0:T(8,128)S(1)}, f32[136,256]{1,0:T(8,128)S(1)}) custom-call(s32[2,8]{1,0:T(2,128)S(1)} %copy-done.2, s32[3,4]{1,0:T(4,128)S(1)} %get-tuple-element.51.table_ref, f32[256,256]{1,0:T(8,128)S(1)} %get-tuple-element.59.kept_ref, f32[256,256]{1,0:T(8,128)} %get-tuple-element.81.refs_0_), custom_call_target="tpu_custom_call" | custom-call | tf_op jit(solution)/shard_map/pallas_call | solution.py:218
  49.2 0.1 collective-permute-start.17
  49.3 1.3 %collective-permute-done.17 = f32[136,256]{1,0:T(8,128)S(1)} collective-permute-done((f32[136,256]{1,0:T(8,128)S(1)}, f32[136,256]{1,0:T(8,128)S(1)}, u32[]{:S(2)}, u32[]{:S(2)}) %collective-permute-start.17) | collective-permute-done | bytes 139296 | tf_op jit(solution)/shard_map/ppermute | solution.py:187
  50.6 2.5 %collective-permute-start.20 = (f32[136,256]{1,0:T(8,128)S(1)}, f32[136,256]{1,0:T(8,128)S(1)}, u32[]{:S(2)}, u32[]{:S(2)}) collective-permute-start(f32[136,256]{1,0:T(8,128)S(1)} %add.43), channel_id=1, source_target_pairs={{0,24},{4,28},{8,16},{12,20},{16,8},{20,12},{24,0},{28,4},{1,25},{... | collective-permute-start | bytes 417800 | tf_op jit(solution)/shard_map/ppermute | solution.py:187
  53.2 0.0 collective-permute-start.19
  53.2 1.9 %collective-permute-start.18 = (f32[136,256]{1,0:T(8,128)S(1)}, f32[136,256]{1,0:T(8,128)S(1)}, u32[]{:S(2)}, u32[]{:S(2)}) collective-permute-start(f32[136,256]{1,0:T(8,128)S(1)} %add.43), channel_id=1, source_target_pairs={{0,8},{4,12},{8,0},{12,4},{16,24},{20,28},{24,16},{28,20},{1,9},{5... | collective-permute-start | bytes 417800 | tf_op jit(solution)/shard_map/ppermute | solution.py:187
  55.1 4.1 %collective-permute-done.20 = f32[136,256]{1,0:T(8,128)S(1)} collective-permute-done((f32[136,256]{1,0:T(8,128)S(1)}, f32[136,256]{1,0:T(8,128)S(1)}, u32[]{:S(2)}, u32[]{:S(2)}) %collective-permute-start.20) | collective-permute-done | bytes 139296 | tf_op jit(solution)/shard_map/ppermute | solution.py:187
  59.1 5.3 %collective-permute-done.19 = f32[136,256]{1,0:T(8,128)S(1)} collective-permute-done((f32[136,256]{1,0:T(8,128)S(1)}, f32[136,256]{1,0:T(8,128)S(1)}, u32[]{:S(2)}, u32[]{:S(2)}) %collective-permute-start.19) | collective-permute-done | bytes 139296 | tf_op jit(solution)/shard_map/ppermute | solution.py:187
  64.5 0.0 collective-permute-done.18
  64.5 0.1 collective-permute-start.21
  64.6 1.3 %collective-permute-done.21.other_ref = f32[136,256]{1,0:T(8,128)S(1)} collective-permute-done((f32[136,256]{1,0:T(8,128)S(1)}, f32[136,256]{1,0:T(8,128)S(1)}, u32[]{:S(2)}, u32[]{:S(2)}) %collective-permute-start.21) | collective-permute-done | bytes 139296 | tf_op jit(solution)/shard_map/ppermute | solution.py:187
  66.0 4.6 %shard_map.46 = (f32[64,512]{1,0:T(8,128)S(1)}, f32[64,512]{1,0:T(8,128)S(1)}, f32[64,512]{1,0:T(8,128)S(1)}, f32[64,512]{1,0:T(8,128)S(1)}, f32[8,256]{1,0:T(8,128)S(1)}) custom-call(s32[2,8]{1,0:T(2,128)S(1)} %copy-done.2, s32[3,4]{1,0:T(4,128)S(1)} %get-tuple-element.51.table_ref, f32[136,256]{1,0:T(8,128)S(1)} %add_add_fusion.mine_ref, ...), custom_call_target="tpu_custom_call" | custom-call | tf_op jit(solution)/shard_map/pallas_call | solution.py:218
  70.6 0.2 collective-permute-start.22
  70.8 1.0 %collective-permute-done.22 = f32[8,256]{1,0:T(8,128)S(1)} collective-permute-done((f32[8,256]{1,0:T(8,128)S(1)}, f32[8,256]{1,0:T(8,128)S(1)}, u32[]{:S(2)}, u32[]{:S(2)}) %collective-permute-start.22) | collective-permute-done | bytes 8224 | tf_op jit(solution)/shard_map/ppermute | solution.py:187
  71.8 0.4 collective-permute-start.23
  72.3 0.3 collective-permute-start.26
  72.6 1.2 %collective-permute-start.27 = (f32[64,512]{1,0:T(8,128)S(1)}, f32[64,512]{1,0:T(8,128)S(1)}, u32[]{:S(2)}, u32[]{:S(2)}) collective-permute-start(f32[64,512]{1,0:T(8,128)S(1)} %get-tuple-element.74), channel_id=1, source_target_pairs={{0,2},{1,3},{2,0},{3,1},{4,6},{5,7},{6,4},{7,5},{8,10},{9,11},{10,... | collective-permute-start | bytes 393224 | tf_op jit(solution)/shard_map/ppermute | solution.py:187
  73.8 1.7 %collective-permute-done.23 = f32[8,256]{1,0:T(8,128)S(1)} collective-permute-done((f32[8,256]{1,0:T(8,128)S(1)}, f32[8,256]{1,0:T(8,128)S(1)}, u32[]{:S(2)}, u32[]{:S(2)}) %collective-permute-start.23) | collective-permute-done | bytes 8224 | tf_op jit(solution)/shard_map/ppermute | solution.py:187
  75.5 0.6 collective-permute-start.28
  76.1 2.0 %collective-permute-start.24 = (f32[8,256]{1,0:T(8,128)S(1)}, f32[8,256]{1,0:T(8,128)S(1)}, u32[]{:S(2)}, u32[]{:S(2)}) collective-permute-start(f32[8,256]{1,0:T(8,128)S(1)} %add.48), channel_id=1, source_target_pairs={{0,16},{4,20},{8,24},{12,28},{16,0},{20,4},{24,8},{28,12},{1,17},{... | collective-permute-start | bytes 24584 | tf_op jit(solution)/shard_map/ppermute | solution.py:187
  78.1 2.5 %collective-permute-done.24 = f32[8,256]{1,0:T(8,128)S(1)} collective-permute-done((f32[8,256]{1,0:T(8,128)S(1)}, f32[8,256]{1,0:T(8,128)S(1)}, u32[]{:S(2)}, u32[]{:S(2)}) %collective-permute-start.24) | collective-permute-done | bytes 8224 | tf_op jit(solution)/shard_map/ppermute | solution.py:187
  80.6 2.4 %collective-permute-start.25 = (f32[8,256]{1,0:T(8,128)S(1)}, f32[8,256]{1,0:T(8,128)S(1)}, u32[]{:S(2)}, u32[]{:S(2)}) collective-permute-start(f32[8,256]{1,0:T(8,128)S(1)} %add.49), channel_id=1, source_target_pairs={{0,1},{1,0},{2,3},{3,2},{4,5},{5,4},{6,7},{7,6},{8,9},{9,8},{10,11... | collective-permute-start | bytes 24584 | tf_op jit(solution)/shard_map/ppermute | solution.py:187
  83.0 1.6 %collective-permute-done.25 = f32[8,256]{1,0:T(8,128)S(1)} collective-permute-done((f32[8,256]{1,0:T(8,128)S(1)}, f32[8,256]{1,0:T(8,128)S(1)}, u32[]{:S(2)}, u32[]{:S(2)}) %collective-permute-start.25) | collective-permute-done | bytes 8224 | tf_op jit(solution)/shard_map/ppermute | solution.py:187
  84.6 0.0 collective-permute-done.26.refs_1_
  84.7 0.0 collective-permute-done.27.refs_2_
  84.7 0.0 collective-permute-done.28.refs_3_
  84.7 0.9 %collective-permute-start.29 = (f32[8,256]{1,0:T(8,128)S(1)}, f32[8,256]{1,0:T(8,128)S(1)}, u32[]{:S(2)}, u32[]{:S(2)}) collective-permute-start(f32[8,256]{1,0:T(8,128)S(1)} %add.50), channel_id=1, source_target_pairs={{0,2},{1,3},{2,0},{3,1},{4,6},{5,7},{6,4},{7,5},{8,10},{9,11},{10,... | collective-permute-start | bytes 24584 | tf_op jit(solution)/shard_map/ppermute | solution.py:187
  85.6 1.4 %shard_map.47 = f32[64,2048]{1,0:T(8,128)} custom-call(s32[2,8]{1,0:T(2,128)S(1)} %copy-done.2, s32[3,4]{1,0:T(4,128)S(1)} %get-tuple-element.51.table_ref, f32[64,512]{1,0:T(8,128)S(1)} %get-tuple-element.76.refs_0_, f32[64,512]{1,0:T(8,128)S(1)} %collective-permute-done.26.refs_1_, f32[64,512]{1,0:T(8,128)S(1)} %collective-permute-done.27.refs_2_, ...), custom_call_target="tpu_custom_call" | custom-call | bytes 1048576 | tf_op jit(solution)/shard_map/pallas_call | solution.py:218
  87.0 1.4 %collective-permute-done.29 = f32[8,256]{1,0:T(8,128)S(1)} collective-permute-done((f32[8,256]{1,0:T(8,128)S(1)}, f32[8,256]{1,0:T(8,128)S(1)}, u32[]{:S(2)}, u32[]{:S(2)}) %collective-permute-start.29) | collective-permute-done | bytes 8224 | tf_op jit(solution)/shard_map/ppermute | solution.py:187
  88.4 0.6 copy.4
  (9 shorter events, 0.1 us)
Async XLA Ops:
  0.6 1.0 %copy-start = (f32[64,2048]{1,0:T(8,128)S(1)}, f32[64,2048]{1,0:T(8,128)}, u32[]{:S(2)}) copy-start(f32[64,2048]{1,0:T(8,128)} %slab_ref.1) | copy-start | bytes 1572868
  1.7 0.7 copy-start.1
  3.0 6.9 %collective-permute-start.9 = (f32[64,512]{1,0:T(8,128)S(1)}, f32[64,512]{1,0:T(8,128)S(1)}, u32[]{:S(2)}, u32[]{:S(2)}) collective-permute-start(f32[64,512]{1,0:T(8,128)S(1)} %get-tuple-element.53), channel_id=1, source_target_pairs={{0,1},{1,0},{2,3},{3,2},{4,5},{5,4},{6,7},{7,6},{8,9},{9,8},{10,11... | collective-permute-start | bytes 393224 | tf_op jit(solution)/shard_map/ppermute | solution.py:187
  6.0 7.8 %collective-permute-start.10 = (f32[64,512]{1,0:T(8,128)S(1)}, f32[64,512]{1,0:T(8,128)S(1)}, u32[]{:S(2)}, u32[]{:S(2)}) collective-permute-start(f32[64,512]{1,0:T(8,128)S(1)} %get-tuple-element.54), channel_id=1, source_target_pairs={{0,2},{1,3},{2,0},{3,1},{4,6},{5,7},{6,4},{7,5},{8,10},{9,11},{10,... | collective-permute-start | bytes 393224 | tf_op jit(solution)/shard_map/ppermute | solution.py:187
  7.5 6.3 %collective-permute-start.11 = (f32[64,512]{1,0:T(8,128)S(1)}, f32[64,512]{1,0:T(8,128)S(1)}, u32[]{:S(2)}, u32[]{:S(2)}) collective-permute-start(f32[64,512]{1,0:T(8,128)S(1)} %get-tuple-element.55), channel_id=1, source_target_pairs={{0,3},{1,2},{2,1},{3,0},{4,7},{5,6},{6,5},{7,4},{8,11},{9,10},{10,... | collective-permute-start | bytes 393224 | tf_op jit(solution)/shard_map/ppermute | solution.py:187
  14.1 1.4 %collective-permute-start.12 = (f32[136,256]{1,0:T(8,128)S(1)}, f32[136,256]{1,0:T(8,128)S(1)}, u32[]{:S(2)}, u32[]{:S(2)}) collective-permute-start(f32[136,256]{1,0:T(8,128)S(1)} %get-tuple-element.57), channel_id=1, source_target_pairs={{0,4},{4,0},{8,12},{12,8},{16,20},{20,16},{24,28},{28,24},{1,5},{5... | collective-permute-start | bytes 417800 | tf_op jit(solution)/shard_map/ppermute | solution.py:187
  15.6 15.9 %copy-start.2 = (s32[2,8]{1,0:T(2,128)S(1)}, s32[2,8]{1,0:T(2,128)}, u32[]{:S(2)}) copy-start(s32[2,8]{1,0:T(2,128)} %plan_ref.9) | copy-start | bytes 196
  15.6 8.5 %collective-permute-start.15 = (f32[136,256]{1,0:T(8,128)S(1)}, f32[136,256]{1,0:T(8,128)S(1)}, u32[]{:S(2)}, u32[]{:S(2)}) collective-permute-start(f32[136,256]{1,0:T(8,128)S(1)} %add.39), channel_id=1, source_target_pairs={{0,24},{4,28},{8,16},{12,20},{16,8},{20,12},{24,0},{28,4},{1,25},{... | collective-permute-start | bytes 417800 | tf_op jit(solution)/shard_map/ppermute | solution.py:187
  19.3 12.1 %collective-permute-start.14 = (f32[136,256]{1,0:T(8,128)S(1)}, f32[136,256]{1,0:T(8,128)S(1)}, u32[]{:S(2)}, u32[]{:S(2)}) collective-permute-start(f32[136,256]{1,0:T(8,128)S(1)} %add.39), channel_id=1, source_target_pairs={{0,16},{4,20},{8,24},{12,28},{16,0},{20,4},{24,8},{28,12},{1,17},{... | collective-permute-start | bytes 417800 | tf_op jit(solution)/shard_map/ppermute | solution.py:187
  19.3 12.1 %collective-permute-start.13 = (f32[136,256]{1,0:T(8,128)S(1)}, f32[136,256]{1,0:T(8,128)S(1)}, u32[]{:S(2)}, u32[]{:S(2)}) collective-permute-start(f32[136,256]{1,0:T(8,128)S(1)} %add.39), channel_id=1, source_target_pairs={{0,8},{4,12},{8,0},{12,4},{16,24},{20,28},{24,16},{28,20},{1,9},{5... | collective-permute-start | bytes 417800 | tf_op jit(solution)/shard_map/ppermute | solution.py:187
  31.4 2.0 %collective-permute-start.16 = (f32[136,256]{1,0:T(8,128)S(1)}, f32[136,256]{1,0:T(8,128)S(1)}, u32[]{:S(2)}, u32[]{:S(2)}) collective-permute-start(f32[136,256]{1,0:T(8,128)S(1)} %add_add_fusion.1.mine_ref), channel_id=1, source_target_pairs={{0,4},{4,0},{8,12},{12,8},{16,20},{20,16},{24,28},{28,24},{1,5},{5... | collective-permute-start | bytes 417800 | tf_op jit(solution)/shard_map/ppermute | solution.py:187
  38.1 9.8 %collective-permute-start.1 = (f32[256,256]{1,0:T(8,128)S(1)}, f32[256,256]{1,0:T(8,128)}, u32[]{:S(2)}, u32[]{:S(2)}) collective-permute-start(f32[256,256]{1,0:T(8,128)S(1)} %param.1), channel_id=1, source_target_pairs={{0,1},{1,2},{2,3},{3,0},{4,5},{5,6},{6,7},{7,4},{8,9},{9,10},{10,1... | collective-permute-start | bytes 786440 | tf_op jit(solution)/shard_map/cond/branch_1_fun/ppermute | solution.py:210
  49.2 1.4 %collective-permute-start.17 = (f32[136,256]{1,0:T(8,128)S(1)}, f32[136,256]{1,0:T(8,128)S(1)}, u32[]{:S(2)}, u32[]{:S(2)}) collective-permute-start(f32[136,256]{1,0:T(8,128)S(1)} %get-tuple-element.63), channel_id=1, source_target_pairs={{0,4},{4,0},{8,12},{12,8},{16,20},{20,16},{24,28},{28,24},{1,5},{5... | collective-permute-start | bytes 417800 | tf_op jit(solution)/shard_map/ppermute | solution.py:187
  50.6 8.5 %collective-permute-start.20 = (f32[136,256]{1,0:T(8,128)S(1)}, f32[136,256]{1,0:T(8,128)S(1)}, u32[]{:S(2)}, u32[]{:S(2)}) collective-permute-start(f32[136,256]{1,0:T(8,128)S(1)} %add.43), channel_id=1, source_target_pairs={{0,24},{4,28},{8,16},{12,20},{16,8},{20,12},{24,0},{28,4},{1,25},{... | collective-permute-start | bytes 417800 | tf_op jit(solution)/shard_map/ppermute | solution.py:187
  53.2 11.3 %collective-permute-start.19 = (f32[136,256]{1,0:T(8,128)S(1)}, f32[136,256]{1,0:T(8,128)S(1)}, u32[]{:S(2)}, u32[]{:S(2)}) collective-permute-start(f32[136,256]{1,0:T(8,128)S(1)} %add.43), channel_id=1, source_target_pairs={{0,16},{4,20},{8,24},{12,28},{16,0},{20,4},{24,8},{28,12},{1,17},{... | collective-permute-start | bytes 417800 | tf_op jit(solution)/shard_map/ppermute | solution.py:187
  53.2 11.3 %collective-permute-start.18 = (f32[136,256]{1,0:T(8,128)S(1)}, f32[136,256]{1,0:T(8,128)S(1)}, u32[]{:S(2)}, u32[]{:S(2)}) collective-permute-start(f32[136,256]{1,0:T(8,128)S(1)} %add.43), channel_id=1, source_target_pairs={{0,8},{4,12},{8,0},{12,4},{16,24},{20,28},{24,16},{28,20},{1,9},{5... | collective-permute-start | bytes 417800 | tf_op jit(solution)/shard_map/ppermute | solution.py:187
  64.5 1.4 %collective-permute-start.21 = (f32[136,256]{1,0:T(8,128)S(1)}, f32[136,256]{1,0:T(8,128)S(1)}, u32[]{:S(2)}, u32[]{:S(2)}) collective-permute-start(f32[136,256]{1,0:T(8,128)S(1)} %add_add_fusion.mine_ref), channel_id=1, source_target_pairs={{0,4},{4,0},{8,12},{12,8},{16,20},{20,16},{24,28},{28,24},{1,5},{5... | collective-permute-start | bytes 417800 | tf_op jit(solution)/shard_map/ppermute | solution.py:187
  70.6 1.2 %collective-permute-start.22 = (f32[8,256]{1,0:T(8,128)S(1)}, f32[8,256]{1,0:T(8,128)S(1)}, u32[]{:S(2)}, u32[]{:S(2)}) collective-permute-start(f32[8,256]{1,0:T(8,128)S(1)} %get-tuple-element.67), channel_id=1, source_target_pairs={{0,4},{4,0},{8,12},{12,8},{16,20},{20,16},{24,28},{28,24},{1,5},{5... | collective-permute-start | bytes 24584 | tf_op jit(solution)/shard_map/ppermute | solution.py:187
  71.8 3.7 %collective-permute-start.23 = (f32[8,256]{1,0:T(8,128)S(1)}, f32[8,256]{1,0:T(8,128)S(1)}, u32[]{:S(2)}, u32[]{:S(2)}) collective-permute-start(f32[8,256]{1,0:T(8,128)S(1)} %add.47), channel_id=1, source_target_pairs={{0,8},{4,12},{8,0},{12,4},{16,24},{20,28},{24,16},{28,20},{1,9},{5... | collective-permute-start | bytes 24584 | tf_op jit(solution)/shard_map/ppermute | solution.py:187
  72.3 12.4 %collective-permute-start.26 = (f32[64,512]{1,0:T(8,128)S(1)}, f32[64,512]{1,0:T(8,128)S(1)}, u32[]{:S(2)}, u32[]{:S(2)}) collective-permute-start(f32[64,512]{1,0:T(8,128)S(1)} %get-tuple-element.73), channel_id=1, source_target_pairs={{0,1},{1,0},{2,3},{3,2},{4,5},{5,4},{6,7},{7,6},{8,9},{9,8},{10,11... | collective-permute-start | bytes 393224 | tf_op jit(solution)/shard_map/ppermute | solution.py:187
  72.6 12.1 %collective-permute-start.27 = (f32[64,512]{1,0:T(8,128)S(1)}, f32[64,512]{1,0:T(8,128)S(1)}, u32[]{:S(2)}, u32[]{:S(2)}) collective-permute-start(f32[64,512]{1,0:T(8,128)S(1)} %get-tuple-element.74), channel_id=1, source_target_pairs={{0,2},{1,3},{2,0},{3,1},{4,6},{5,7},{6,4},{7,5},{8,10},{9,11},{10,... | collective-permute-start | bytes 393224 | tf_op jit(solution)/shard_map/ppermute | solution.py:187
  75.5 9.2 %collective-permute-start.28 = (f32[64,512]{1,0:T(8,128)S(1)}, f32[64,512]{1,0:T(8,128)S(1)}, u32[]{:S(2)}, u32[]{:S(2)}) collective-permute-start(f32[64,512]{1,0:T(8,128)S(1)} %get-tuple-element.75), channel_id=1, source_target_pairs={{0,3},{1,2},{2,1},{3,0},{4,7},{5,6},{6,5},{7,4},{8,11},{9,10},{10,... | collective-permute-start | bytes 393224 | tf_op jit(solution)/shard_map/ppermute | solution.py:187
  76.1 4.5 %collective-permute-start.24 = (f32[8,256]{1,0:T(8,128)S(1)}, f32[8,256]{1,0:T(8,128)S(1)}, u32[]{:S(2)}, u32[]{:S(2)}) collective-permute-start(f32[8,256]{1,0:T(8,128)S(1)} %add.48), channel_id=1, source_target_pairs={{0,16},{4,20},{8,24},{12,28},{16,0},{20,4},{24,8},{28,12},{1,17},{... | collective-permute-start | bytes 24584 | tf_op jit(solution)/shard_map/ppermute | solution.py:187
  80.6 4.0 %collective-permute-start.25 = (f32[8,256]{1,0:T(8,128)S(1)}, f32[8,256]{1,0:T(8,128)S(1)}, u32[]{:S(2)}, u32[]{:S(2)}) collective-permute-start(f32[8,256]{1,0:T(8,128)S(1)} %add.49), channel_id=1, source_target_pairs={{0,1},{1,0},{2,3},{3,2},{4,5},{5,4},{6,7},{7,6},{8,9},{9,8},{10,11... | collective-permute-start | bytes 24584 | tf_op jit(solution)/shard_map/ppermute | solution.py:187
  84.7 3.7 %collective-permute-start.29 = (f32[8,256]{1,0:T(8,128)S(1)}, f32[8,256]{1,0:T(8,128)S(1)}, u32[]{:S(2)}, u32[]{:S(2)}) collective-permute-start(f32[8,256]{1,0:T(8,128)S(1)} %add.50), channel_id=1, source_target_pairs={{0,2},{1,3},{2,0},{3,1},{4,6},{5,7},{6,4},{7,5},{8,10},{9,11},{10,... | collective-permute-start | bytes 24584 | tf_op jit(solution)/shard_map/ppermute | solution.py:187

commit v3 on v2

v3 whole, which is shorter than its diff:
```python
import functools

import jax
import jax.numpy as jnp
from jax import lax
from jax.experimental import pallas as pl
from jax.experimental.pallas import tpu as pltpu
from jax.sharding import PartitionSpec as P

NS_STEPS = 4
PAD = 8
LANES = 128
NOTES = PAIR, KEEPS, NEXT, COMES_FROM = range(4)

VMEM = pl.BlockSpec(memory_space=pltpu.VMEM)
SMEM = pl.BlockSpec(memory_space=pltpu.SMEM)
HBM = pl.BlockSpec(memory_space=pltpu.HBM)
COLS_BY_COLS = (((0,), (0,)), ((), ()))


def split(x):
    high = x.astype(jnp.bfloat16)
    return high, (x - high.astype(jnp.float32)).astype(jnp.bfloat16)


def mul(a, b):
    dot = functools.partial(jnp.dot, preferred_element_type=jnp.float32)
    rows = a[0].shape[0]
    both = dot(jnp.concatenate(a, axis=0), b[0])
    return both[:rows] + (both[rows:] + dot(a[0], b[1]))


def mul_by_cols(a, b):
    dot = functools.partial(lax.dot_general, dimension_numbers=COLS_BY_COLS, preferred_element_type=jnp.float32)
    return dot(a[0], b[0]) + (dot(a[0], b[1]) + dot(a[1], b[0]))


def slot_of(plan_ref, rnd, block, count):
    found = jnp.int32(0)
    for slot in range(1, count):
        found = jnp.where(plan_ref[rnd, slot] == block, slot, found)
    return found


def note(table_ref, kind, device):
    return table_ref[table_ref.shape[0] - len(NOTES) + kind, device]


def sender(table_ref, me):
    return note(table_ref, COMES_FROM, me)


def lay_out(plan_ref, table_ref, rnd):
    rounds, slots = plan_ref.shape
    count = slots // 2
    for row in range(rounds):
        for slot in range(slots):
            table_ref[row, slot] = plan_ref[row, slot]
    pair, half, seen, start = jnp.int32(0), jnp.int32(0), jnp.int32(0), jnp.int32(0)
    for step in range(count):
        device, before = step ^ (step >> 1), (step - 1) ^ ((step - 1) >> 1)
        seen = seen | (jnp.int32(1) << pair)
        table_ref[rounds + PAIR, device] = pair
        table_ref[rounds + KEEPS, device] = half
        table_ref[rounds + NEXT, device] = slot_of(plan_ref, rnd + 1, plan_ref[rnd, 2 * pair + half], slots) // 2
        table_ref[rounds + COMES_FROM, device] = before if step else 0
        table_ref[rounds + COMES_FROM, start] = device
        slot = slot_of(plan_ref, rnd + 1, plan_ref[rnd, 2 * pair + 1 - half], slots)
        joins = slot_of(plan_ref, rnd, plan_ref[rnd + 1, slot ^ 1], slots)
        closed = ((seen >> (joins // 2)) & 1) == 1
        unseen = jnp.int32(0)
        for other in reversed(range(count)):
            unseen = jnp.where(((seen >> other) & 1) == 0, other, unseen)
        pair, half = jnp.where(closed, unseen, joins // 2), jnp.where(closed, 0, joins % 2)
        start = jnp.where(closed, (step + 1) ^ ((step + 1) >> 1), start)


def deal_kernel(plan_hbm, slab_hbm, table_ref, *refs, rnd):
    *outs, plan_ref, slab_ref, plan_sem, slab_sem = refs
    slab_copy = pltpu.make_async_copy(slab_hbm, slab_ref, slab_sem)
    slab_copy.start()
    plan_copy = pltpu.make_async_copy(plan_hbm, plan_ref, plan_sem)
    plan_copy.start()
    plan_copy.wait()
    lay_out(plan_ref, table_ref, rnd)
    slab_copy.wait()
    me = lax.axis_index("pair")
    width = outs[0].shape[1] // 2
    for mask, out in enumerate(outs):
        pair = note(table_ref, PAIR, me ^ mask)
        for half in range(2):
            block = plan_ref[rnd, 2 * pair + half]
            start = pl.multiple_of(block * width, width)
            out[:, half * width : (half + 1) * width] = slab_ref[:, pl.ds(start, width)]


def cross_of(first, second, keep_ref, send_ref, scratch):
    width = first.shape[1]
    scratch[...] = mul_by_cols(split(first), split(second))
    diag = jnp.concatenate(
        [
            jnp.sum(first * first, axis=0, keepdims=True),
            jnp.sum(second * second, axis=0, keepdims=True),
            jnp.zeros((PAD - 2, width), jnp.float32),
        ],
        axis=0,
    )
    core = lax.axis_index("row") & 1
    part = width // 2
    for ref, which in ((keep_ref, core), (send_ref, 1 - core)):
        ref[:part, :] = scratch[pl.ds(pl.multiple_of(which * part, part), part), :]
        ref[part:, :] = diag


def copy_kernel(in_ref, out_ref):
    out_ref[...] = in_ref[...]


def first_cross_kernel(*refs):
    *ins, local_ref, keep_ref, send_ref, scratch = refs
    me = lax.axis_index("pair")
    rows = ins[0].shape[0]
    width = ins[0].shape[1] // 2
    for mask, ref in enumerate(ins):
        local_ref[pl.ds(pl.multiple_of((me ^ mask) * rows, rows), rows), :] = ref[...]
    cross_of(local_ref[:, :width], local_ref[:, width:], keep_ref, send_ref, scratch)


def coupling_of(mine, other):
    part = mine.shape[0] - PAD
    upper = (lax.axis_index("row") & 1) == 0
    cross = jnp.concatenate(
        [jnp.where(upper, mine[:part], other[:part]), jnp.where(upper, other[:part], mine[:part])], axis=0
    )
    diag_first = jnp.transpose(mine[part:])[:, :1]
    diag_second = mine[part + 1 : part + 2]
    coupling = cross / (diag_first + diag_second + 1e-06)
    return coupling, jnp.transpose(coupling)


def turned(sides):
    width = sides[0][0].shape[0]
    ident = lax.broadcasted_iota(jnp.int32, (width, width), 0) == lax.broadcasted_iota(jnp.int32, (width, width), 1)
    scales, squares, blocks = [], [], []
    for k, kt, block, sign, partner in sides:
        inv_sq = 1.0 / (1.0 + jnp.sum(k * k))
        product = mul(split(jnp.concatenate([k, partner], axis=0)), split(kt))
        square = product[:width]
        squares.append(jnp.where(ident, square + 1.0, square) * inv_sq)
        blocks.append(block + sign * product[width:])
        scales.append(jnp.sqrt(inv_sq))
    for step in range(NS_STEPS):
        moves = []
        for square in squares:
            half = -0.5 * square
            moves.append(split(jnp.where(ident, half + 1.5, half)))
        if step < NS_STEPS - 1:
            products = [
                mul(split(jnp.concatenate([square, block], axis=0)), move)
                for square, block, move in zip(squares, blocks, moves)
            ]
            squares = [mul(split(product[:width]), move) for product, move in zip(products, moves)]
            blocks = [product[width:] for product in products]
        else:
            blocks = [mul(split(block), move) for block, move in zip(blocks, moves)]
    return [block * scale for block, scale in zip(blocks, scales)]


def half_of(ref, half):
    width = ref.shape[1] // 2
    return ref[:, pl.ds(pl.multiple_of(half * width, width), width)]


def turn_kernel(table_ref, mine_ref, other_ref, local_ref, *refs, rnd, masks):
    came_refs, came_other_refs, raw_refs = (refs[i * len(masks) : (i + 1) * len(masks)] for i in range(3))
    outs = refs[3 * len(masks) :]
    next_ref, keep_ref, send_ref, scratch = outs
    me = lax.axis_index("pair")
    kept = note(table_ref, KEEPS, me)
    gets = 1 - note(table_ref, KEEPS, sender(table_ref, me))
    source = sender(table_ref, me)

    def pick(parts):
        picked = parts[0]
        for mask, part in zip(masks[1:], parts[1:]):
            picked = jnp.where(source == (me ^ mask), part, picked)
        return picked

    sides = []
    for half, mine, other, halves in (
        (kept, mine_ref[...], other_ref[...], [half_of(local_ref, kept), half_of(local_ref, 1 - kept)]),
        (
            gets,
            pick([ref[...] for ref in came_refs]),
            pick([ref[...] for ref in came_other_refs]),
            [pick([half_of(ref, half) for ref in raw_refs]) for half in (gets, 1 - gets)],
        ),
    ):
        k, kt = coupling_of(mine, other)
        is_first = half == 0
        sides.append(
            (
                jnp.where(is_first, k, kt),
                jnp.where(is_first, kt, k),
                halves[0],
                jnp.where(is_first, -1.0, 1.0),
                halves[1],
            )
        )
    new = turned(sides)
    kept_first = table_ref[rnd, 2 * note(table_ref, PAIR, me) + kept] == table_ref[rnd + 1, 2 * note(table_ref, NEXT, me)]
    first = jnp.where(kept_first, new[0], new[1])
    second = jnp.where(kept_first, new[1], new[0])
    width = first.shape[1]
    next_ref[:, :width] = first
    next_ref[:, width:] = second
    cross_of(first, second, keep_ref, send_ref, scratch)


def last_turn_kernel(table_ref, mine_ref, other_ref, local_ref, *refs, rnd):
    *outs, squares_ref, scratch = refs
    width = local_ref.shape[1] // 2
    first, second = local_ref[:, :width], local_ref[:, width:]
    k, kt = coupling_of(mine_ref[...], other_ref[...])
    new = turned([(k, kt, first, -1.0, second), (kt, k, second, 1.0, first)])
    me = lax.axis_index("pair")
    squares_ref[...] = jnp.zeros_like(squares_ref)
    for half in range(2):
        scratch[:, half * width : (half + 1) * width] = new[half]
        block = table_ref[rnd, 2 * note(table_ref, NEXT, me) + half]
        sums = jnp.sum(new[half] * new[half], axis=0, keepdims=True)
        for lane in range(0, width, LANES):
            squares_ref[pl.ds((block * width + lane) // LANES, 1), :] = sums[:, lane : lane + LANES]
    rows = outs[0].shape[0]
    for mask, out in enumerate(outs):
        out[...] = scratch[pl.ds(pl.multiple_of((me ^ mask) * rows, rows), rows), :]


def place_kernel(table_ref, *refs, rnd):
    *ins, out_ref = refs
    width = ins[0].shape[1] // 2
    me = lax.axis_index("pair")
    for mask, ref in enumerate(ins):
        for half in range(2):
            block = table_ref[rnd, 2 * note(table_ref, NEXT, me ^ mask) + half]
            start = pl.multiple_of(block * width, width)
            out_ref[:, pl.ds(start, width)] = ref[:, half * width : (half + 1) * width]


def swap(x, axis, mask):
    return lax.ppermute(x, axis, [(i, i ^ mask) for i in range(lax.axis_size(axis))])


def spread(parts):
    return [parts[0]] + [swap(parts[mask], "pair", mask) for mask in range(1, len(parts))]


def tree_sum(parts):
    while len(parts) > 1:
        parts = [a + b for a, b in zip(parts[::2], parts[1::2])]
    return parts[0]


def over_chips(x):
    return tree_sum([x] + [swap(x, "row", mask) for mask in range(2, lax.axis_size("row"), 2)])


def powers(size):
    return [1 << bit for bit in range(size.bit_length() - 1)]


def call(kernel, ins, outs, scratch=(), table=None, cost=None):
    ins = ([] if table is None else [table]) + ins
    return pl.pallas_call(
        kernel,
        out_shape=[jax.ShapeDtypeStruct(shape, jnp.float32) for shape in outs],
        in_specs=[SMEM] * (table is not None) + [VMEM] * (len(ins) - (table is not None)),
        out_specs=[VMEM] * len(outs),
        scratch_shapes=[pltpu.VMEM(shape, jnp.float32) for shape in scratch],
        compiler_params=pltpu.CompilerParams(vmem_limit_bytes=24 * 2**20),
        cost_estimate=cost,
    )(*ins)


def deal(plan, slab, rnd):
    piece_rows, ncols = slab.shape
    rounds, blocks = plan.shape
    pieces = [jax.ShapeDtypeStruct((piece_rows, 2 * ncols // blocks), jnp.float32)] * (blocks // 2)
    table, *pieces = pl.pallas_call(
        functools.partial(deal_kernel, rnd=rnd),
        out_shape=[jax.ShapeDtypeStruct((rounds + len(NOTES), blocks), jnp.int32)] + pieces,
        in_specs=[HBM, HBM],
        out_specs=[SMEM] + [VMEM] * len(pieces),
        scratch_shapes=[
            pltpu.SMEM(plan.shape, jnp.int32),
            pltpu.VMEM(slab.shape, jnp.float32),
            pltpu.SemaphoreType.DMA,
            pltpu.SemaphoreType.DMA,
        ],
        compiler_params=pltpu.CompilerParams(vmem_limit_bytes=58 * 2**20),
    )(plan, slab)
    return table, pieces


def on_device(slab, plan):
    piece_rows, ncols = slab.shape
    pair_count = lax.axis_size("pair")
    both = ncols // pair_count
    width = both // 2
    group_rows = piece_rows * pair_count
    total_rows = group_rows * lax.axis_size("row")
    crossed = [(group_rows, both), (width // 2 + PAD, width), (width // 2 + PAD, width)]
    square = (width, width)
    masks = powers(pair_count) if pair_count <= 4 else list(range(1, pair_count))

    table, dealt = deal(plan, slab, 0)
    own, *others = spread(dealt)
    own = call(copy_kernel, [own], [own.shape])
    local, keep, send = call(first_cross_kernel, [*own, *others], crossed, [square])
    raw = [swap(local, "pair", mask) for mask in masks]
    mine = over_chips(keep + swap(send, "row", 1))
    came = [swap(mine, "pair", mask) for mask in masks]
    came_other = [swap(x, "row", 1) for x in came]
    local, keep, send = call(
        functools.partial(turn_kernel, rnd=0, masks=masks),
        [mine, swap(mine, "row", 1), local] + came + came_other + raw,
        crossed,
        [square],
        table,
    )
    mine = over_chips(keep + swap(send, "row", 1))
    *sent, squares = call(
        functools.partial(last_turn_kernel, rnd=1),
        [mine, swap(mine, "row", 1), local],
        [(piece_rows, both)] * pair_count + [(ncols // LANES, LANES)],
        [(group_rows, both)],
        table,
    )
    back = spread(sent)
    squares = over_chips(squares + swap(squares, "row", 1))
    hops = powers(pair_count)
    for mask in hops[:-1]:
        squares = squares + swap(squares, "pair", mask)
    squares, back = lax.optimization_barrier((squares, back))
    squares = squares + swap(squares, "pair", hops[-1])
    (rotated,) = call(
        functools.partial(place_kernel, rnd=1),
        back,
        [(piece_rows, ncols)],
        table=table,
        cost=pl.CostEstimate(flops=0, bytes_accessed=8 * slab.size, transcendentals=0),
    )
    return rotated, jnp.sqrt(squares / total_rows).reshape(ncols)


def solution(mesh):
    specs = (P(("row", "pair"), None), P())
    return jax.shard_map(on_device, mesh=mesh, in_specs=specs, out_specs=specs, check_vma=False)
```

time: 89 us -> 84.3 us (0.947)
  waiting for transfers between devices: 47.7 us -> 41.6 us
  starting transfers between devices: 23.1 us -> 27.6 us
  Pallas kernels: 14.3 us -> 12.6 us
  local copies, waits for them, and re-layouts: 2.33 us -> 0.91 us
    ppermute x1 -> x0, waiting for transfers between devices: 8.49 us -> none  [hand_on(): lax.ppermute(x, 'pair', list(enumerate(move)))]
    ppermute x21 -> x28, starting transfers between devices: 21.8 us -> 27.6 us  [swap(): lax.ppermute(x, axis, [(i, i ^ mask) for i in range(lax.axis_size(axis))])]
    ppermute x21 -> x28, waiting for transfers between devices: 39.3 us -> 41.6 us  [swap(): lax.ppermute(x, axis, [(i, i ^ mask) for i in range(lax.axis_size(axis))])]
    pallas_call x7 -> x6, Pallas kernels: 14.3 us -> 12.6 us  [the longest x5 10.7 us: call(): pl.pallas_call(kernel, out_shape=[jax.ShapeDtypeStruct(shape, jnp.float32...]
    unnamed x7 -> x4, local copies, waits for them, and re-layouts: 2.33 us -> 0.91 us
    ppermute x1 -> x0, starting transfers between devices: 1.27 us -> none  [hand_on(): lax.ppermute(x, 'pair', list(enumerate(move)))]
  transfers between devices with their start and end apart: 22 -> 28, of which waited for: 15 -> 16; matrix products, arithmetic and copies ran while one was open for 0% -> 0% of each run, Pallas kernels for 3% -> 2%
where the time goes in v3:
time: 84.3 us; the launch traced here: 84.1 us
  waiting for transfers between devices  41.6 us (49%)
  starting transfers between devices  27.6 us (33%)
  Pallas kernels  12.6 us (15%)
  local copies, waits for them, and re-layouts  0.91 us (1%)
    ppermute x28, waiting for transfers between devices, swap(): lax.ppermute(x, axis, [(i, i ^ mask) for i in range(lax.axis_size(axis))])  41.6 us
    ppermute x28, starting transfers between devices, swap(): lax.ppermute(x, axis, [(i, i ^ mask) for i in range(lax.axis_size(axis))])  27.6 us
    pallas_call x5, Pallas kernels, call(): pl.pallas_call(kernel, out_shape=[jax.ShapeDtypeStruct(shape, jnp.float32...  10.7 us
    pallas_call x1, Pallas kernels, deal(): pl.pallas_call(functools.partial(deal_kernel, rnd=rnd), out_shape=[jax.Sh...  1.88 us
  transfers between devices with their start and end apart: 28, of which 16 were waited for; matrix products, arithmetic and copies ran while one was open for 0% of the time, Pallas kernels for 2%

profile of v3, /device:TPU:0, one launch (start us, length us, event | category | flops | bytes accessed | tf_op | source)
XLA Modules:
  0.0 84.1 jit_solution(5849131682036986737)
XLA Ops:
  0.6 1.9 %shard_map.41 = (s32[6,8]{1,0:T(8,128)}, f32[64,512]{1,0:T(8,128)}, f32[64,512]{1,0:T(8,128)}, f32[64,512]{1,0:T(8,128)}, f32[64,512]{1,0:T(8,128)}) custom-call(s32[2,8]{1,0:T(2,128)} %plan_hbm.1, f32[64,2048]{1,0:T(8,128)} %slab_hbm.1), custom_call_target="tpu_custom_call" | custom-call | tf_op jit(solution)/shard_map/pallas_call | solution.py:289
  2.5 3.0 %collective-permute-start = (f32[64,512]{1,0:T(8,128)}, f32[64,512]{1,0:T(8,128)S(1)}, u32[]{:S(2)}, u32[]{:S(2)}) collective-permute-start(f32[64,512]{1,0:T(8,128)} %get-tuple-element.25), channel_id=1, source_target_pairs={{0,1},{1,0},{2,3},{3,2},{4,5},{5,4},{6,7},{7,6},{8,9},{9,8},{10,11... | collective-permute-start | bytes 393224 | tf_op jit(solution)/shard_map/ppermute | solution.py:251
  5.5 1.5 %collective-permute-start.1 = (f32[64,512]{1,0:T(8,128)}, f32[64,512]{1,0:T(8,128)S(1)}, u32[]{:S(2)}, u32[]{:S(2)}) collective-permute-start(f32[64,512]{1,0:T(8,128)} %get-tuple-element.26), channel_id=1, source_target_pairs={{0,2},{1,3},{2,0},{3,1},{4,6},{5,7},{6,4},{7,5},{8,10},{9,11},{10,... | collective-permute-start | bytes 393224 | tf_op jit(solution)/shard_map/ppermute | solution.py:251
  7.0 0.0 collective-permute-start.2
  7.1 0.9 %copy-done = f32[64,512]{1,0:T(8,128)S(1)} copy-done((f32[64,512]{1,0:T(8,128)S(1)}, f32[64,512]{1,0:T(8,128)}, u32[]{:S(2)}) %copy-start) | copy-done | bytes 131096
  8.0 1.8 %collective-permute-done.refs_1_ = f32[64,512]{1,0:T(8,128)S(1)} collective-permute-done((f32[64,512]{1,0:T(8,128)}, f32[64,512]{1,0:T(8,128)S(1)}, u32[]{:S(2)}, u32[]{:S(2)}) %collective-permute-start) | collective-permute-done | bytes 131104 | tf_op jit(solution)/shard_map/ppermute | solution.py:251
  9.7 3.8 %collective-permute-done.1.refs_2_ = f32[64,512]{1,0:T(8,128)S(1)} collective-permute-done((f32[64,512]{1,0:T(8,128)}, f32[64,512]{1,0:T(8,128)S(1)}, u32[]{:S(2)}, u32[]{:S(2)}) %collective-permute-start.1) | collective-permute-done | bytes 131104 | tf_op jit(solution)/shard_map/ppermute | solution.py:251
  13.5 0.0 collective-permute-done.2.refs_3_
  13.5 0.4 shard_map.43
  13.9 0.1 collective-permute-start.3
  14.0 1.3 %collective-permute-done.3 = f32[136,256]{1,0:T(8,128)S(1)} collective-permute-done((f32[136,256]{1,0:T(8,128)S(1)}, f32[136,256]{1,0:T(8,128)S(1)}, u32[]{:S(2)}, u32[]{:S(2)}) %collective-permute-start.3) | collective-permute-done | bytes 139296 | tf_op jit(solution)/shard_map/ppermute | solution.py:251
  15.4 3.7 %collective-permute-start.6 = (f32[136,256]{1,0:T(8,128)S(1)}, f32[136,256]{1,0:T(8,128)S(1)}, u32[]{:S(2)}, u32[]{:S(2)}) collective-permute-start(f32[136,256]{1,0:T(8,128)S(1)} %add.42), channel_id=1, source_target_pairs={{0,24},{4,28},{8,16},{12,20},{16,8},{20,12},{24,0},{28,4},{1,25},{... | collective-permute-start | bytes 417800 | tf_op jit(solution)/shard_map/ppermute | solution.py:251
  19.0 0.0 collective-permute-start.5
  19.0 0.8 collective-permute-start.4
  19.8 1.5 %collective-permute-start.13 = (f32[256,512]{1,0:T(8,128)S(1)}, f32[256,512]{1,0:T(8,128)S(1)}, u32[]{:S(2)}, u32[]{:S(2)}) collective-permute-start(f32[256,512]{1,0:T(8,128)S(1)} %get-tuple-element.30.local_ref), channel_id=1, source_target_pairs={{0,2},{1,3},{2,0},{3,1},{4,6},{5,7},{6,4},{7,5},{8,10},{9,11},{10,... | collective-permute-start | bytes 1572872 | tf_op jit(solution)/shard_map/ppermute | solution.py:251
  21.3 0.5 collective-permute-start.12
  21.9 2.0 %collective-permute-done.6 = f32[136,256]{1,0:T(8,128)S(1)} collective-permute-done((f32[136,256]{1,0:T(8,128)S(1)}, f32[136,256]{1,0:T(8,128)S(1)}, u32[]{:S(2)}, u32[]{:S(2)}) %collective-permute-start.6) | collective-permute-done | bytes 139296 | tf_op jit(solution)/shard_map/ppermute | solution.py:251
  23.8 7.3 %collective-permute-done.5 = f32[136,256]{1,0:T(8,128)S(1)} collective-permute-done((f32[136,256]{1,0:T(8,128)S(1)}, f32[136,256]{1,0:T(8,128)S(1)}, u32[]{:S(2)}, u32[]{:S(2)}) %collective-permute-start.5) | collective-permute-done | bytes 139296 | tf_op jit(solution)/shard_map/ppermute | solution.py:251
  31.1 0.0 collective-permute-done.4
  31.2 1.6 %collective-permute-start.9 = (f32[136,256]{1,0:T(8,128)S(1)}, f32[136,256]{1,0:T(8,128)S(1)}, u32[]{:S(2)}, u32[]{:S(2)}) collective-permute-start(f32[136,256]{1,0:T(8,128)S(1)} %add_add_fusion.1.mine_ref), channel_id=1, source_target_pairs={{0,2},{1,3},{2,0},{3,1},{4,6},{5,7},{6,4},{7,5},{8,10},{9,11},{10,... | collective-permute-start | bytes 417800 | tf_op jit(solution)/shard_map/ppermute | solution.py:251
  32.7 0.5 collective-permute-start.8
  33.3 0.0 collective-permute-start.7
  33.3 3.0 %collective-permute-done.9.refs_1_ = f32[136,256]{1,0:T(8,128)S(1)} collective-permute-done((f32[136,256]{1,0:T(8,128)S(1)}, f32[136,256]{1,0:T(8,128)S(1)}, u32[]{:S(2)}, u32[]{:S(2)}) %collective-permute-start.9) | collective-permute-done | bytes 139296 | tf_op jit(solution)/shard_map/ppermute | solution.py:251
  36.3 0.0 collective-permute-start.11
  36.3 1.5 %collective-permute-done.8.refs_0_ = f32[136,256]{1,0:T(8,128)S(1)} collective-permute-done((f32[136,256]{1,0:T(8,128)S(1)}, f32[136,256]{1,0:T(8,128)S(1)}, u32[]{:S(2)}, u32[]{:S(2)}) %collective-permute-start.8) | collective-permute-done | bytes 139296 | tf_op jit(solution)/shard_map/ppermute | solution.py:251
  37.8 0.0 collective-permute-start.10
  37.8 0.0 collective-permute-done.7.other_ref
  37.8 0.0 collective-permute-done.13.refs_5_
  37.8 0.0 collective-permute-done.12.refs_4_
  37.8 0.0 collective-permute-done.11.refs_3_
  37.8 1.3 %collective-permute-done.10.refs_2_ = f32[136,256]{1,0:T(8,128)S(1)} collective-permute-done((f32[136,256]{1,0:T(8,128)S(1)}, f32[136,256]{1,0:T(8,128)S(1)}, u32[]{:S(2)}, u32[]{:S(2)}) %collective-permute-start.10) | collective-permute-done | bytes 139296 | tf_op jit(solution)/shard_map/ppermute | solution.py:251
  39.2 0.0 copy-done.1
  39.2 4.8 %shard_map.44 = (f32[256,512]{1,0:T(8,128)S(1)}, f32[136,256]{1,0:T(8,128)S(1)}, f32[136,256]{1,0:T(8,128)S(1)}) custom-call(s32[6,8]{1,0:T(8,128)S(1)} %copy-done.1, f32[136,256]{1,0:T(8,128)S(1)} %add_add_fusion.1.mine_ref, f32[136,256]{1,0:T(8,128)S(1)} %collective-permute-done.7.other_ref, f32[256,512]{1,0:T(8,128)S(1)} %get-tuple-element.30.local_ref, ...), custom_call_target="tpu_custom_call" | custom-call | tf_op jit(solution)/shard_map/pallas_call | solution.py:274
  44.0 0.2 collective-permute-start.14
  44.2 1.2 %collective-permute-done.14 = f32[136,256]{1,0:T(8,128)S(1)} collective-permute-done((f32[136,256]{1,0:T(8,128)S(1)}, f32[136,256]{1,0:T(8,128)S(1)}, u32[]{:S(2)}, u32[]{:S(2)}) %collective-permute-start.14) | collective-permute-done | bytes 139296 | tf_op jit(solution)/shard_map/ppermute | solution.py:251
  45.4 3.0 %collective-permute-start.17 = (f32[136,256]{1,0:T(8,128)S(1)}, f32[136,256]{1,0:T(8,128)S(1)}, u32[]{:S(2)}, u32[]{:S(2)}) collective-permute-start(f32[136,256]{1,0:T(8,128)S(1)} %add.46), channel_id=1, source_target_pairs={{0,24},{4,28},{8,16},{12,20},{16,8},{20,12},{24,0},{28,4},{1,25},{... | collective-permute-start | bytes 417800 | tf_op jit(solution)/shard_map/ppermute | solution.py:251
  48.4 0.0 collective-permute-start.16
  48.4 1.4 %collective-permute-start.15 = (f32[136,256]{1,0:T(8,128)S(1)}, f32[136,256]{1,0:T(8,128)S(1)}, u32[]{:S(2)}, u32[]{:S(2)}) collective-permute-start(f32[136,256]{1,0:T(8,128)S(1)} %add.46), channel_id=1, source_target_pairs={{0,8},{4,12},{8,0},{12,4},{16,24},{20,28},{24,16},{28,20},{1,9},{5... | collective-permute-start | bytes 417800 | tf_op jit(solution)/shard_map/ppermute | solution.py:251
  49.9 4.0 %collective-permute-done.17 = f32[136,256]{1,0:T(8,128)S(1)} collective-permute-done((f32[136,256]{1,0:T(8,128)S(1)}, f32[136,256]{1,0:T(8,128)S(1)}, u32[]{:S(2)}, u32[]{:S(2)}) %collective-permute-start.17) | collective-permute-done | bytes 139296 | tf_op jit(solution)/shard_map/ppermute | solution.py:251
  53.9 6.6 %collective-permute-done.16 = f32[136,256]{1,0:T(8,128)S(1)} collective-permute-done((f32[136,256]{1,0:T(8,128)S(1)}, f32[136,256]{1,0:T(8,128)S(1)}, u32[]{:S(2)}, u32[]{:S(2)}) %collective-permute-start.16) | collective-permute-done | bytes 139296 | tf_op jit(solution)/shard_map/ppermute | solution.py:251
  60.5 0.0 collective-permute-done.15
  60.5 0.1 collective-permute-start.18
  60.6 1.3 %collective-permute-done.18.other_ref = f32[136,256]{1,0:T(8,128)S(1)} collective-permute-done((f32[136,256]{1,0:T(8,128)S(1)}, f32[136,256]{1,0:T(8,128)S(1)}, u32[]{:S(2)}, u32[]{:S(2)}) %collective-permute-start.18) | collective-permute-done | bytes 139296 | tf_op jit(solution)/shard_map/ppermute | solution.py:251
  61.9 4.0 %shard_map.45 = (f32[64,512]{1,0:T(8,128)S(1)}, f32[64,512]{1,0:T(8,128)S(1)}, f32[64,512]{1,0:T(8,128)S(1)}, f32[64,512]{1,0:T(8,128)S(1)}, f32[16,128]{1,0:T(8,128)S(1)}) custom-call(s32[6,8]{1,0:T(8,128)S(1)} %copy-done.1, f32[136,256]{1,0:T(8,128)S(1)} %add_add_fusion.mine_ref, f32[136,256]{1,0:T(8,128)S(1)} %collective-permute-done.18.other_ref, ...), custom_call_target="tpu_custom_call" | custom-call | tf_op jit(solution)/shard_map/pallas_call | solution.py:274
  66.0 0.2 collective-permute-start.19
  66.2 1.0 %collective-permute-done.19 = f32[16,128]{1,0:T(8,128)S(1)} collective-permute-done((f32[16,128]{1,0:T(8,128)S(1)}, f32[16,128]{1,0:T(8,128)S(1)}, u32[]{:S(2)}, u32[]{:S(2)}) %collective-permute-start.19) | collective-permute-done | bytes 8224 | tf_op jit(solution)/shard_map/ppermute | solution.py:251
  67.2 2.4 %collective-permute-start.22 = (f32[16,128]{1,0:T(8,128)S(1)}, f32[16,128]{1,0:T(8,128)S(1)}, u32[]{:S(2)}, u32[]{:S(2)}) collective-permute-start(f32[16,128]{1,0:T(8,128)S(1)} %add.50), channel_id=1, source_target_pairs={{0,24},{4,28},{8,16},{12,20},{16,8},{20,12},{24,0},{28,4},{1,25},{... | collective-permute-start | bytes 24584 | tf_op jit(solution)/shard_map/ppermute | solution.py:251
  69.6 0.0 collective-permute-start.21
  69.6 2.0 %collective-permute-start.20 = (f32[16,128]{1,0:T(8,128)S(1)}, f32[16,128]{1,0:T(8,128)S(1)}, u32[]{:S(2)}, u32[]{:S(2)}) collective-permute-start(f32[16,128]{1,0:T(8,128)S(1)} %add.50), channel_id=1, source_target_pairs={{0,8},{4,12},{8,0},{12,4},{16,24},{20,28},{24,16},{28,20},{1,9},{5... | collective-permute-start | bytes 24584 | tf_op jit(solution)/shard_map/ppermute | solution.py:251
  71.6 0.5 collective-permute-start.24
  72.2 1.2 %collective-permute-start.25 = (f32[64,512]{1,0:T(8,128)S(1)}, f32[64,512]{1,0:T(8,128)S(1)}, u32[]{:S(2)}, u32[]{:S(2)}) collective-permute-start(f32[64,512]{1,0:T(8,128)S(1)} %get-tuple-element.37), channel_id=1, source_target_pairs={{0,2},{1,3},{2,0},{3,1},{4,6},{5,7},{6,4},{7,5},{8,10},{9,11},{10,... | collective-permute-start | bytes 393224 | tf_op jit(solution)/shard_map/ppermute | solution.py:251
  73.4 0.0 collective-permute-done.22
  73.4 1.7 %collective-permute-start.26 = (f32[64,512]{1,0:T(8,128)S(1)}, f32[64,512]{1,0:T(8,128)S(1)}, u32[]{:S(2)}, u32[]{:S(2)}) collective-permute-start(f32[64,512]{1,0:T(8,128)S(1)} %get-tuple-element.38), channel_id=1, source_target_pairs={{0,3},{1,2},{2,1},{3,0},{4,7},{5,6},{6,5},{7,4},{8,11},{9,10},{10,... | collective-permute-start | bytes 393224 | tf_op jit(solution)/shard_map/ppermute | solution.py:251
  75.1 0.0 collective-permute-done.21
  75.1 0.0 collective-permute-done.20
  75.1 0.6 collective-permute-start.23
  75.7 3.6 %collective-permute-done.23 = f32[16,128]{1,0:T(8,128)S(1)} collective-permute-done((f32[16,128]{1,0:T(8,128)S(1)}, f32[16,128]{1,0:T(8,128)S(1)}, u32[]{:S(2)}, u32[]{:S(2)}) %collective-permute-start.23) | collective-permute-done | bytes 8224 | tf_op jit(solution)/shard_map/ppermute | solution.py:251
  79.4 0.0 collective-permute-done.24.refs_1_
  79.4 0.5 collective-permute-done.25.refs_2_
  79.9 0.0 collective-permute-done.26.refs_3_
  79.9 1.0 %collective-permute-start.27 = (f32[16,128]{1,0:T(8,128)S(1)}, f32[16,128]{1,0:T(8,128)S(1)}, u32[]{:S(2)}, u32[]{:S(2)}) collective-permute-start(f32[16,128]{1,0:T(8,128)S(1)} %add.54), channel_id=1, source_target_pairs={{0,2},{1,3},{2,0},{3,1},{4,6},{5,7},{6,4},{7,5},{8,10},{9,11},{10,... | collective-permute-start | bytes 24584 | tf_op jit(solution)/shard_map/ppermute | solution.py:251
  80.8 1.4 %shard_map.46 = f32[64,2048]{1,0:T(8,128)} custom-call(s32[6,8]{1,0:T(8,128)S(1)} %copy-done.1, f32[64,512]{1,0:T(8,128)S(1)} %get-tuple-element.39.refs_0_, f32[64,512]{1,0:T(8,128)S(1)} %collective-permute-done.24.refs_1_, f32[64,512]{1,0:T(8,128)S(1)} %collective-permute-done.25.refs_2_, f32[64,512]{1,0:T(8,128)S(1)} %collective-permute-done.26.refs_3_), custom_call_target="tpu_custom_call" | custom-call | bytes 1048576 | tf_op jit(solution)/shard_map/pallas_call | solution.py:274
  82.3 1.3 %collective-permute-done.27 = f32[16,128]{1,0:T(8,128)S(1)} collective-permute-done((f32[16,128]{1,0:T(8,128)S(1)}, f32[16,128]{1,0:T(8,128)S(1)}, u32[]{:S(2)}, u32[]{:S(2)}) %collective-permute-start.27) | collective-permute-done | bytes 8224 | tf_op jit(solution)/shard_map/ppermute | solution.py:251
  83.5 0.6 sqrt_bitcast_fusion
  (10 shorter events, 0.1 us)
Async XLA Ops:
  2.5 7.2 %collective-permute-start = (f32[64,512]{1,0:T(8,128)}, f32[64,512]{1,0:T(8,128)S(1)}, u32[]{:S(2)}, u32[]{:S(2)}) collective-permute-start(f32[64,512]{1,0:T(8,128)} %get-tuple-element.25), channel_id=1, source_target_pairs={{0,1},{1,0},{2,3},{3,2},{4,5},{5,4},{6,7},{7,6},{8,9},{9,8},{10,11... | collective-permute-start | bytes 393224 | tf_op jit(solution)/shard_map/ppermute | solution.py:251
  5.5 8.0 %collective-permute-start.1 = (f32[64,512]{1,0:T(8,128)}, f32[64,512]{1,0:T(8,128)S(1)}, u32[]{:S(2)}, u32[]{:S(2)}) collective-permute-start(f32[64,512]{1,0:T(8,128)} %get-tuple-element.26), channel_id=1, source_target_pairs={{0,2},{1,3},{2,0},{3,1},{4,6},{5,7},{6,4},{7,5},{8,10},{9,11},{10,... | collective-permute-start | bytes 393224 | tf_op jit(solution)/shard_map/ppermute | solution.py:251
  7.0 6.5 %collective-permute-start.2 = (f32[64,512]{1,0:T(8,128)}, f32[64,512]{1,0:T(8,128)S(1)}, u32[]{:S(2)}, u32[]{:S(2)}) collective-permute-start(f32[64,512]{1,0:T(8,128)} %get-tuple-element.27), channel_id=1, source_target_pairs={{0,3},{1,2},{2,1},{3,0},{4,7},{5,6},{6,5},{7,4},{8,11},{9,10},{10,... | collective-permute-start | bytes 393224 | tf_op jit(solution)/shard_map/ppermute | solution.py:251
  7.1 0.9 %copy-start = (f32[64,512]{1,0:T(8,128)S(1)}, f32[64,512]{1,0:T(8,128)}, u32[]{:S(2)}) copy-start(f32[64,512]{1,0:T(8,128)} %get-tuple-element.24.in_ref) | copy-start | bytes 393220
  13.9 1.4 %collective-permute-start.3 = (f32[136,256]{1,0:T(8,128)S(1)}, f32[136,256]{1,0:T(8,128)S(1)}, u32[]{:S(2)}, u32[]{:S(2)}) collective-permute-start(f32[136,256]{1,0:T(8,128)S(1)} %get-tuple-element.29), channel_id=1, source_target_pairs={{0,4},{4,0},{8,12},{12,8},{16,20},{20,16},{24,28},{28,24},{1,5},{5... | collective-permute-start | bytes 417800 | tf_op jit(solution)/shard_map/ppermute | solution.py:251
  15.4 8.5 %collective-permute-start.6 = (f32[136,256]{1,0:T(8,128)S(1)}, f32[136,256]{1,0:T(8,128)S(1)}, u32[]{:S(2)}, u32[]{:S(2)}) collective-permute-start(f32[136,256]{1,0:T(8,128)S(1)} %add.42), channel_id=1, source_target_pairs={{0,24},{4,28},{8,16},{12,20},{16,8},{20,12},{24,0},{28,4},{1,25},{... | collective-permute-start | bytes 417800 | tf_op jit(solution)/shard_map/ppermute | solution.py:251
  19.0 12.1 %collective-permute-start.5 = (f32[136,256]{1,0:T(8,128)S(1)}, f32[136,256]{1,0:T(8,128)S(1)}, u32[]{:S(2)}, u32[]{:S(2)}) collective-permute-start(f32[136,256]{1,0:T(8,128)S(1)} %add.42), channel_id=1, source_target_pairs={{0,16},{4,20},{8,24},{12,28},{16,0},{20,4},{24,8},{28,12},{1,17},{... | collective-permute-start | bytes 417800 | tf_op jit(solution)/shard_map/ppermute | solution.py:251
  19.0 12.1 %collective-permute-start.4 = (f32[136,256]{1,0:T(8,128)S(1)}, f32[136,256]{1,0:T(8,128)S(1)}, u32[]{:S(2)}, u32[]{:S(2)}) collective-permute-start(f32[136,256]{1,0:T(8,128)S(1)} %add.42), channel_id=1, source_target_pairs={{0,8},{4,12},{8,0},{12,4},{16,24},{20,28},{24,16},{28,20},{1,9},{5... | collective-permute-start | bytes 417800 | tf_op jit(solution)/shard_map/ppermute | solution.py:251
  19.8 18.0 %collective-permute-start.13 = (f32[256,512]{1,0:T(8,128)S(1)}, f32[256,512]{1,0:T(8,128)S(1)}, u32[]{:S(2)}, u32[]{:S(2)}) collective-permute-start(f32[256,512]{1,0:T(8,128)S(1)} %get-tuple-element.30.local_ref), channel_id=1, source_target_pairs={{0,2},{1,3},{2,0},{3,1},{4,6},{5,7},{6,4},{7,5},{8,10},{9,11},{10,... | collective-permute-start | bytes 1572872 | tf_op jit(solution)/shard_map/ppermute | solution.py:251
  21.3 16.5 %collective-permute-start.12 = (f32[256,512]{1,0:T(8,128)S(1)}, f32[256,512]{1,0:T(8,128)S(1)}, u32[]{:S(2)}, u32[]{:S(2)}) collective-permute-start(f32[256,512]{1,0:T(8,128)S(1)} %get-tuple-element.30.local_ref), channel_id=1, source_target_pairs={{0,1},{1,0},{2,3},{3,2},{4,5},{5,4},{6,7},{7,6},{8,9},{9,8},{10,11... | collective-permute-start | bytes 1572872 | tf_op jit(solution)/shard_map/ppermute | solution.py:251
  31.1 8.0 %copy-start.1 = (s32[6,8]{1,0:T(8,128)S(1)}, s32[6,8]{1,0:T(8,128)}, u32[]{:S(2)}) copy-start(s32[6,8]{1,0:T(8,128)} %get-tuple-element.23.table_ref) | copy-start | bytes 580
  31.2 5.1 %collective-permute-start.9 = (f32[136,256]{1,0:T(8,128)S(1)}, f32[136,256]{1,0:T(8,128)S(1)}, u32[]{:S(2)}, u32[]{:S(2)}) collective-permute-start(f32[136,256]{1,0:T(8,128)S(1)} %add_add_fusion.1.mine_ref), channel_id=1, source_target_pairs={{0,2},{1,3},{2,0},{3,1},{4,6},{5,7},{6,4},{7,5},{8,10},{9,11},{10,... | collective-permute-start | bytes 417800 | tf_op jit(solution)/shard_map/ppermute | solution.py:251
  32.7 5.1 %collective-permute-start.8 = (f32[136,256]{1,0:T(8,128)S(1)}, f32[136,256]{1,0:T(8,128)S(1)}, u32[]{:S(2)}, u32[]{:S(2)}) collective-permute-start(f32[136,256]{1,0:T(8,128)S(1)} %add_add_fusion.1.mine_ref), channel_id=1, source_target_pairs={{0,1},{1,0},{2,3},{3,2},{4,5},{5,4},{6,7},{7,6},{8,9},{9,8},{10,11... | collective-permute-start | bytes 417800 | tf_op jit(solution)/shard_map/ppermute | solution.py:251
  33.3 4.5 %collective-permute-start.7 = (f32[136,256]{1,0:T(8,128)S(1)}, f32[136,256]{1,0:T(8,128)S(1)}, u32[]{:S(2)}, u32[]{:S(2)}) collective-permute-start(f32[136,256]{1,0:T(8,128)S(1)} %add_add_fusion.1.mine_ref), channel_id=1, source_target_pairs={{0,4},{4,0},{8,12},{12,8},{16,20},{20,16},{24,28},{28,24},{1,5},{5... | collective-permute-start | bytes 417800 | tf_op jit(solution)/shard_map/ppermute | solution.py:251
  36.3 1.5 %collective-permute-start.11 = (f32[136,256]{1,0:T(8,128)S(1)}, f32[136,256]{1,0:T(8,128)S(1)}, u32[]{:S(2)}, u32[]{:S(2)}) collective-permute-start(f32[136,256]{1,0:T(8,128)S(1)} %collective-permute-done.9.refs_1_), channel_id=1, source_target_pairs={{0,4},{4,0},{8,12},{12,8},{16,20},{20,16},{24,28},{28,24},{1,5},{5... | collective-permute-start | bytes 417800 | tf_op jit(solution)/shard_map/ppermute | solution.py:251
  37.8 1.4 %collective-permute-start.10 = (f32[136,256]{1,0:T(8,128)S(1)}, f32[136,256]{1,0:T(8,128)S(1)}, u32[]{:S(2)}, u32[]{:S(2)}) collective-permute-start(f32[136,256]{1,0:T(8,128)S(1)} %collective-permute-done.8.refs_0_), channel_id=1, source_target_pairs={{0,4},{4,0},{8,12},{12,8},{16,20},{20,16},{24,28},{28,24},{1,5},{5... | collective-permute-start | bytes 417800 | tf_op jit(solution)/shard_map/ppermute | solution.py:251
  44.0 1.4 %collective-permute-start.14 = (f32[136,256]{1,0:T(8,128)S(1)}, f32[136,256]{1,0:T(8,128)S(1)}, u32[]{:S(2)}, u32[]{:S(2)}) collective-permute-start(f32[136,256]{1,0:T(8,128)S(1)} %get-tuple-element.32), channel_id=1, source_target_pairs={{0,4},{4,0},{8,12},{12,8},{16,20},{20,16},{24,28},{28,24},{1,5},{5... | collective-permute-start | bytes 417800 | tf_op jit(solution)/shard_map/ppermute | solution.py:251
  45.4 8.5 %collective-permute-start.17 = (f32[136,256]{1,0:T(8,128)S(1)}, f32[136,256]{1,0:T(8,128)S(1)}, u32[]{:S(2)}, u32[]{:S(2)}) collective-permute-start(f32[136,256]{1,0:T(8,128)S(1)} %add.46), channel_id=1, source_target_pairs={{0,24},{4,28},{8,16},{12,20},{16,8},{20,12},{24,0},{28,4},{1,25},{... | collective-permute-start | bytes 417800 | tf_op jit(solution)/shard_map/ppermute | solution.py:251
  48.4 12.0 %collective-permute-start.16 = (f32[136,256]{1,0:T(8,128)S(1)}, f32[136,256]{1,0:T(8,128)S(1)}, u32[]{:S(2)}, u32[]{:S(2)}) collective-permute-start(f32[136,256]{1,0:T(8,128)S(1)} %add.46), channel_id=1, source_target_pairs={{0,16},{4,20},{8,24},{12,28},{16,0},{20,4},{24,8},{28,12},{1,17},{... | collective-permute-start | bytes 417800 | tf_op jit(solution)/shard_map/ppermute | solution.py:251
  48.4 12.0 %collective-permute-start.15 = (f32[136,256]{1,0:T(8,128)S(1)}, f32[136,256]{1,0:T(8,128)S(1)}, u32[]{:S(2)}, u32[]{:S(2)}) collective-permute-start(f32[136,256]{1,0:T(8,128)S(1)} %add.46), channel_id=1, source_target_pairs={{0,8},{4,12},{8,0},{12,4},{16,24},{20,28},{24,16},{28,20},{1,9},{5... | collective-permute-start | bytes 417800 | tf_op jit(solution)/shard_map/ppermute | solution.py:251
  60.5 1.4 %collective-permute-start.18 = (f32[136,256]{1,0:T(8,128)S(1)}, f32[136,256]{1,0:T(8,128)S(1)}, u32[]{:S(2)}, u32[]{:S(2)}) collective-permute-start(f32[136,256]{1,0:T(8,128)S(1)} %add_add_fusion.mine_ref), channel_id=1, source_target_pairs={{0,4},{4,0},{8,12},{12,8},{16,20},{20,16},{24,28},{28,24},{1,5},{5... | collective-permute-start | bytes 417800 | tf_op jit(solution)/shard_map/ppermute | solution.py:251
  66.0 1.2 %collective-permute-start.19 = (f32[16,128]{1,0:T(8,128)S(1)}, f32[16,128]{1,0:T(8,128)S(1)}, u32[]{:S(2)}, u32[]{:S(2)}) collective-permute-start(f32[16,128]{1,0:T(8,128)S(1)} %get-tuple-element.34), channel_id=1, source_target_pairs={{0,4},{4,0},{8,12},{12,8},{16,20},{20,16},{24,28},{28,24},{1,5},{5... | collective-permute-start | bytes 24584 | tf_op jit(solution)/shard_map/ppermute | solution.py:251
  67.2 6.1 %collective-permute-start.22 = (f32[16,128]{1,0:T(8,128)S(1)}, f32[16,128]{1,0:T(8,128)S(1)}, u32[]{:S(2)}, u32[]{:S(2)}) collective-permute-start(f32[16,128]{1,0:T(8,128)S(1)} %add.50), channel_id=1, source_target_pairs={{0,24},{4,28},{8,16},{12,20},{16,8},{20,12},{24,0},{28,4},{1,25},{... | collective-permute-start | bytes 24584 | tf_op jit(solution)/shard_map/ppermute | solution.py:251
  69.6 5.5 %collective-permute-start.21 = (f32[16,128]{1,0:T(8,128)S(1)}, f32[16,128]{1,0:T(8,128)S(1)}, u32[]{:S(2)}, u32[]{:S(2)}) collective-permute-start(f32[16,128]{1,0:T(8,128)S(1)} %add.50), channel_id=1, source_target_pairs={{0,16},{4,20},{8,24},{12,28},{16,0},{20,4},{24,8},{28,12},{1,17},{... | collective-permute-start | bytes 24584 | tf_op jit(solution)/shard_map/ppermute | solution.py:251
  69.6 5.5 %collective-permute-start.20 = (f32[16,128]{1,0:T(8,128)S(1)}, f32[16,128]{1,0:T(8,128)S(1)}, u32[]{:S(2)}, u32[]{:S(2)}) collective-permute-start(f32[16,128]{1,0:T(8,128)S(1)} %add.50), channel_id=1, source_target_pairs={{0,8},{4,12},{8,0},{12,4},{16,24},{20,28},{24,16},{28,20},{1,9},{5... | collective-permute-start | bytes 24584 | tf_op jit(solution)/shard_map/ppermute | solution.py:251
  71.6 7.8 %collective-permute-start.24 = (f32[64,512]{1,0:T(8,128)S(1)}, f32[64,512]{1,0:T(8,128)S(1)}, u32[]{:S(2)}, u32[]{:S(2)}) collective-permute-start(f32[64,512]{1,0:T(8,128)S(1)} %get-tuple-element.36), channel_id=1, source_target_pairs={{0,1},{1,0},{2,3},{3,2},{4,5},{5,4},{6,7},{7,6},{8,9},{9,8},{10,11... | collective-permute-start | bytes 393224 | tf_op jit(solution)/shard_map/ppermute | solution.py:251
  72.2 7.7 %collective-permute-start.25 = (f32[64,512]{1,0:T(8,128)S(1)}, f32[64,512]{1,0:T(8,128)S(1)}, u32[]{:S(2)}, u32[]{:S(2)}) collective-permute-start(f32[64,512]{1,0:T(8,128)S(1)} %get-tuple-element.37), channel_id=1, source_target_pairs={{0,2},{1,3},{2,0},{3,1},{4,6},{5,7},{6,4},{7,5},{8,10},{9,11},{10,... | collective-permute-start | bytes 393224 | tf_op jit(solution)/shard_map/ppermute | solution.py:251
  73.4 6.5 %collective-permute-start.26 = (f32[64,512]{1,0:T(8,128)S(1)}, f32[64,512]{1,0:T(8,128)S(1)}, u32[]{:S(2)}, u32[]{:S(2)}) collective-permute-start(f32[64,512]{1,0:T(8,128)S(1)} %get-tuple-element.38), channel_id=1, source_target_pairs={{0,3},{1,2},{2,1},{3,0},{4,7},{5,6},{6,5},{7,4},{8,11},{9,10},{10,... | collective-permute-start | bytes 393224 | tf_op jit(solution)/shard_map/ppermute | solution.py:251
  75.1 4.3 %collective-permute-start.23 = (f32[16,128]{1,0:T(8,128)S(1)}, f32[16,128]{1,0:T(8,128)S(1)}, u32[]{:S(2)}, u32[]{:S(2)}) collective-permute-start(f32[16,128]{1,0:T(8,128)S(1)} %add_add_fusion.2), channel_id=1, source_target_pairs={{0,1},{1,0},{2,3},{3,2},{4,5},{5,4},{6,7},{7,6},{8,9},{9,8},{10,11... | collective-permute-start | bytes 24584 | tf_op jit(solution)/shard_map/ppermute | solution.py:251
  79.9 3.7 %collective-permute-start.27 = (f32[16,128]{1,0:T(8,128)S(1)}, f32[16,128]{1,0:T(8,128)S(1)}, u32[]{:S(2)}, u32[]{:S(2)}) collective-permute-start(f32[16,128]{1,0:T(8,128)S(1)} %add.54), channel_id=1, source_target_pairs={{0,2},{1,3},{2,0},{3,1},{4,6},{5,7},{6,4},{7,5},{8,10},{9,11},{10,... | collective-permute-start | bytes 24584 | tf_op jit(solution)/shard_map/ppermute | solution.py:251

commit v4 on v3

--- a/solution.py
+++ b/solution.py
@@ -75,6 +75,14 @@
         start = jnp.where(closed, (step + 1) ^ ((step + 1) >> 1), start)
 
 
+def deal_piece(table_ref, slab_ref, out, rnd, device):
+    width = out.shape[1] // 2
+    for half in range(2):
+        block = table_ref[rnd, 2 * note(table_ref, PAIR, device) + half]
+        start = pl.multiple_of(block * width, width)
+        out[: slab_ref.shape[0], half * width : (half + 1) * width] = slab_ref[:, pl.ds(start, width)]
+
+
 def deal_kernel(plan_hbm, slab_hbm, table_ref, *refs, rnd):
     *outs, plan_ref, slab_ref, plan_sem, slab_sem = refs
     slab_copy = pltpu.make_async_copy(slab_hbm, slab_ref, slab_sem)
@@ -85,31 +93,31 @@
     lay_out(plan_ref, table_ref, rnd)
     slab_copy.wait()
     me = lax.axis_index("pair")
-    width = outs[0].shape[1] // 2
     for mask, out in enumerate(outs):
-        pair = note(table_ref, PAIR, me ^ mask)
-        for half in range(2):
-            block = plan_ref[rnd, 2 * pair + half]
-            start = pl.multiple_of(block * width, width)
-            out[:, half * width : (half + 1) * width] = slab_ref[:, pl.ds(start, width)]
+        deal_piece(table_ref, slab_ref, out, rnd, me ^ mask)
+
+
+def parts_of(width):
+    lanes = width // LANES
+    return (lanes * width // 2 + -(-2 * lanes // PAD) * PAD, LANES)
 
 
 def cross_of(first, second, keep_ref, send_ref, scratch):
     width = first.shape[1]
     scratch[...] = mul_by_cols(split(first), split(second))
-    diag = jnp.concatenate(
-        [
-            jnp.sum(first * first, axis=0, keepdims=True),
-            jnp.sum(second * second, axis=0, keepdims=True),
-            jnp.zeros((PAD - 2, width), jnp.float32),
-        ],
-        axis=0,
-    )
+    sums = [jnp.sum(block * block, axis=0, keepdims=True) for block in (first, second)]
     core = lax.axis_index("row") & 1
-    part = width // 2
+    part, lanes = width // 2, width // LANES
     for ref, which in ((keep_ref, core), (send_ref, 1 - core)):
-        ref[:part, :] = scratch[pl.ds(pl.multiple_of(which * part, part), part), :]
-        ref[part:, :] = diag
+        rows = pl.ds(pl.multiple_of(which * part, part), part)
+        for lane in range(lanes):
+            columns = slice(lane * LANES, (lane + 1) * LANES)
+            ref[lane * part : (lane + 1) * part, :] = scratch[rows, columns]
+            for block in range(2):
+                row = lanes * part + block * lanes + lane
+                ref[row : row + 1, :] = sums[block][:, columns]
+        filled = lanes * (part + 2)
+        ref[filled:, :] = jnp.zeros((ref.shape[0] - filled, LANES), jnp.float32)
 
 
 def copy_kernel(in_ref, out_ref):
@@ -126,14 +134,19 @@
     cross_of(local_ref[:, :width], local_ref[:, width:], keep_ref, send_ref, scratch)
 
 
-def coupling_of(mine, other):
-    part = mine.shape[0] - PAD
+def coupling_of(mine, other, width):
+    part, lanes = width // 2, width // LANES
     upper = (lax.axis_index("row") & 1) == 0
+    halves = [
+        jnp.concatenate([half[lane * part : (lane + 1) * part] for lane in range(lanes)], axis=1)
+        for half in (mine, other)
+    ]
     cross = jnp.concatenate(
-        [jnp.where(upper, mine[:part], other[:part]), jnp.where(upper, other[:part], mine[:part])], axis=0
-    )
-    diag_first = jnp.transpose(mine[part:])[:, :1]
-    diag_second = mine[part + 1 : part + 2]
+        [jnp.where(upper, halves[0], halves[1]), jnp.where(upper, halves[1], halves[0])], axis=0
+    )
+    sums = mine[lanes * part :]
+    diag_first = jnp.concatenate([jnp.transpose(sums)[:, lane : lane + 1] for lane in range(lanes)], axis=0)
+    diag_second = jnp.concatenate([sums[lanes + lane : lanes + lane + 1] for lane in range(lanes)], axis=1)
     coupling = cross / (diag_first + diag_second + 1e-06)
     return coupling, jnp.transpose(coupling)
 
@@ -171,14 +184,36 @@
     return ref[:, pl.ds(pl.multiple_of(half * width, width), width)]
 
 
-def turn_kernel(table_ref, mine_ref, other_ref, local_ref, *refs, rnd, masks):
+def ahead_kernel(table_ref, slab_ref, local_ref, own_ref, *outs, rnd, masks, rest):
+    me = lax.axis_index("pair")
+    rows = own_ref.shape[0]
+    for mask, out in zip([0, *masks], [own_ref, *outs]):
+        device = me ^ mask
+        deal_piece(table_ref, slab_ref, out, rnd, sender(table_ref, device))
+        if mask:
+            for index, other in enumerate(rest):
+                start = pl.multiple_of((device ^ other) * rows, rows)
+                out[(index + 1) * rows : (index + 2) * rows, :] = local_ref[pl.ds(start, rows), :]
+
+
+def one_side(mine, other, ref, half):
+    k, kt = coupling_of(mine, other, ref.shape[1] // 2)
+    is_first = half == 0
+    return (
+        jnp.where(is_first, k, kt),
+        jnp.where(is_first, kt, k),
+        half_of(ref, half),
+        jnp.where(is_first, -1.0, 1.0),
+        half_of(ref, 1 - half),
+    )
+
+
+def turn_kernel(table_ref, mine_ref, other_ref, local_ref, own_ref, *refs, rnd, masks, rest):
+    *refs, next_ref, keep_ref, send_ref, scratch, raw_ref = refs
     came_refs, came_other_refs, raw_refs = (refs[i * len(masks) : (i + 1) * len(masks)] for i in range(3))
-    outs = refs[3 * len(masks) :]
-    next_ref, keep_ref, send_ref, scratch = outs
-    me = lax.axis_index("pair")
-    kept = note(table_ref, KEEPS, me)
-    gets = 1 - note(table_ref, KEEPS, sender(table_ref, me))
+    me = lax.axis_index("pair")
     source = sender(table_ref, me)
+    rows = own_ref.shape[0]
 
     def pick(parts):
         picked = parts[0]
@@ -186,31 +221,25 @@
             picked = jnp.where(source == (me ^ mask), part, picked)
         return picked
 
-    sides = []
-    for half, mine, other, halves in (
-        (kept, mine_ref[...], other_ref[...], [half_of(local_ref, kept), half_of(local_ref, 1 - kept)]),
-        (
-            gets,
-            pick([ref[...] for ref in came_refs]),
-            pick([ref[...] for ref in came_other_refs]),
-            [pick([half_of(ref, half) for ref in raw_refs]) for half in (gets, 1 - gets)],
-        ),
-    ):
-        k, kt = coupling_of(mine, other)
-        is_first = half == 0
-        sides.append(
-            (
-                jnp.where(is_first, k, kt),
-                jnp.where(is_first, kt, k),
-                halves[0],
-                jnp.where(is_first, -1.0, 1.0),
-                halves[1],
-            )
-        )
-    new = turned(sides)
-    kept_first = table_ref[rnd, 2 * note(table_ref, PAIR, me) + kept] == table_ref[rnd + 1, 2 * note(table_ref, NEXT, me)]
-    first = jnp.where(kept_first, new[0], new[1])
-    second = jnp.where(kept_first, new[1], new[0])
+    def put(other, piece):
+        raw_ref[pl.ds(pl.multiple_of((me ^ other) * rows, rows), rows), :] = piece
+
+    put(0, own_ref[...])
+    for mask, ref in zip(masks, raw_refs):
+        put(mask, ref[:rows, :])
+    for index, other in enumerate(rest):
+        put(other, pick([ref[(index + 1) * rows : (index + 2) * rows, :] for ref in raw_refs]))
+    half = 1 - note(table_ref, KEEPS, source)
+    came_pair = pick([ref[...] for ref in came_refs]), pick([ref[...] for ref in came_other_refs])
+    kept, came = turned(
+        [
+            one_side(mine_ref[...], other_ref[...], local_ref, note(table_ref, KEEPS, me)),
+            one_side(*came_pair, raw_ref, half),
+        ]
+    )
+    kept_block = table_ref[rnd, 2 * note(table_ref, PAIR, me) + note(table_ref, KEEPS, me)]
+    kept_first = kept_block == table_ref[rnd + 1, 2 * note(table_ref, NEXT, me)]
+    first, second = jnp.where(kept_first, kept, came), jnp.where(kept_first, came, kept)
     width = first.shape[1]
     next_ref[:, :width] = first
     next_ref[:, width:] = second
@@ -221,7 +250,7 @@
     *outs, squares_ref, scratch = refs
     width = local_ref.shape[1] // 2
     first, second = local_ref[:, :width], local_ref[:, width:]
-    k, kt = coupling_of(mine_ref[...], other_ref[...])
+    k, kt = coupling_of(mine_ref[...], other_ref[...], width)
     new = turned([(k, kt, first, -1.0, second), (kt, k, second, 1.0, first)])
     me = lax.axis_index("pair")
     squares_ref[...] = jnp.zeros_like(squares_ref)
@@ -309,23 +338,31 @@
     width = both // 2
     group_rows = piece_rows * pair_count
     total_rows = group_rows * lax.axis_size("row")
-    crossed = [(group_rows, both), (width // 2 + PAD, width), (width // 2 + PAD, width)]
+    crossed = [(group_rows, both), parts_of(width), parts_of(width)]
     square = (width, width)
     masks = powers(pair_count) if pair_count <= 4 else list(range(1, pair_count))
+    rest = [mask for mask in range(1, pair_count) if mask not in masks]
 
     table, dealt = deal(plan, slab, 0)
     own, *others = spread(dealt)
     own = call(copy_kernel, [own], [own.shape])
     local, keep, send = call(first_cross_kernel, [*own, *others], crossed, [square])
-    raw = [swap(local, "pair", mask) for mask in masks]
-    mine = over_chips(keep + swap(send, "row", 1))
+    own, *ahead = call(
+        functools.partial(ahead_kernel, rnd=0, masks=masks, rest=rest),
+        [slab, local],
+        [(piece_rows, both)] + [((1 + len(rest)) * piece_rows, both)] * len(masks),
+        table=table,
+    )
+    total, ahead = lax.optimization_barrier((keep + swap(send, "row", 1), ahead))
+    raw = [swap(x, "pair", mask) for x, mask in zip(ahead, masks)]
+    mine, raw = lax.optimization_barrier((over_chips(total), raw))
     came = [swap(mine, "pair", mask) for mask in masks]
     came_other = [swap(x, "row", 1) for x in came]
     local, keep, send = call(
-        functools.partial(turn_kernel, rnd=0, masks=masks),
-        [mine, swap(mine, "row", 1), local] + came + came_other + raw,
+        functools.partial(turn_kernel, rnd=0, masks=masks, rest=rest),
+        [mine, swap(mine, "row", 1), local, own] + came + came_other + raw,
         crossed,
-        [square],
+        [square, (group_rows, both)],
         table,
     )
     mine = over_chips(keep + swap(send, "row", 1))

time: 84.3 us -> 82.4 us (0.977)
  waiting for transfers between devices: 41.6 us -> 38.5 us
    ppermute x28, waiting for transfers between devices: 41.6 us -> 38.5 us  [swap(): lax.ppermute(x, axis, [(i, i ^ mask) for i in range(lax.axis_size(axis))])]
    pallas_call x5 -> x6, Pallas kernels: 10.7 us -> 11.3 us  [call(): pl.pallas_call(kernel, out_shape=[jax.ShapeDtypeStruct(shape, jnp.float32...]
  transfers between devices with their start and end apart: 28 -> 28, of which waited for: 16 -> 16; matrix products, arithmetic and copies ran while one was open for 0% -> 0% of each run, Pallas kernels for 2% -> 3%
where the time goes in v4:
time: 82.4 us; the launch traced here: 82.2 us
  waiting for transfers between devices  38.5 us (47%)
  starting transfers between devices  27.6 us (33%)
  Pallas kernels  13.2 us (16%)
  local copies, waits for them, and re-layouts  1.5 us (2%)
    ppermute x28, waiting for transfers between devices, swap(): lax.ppermute(x, axis, [(i, i ^ mask) for i in range(lax.axis_size(axis))])  38.5 us
    ppermute x28, starting transfers between devices, swap(): lax.ppermute(x, axis, [(i, i ^ mask) for i in range(lax.axis_size(axis))])  27.6 us
    pallas_call x6, Pallas kernels, call(): pl.pallas_call(kernel, out_shape=[jax.ShapeDtypeStruct(shape, jnp.float32...  11.3 us
    pallas_call x1, Pallas kernels, deal(): pl.pallas_call(functools.partial(deal_kernel, rnd=rnd), out_shape=[jax.Sh...  1.88 us
  transfers between devices with their start and end apart: 28, of which 16 were waited for; matrix products, arithmetic and copies ran while one was open for 0% of the time, Pallas kernels for 3%

profile of v4, /device:TPU:0, one launch (start us, length us, event | category | flops | bytes accessed | tf_op | source)
XLA Modules:
  0.0 82.2 jit_solution(17460072089177045990)
XLA Ops:
  0.6 1.9 %shard_map.41 = (s32[6,8]{1,0:T(8,128)}, f32[64,512]{1,0:T(8,128)}, f32[64,512]{1,0:T(8,128)}, f32[64,512]{1,0:T(8,128)}, f32[64,512]{1,0:T(8,128)}) custom-call(s32[2,8]{1,0:T(2,128)} %plan_hbm.1, f32[64,2048]{1,0:T(8,128)} %slab_ref.1), custom_call_target="tpu_custom_call" | custom-call | tf_op jit(solution)/shard_map/pallas_call | solution.py:318
  2.5 0.0 copy-start
  2.5 3.0 %collective-permute-start = (f32[64,512]{1,0:T(8,128)}, f32[64,512]{1,0:T(8,128)S(1)}, u32[]{:S(2)}, u32[]{:S(2)}) collective-permute-start(f32[64,512]{1,0:T(8,128)} %get-tuple-element.34), channel_id=1, source_target_pairs={{0,1},{1,0},{2,3},{3,2},{4,5},{5,4},{6,7},{7,6},{8,9},{9,8},{10,11... | collective-permute-start | bytes 393224 | tf_op jit(solution)/shard_map/ppermute | solution.py:280
  5.5 1.5 %collective-permute-start.1 = (f32[64,512]{1,0:T(8,128)}, f32[64,512]{1,0:T(8,128)S(1)}, u32[]{:S(2)}, u32[]{:S(2)}) collective-permute-start(f32[64,512]{1,0:T(8,128)} %get-tuple-element.35), channel_id=1, source_target_pairs={{0,2},{1,3},{2,0},{3,1},{4,6},{5,7},{6,4},{7,5},{8,10},{9,11},{10,... | collective-permute-start | bytes 393224 | tf_op jit(solution)/shard_map/ppermute | solution.py:280
  7.1 0.0 collective-permute-start.2
  7.1 0.9 %copy-done.1 = f32[64,512]{1,0:T(8,128)S(1)} copy-done((f32[64,512]{1,0:T(8,128)S(1)}, f32[64,512]{1,0:T(8,128)}, u32[]{:S(2)}) %copy-start.1) | copy-done | bytes 131096
  8.0 1.8 %collective-permute-done.refs_1_ = f32[64,512]{1,0:T(8,128)S(1)} collective-permute-done((f32[64,512]{1,0:T(8,128)}, f32[64,512]{1,0:T(8,128)S(1)}, u32[]{:S(2)}, u32[]{:S(2)}) %collective-permute-start) | collective-permute-done | bytes 131104 | tf_op jit(solution)/shard_map/ppermute | solution.py:280
  9.7 3.8 %collective-permute-done.1.refs_2_ = f32[64,512]{1,0:T(8,128)S(1)} collective-permute-done((f32[64,512]{1,0:T(8,128)}, f32[64,512]{1,0:T(8,128)S(1)}, u32[]{:S(2)}, u32[]{:S(2)}) %collective-permute-start.1) | collective-permute-done | bytes 131104 | tf_op jit(solution)/shard_map/ppermute | solution.py:280
  13.5 0.0 collective-permute-done.2.refs_3_
  13.5 0.4 shard_map.43
  13.9 0.0 copy-start.2
  13.9 0.1 collective-permute-start.3
  14.0 0.6 copy-done.2
  14.6 0.7 shard_map.44
  15.3 0.1 collective-permute-done.3
  15.4 3.7 %collective-permute-start.6 = (f32[264,128]{1,0:T(8,128)S(1)}, f32[264,128]{1,0:T(8,128)S(1)}, u32[]{:S(2)}, u32[]{:S(2)}) collective-permute-start(f32[264,128]{1,0:T(8,128)S(1)} %add.42), channel_id=1, source_target_pairs={{0,24},{4,28},{8,16},{12,20},{16,8},{20,12},{24,0},{28,4},{1,25},{... | collective-permute-start | bytes 405512 | tf_op jit(solution)/shard_map/ppermute | solution.py:280
  19.1 0.0 collective-permute-start.5
  19.1 0.8 collective-permute-start.4
  19.8 1.2 %collective-permute-start.7 = (f32[128,512]{1,0:T(8,128)S(1)}, f32[128,512]{1,0:T(8,128)S(1)}, u32[]{:S(2)}, u32[]{:S(2)}) collective-permute-start(f32[128,512]{1,0:T(8,128)S(1)} %get-tuple-element.43), channel_id=1, source_target_pairs={{0,1},{1,0},{2,3},{3,2},{4,5},{5,4},{6,7},{7,6},{8,9},{9,8},{10,11... | collective-permute-start | bytes 786440 | tf_op jit(solution)/shard_map/ppermute | solution.py:280
  21.1 0.8 collective-permute-start.8
  21.9 1.9 %collective-permute-done.6 = f32[264,128]{1,0:T(8,128)S(1)} collective-permute-done((f32[264,128]{1,0:T(8,128)S(1)}, f32[264,128]{1,0:T(8,128)S(1)}, u32[]{:S(2)}, u32[]{:S(2)}) %collective-permute-start.6) | collective-permute-done | bytes 135200 | tf_op jit(solution)/shard_map/ppermute | solution.py:280
  23.8 7.0 %collective-permute-done.5 = f32[264,128]{1,0:T(8,128)S(1)} collective-permute-done((f32[264,128]{1,0:T(8,128)S(1)}, f32[264,128]{1,0:T(8,128)S(1)}, u32[]{:S(2)}, u32[]{:S(2)}) %collective-permute-start.5) | collective-permute-done | bytes 135200 | tf_op jit(solution)/shard_map/ppermute | solution.py:280
  30.8 0.0 collective-permute-done.4
  30.8 0.0 collective-permute-done.7.refs_4_
  30.8 0.0 collective-permute-done.8.refs_5_
  30.8 1.6 %collective-permute-start.11 = (f32[264,128]{1,0:T(8,128)S(1)}, f32[264,128]{1,0:T(8,128)S(1)}, u32[]{:S(2)}, u32[]{:S(2)}) collective-permute-start(f32[264,128]{1,0:T(8,128)S(1)} %add_add_fusion.1.mine_ref), channel_id=1, source_target_pairs={{0,2},{1,3},{2,0},{3,1},{4,6},{5,7},{6,4},{7,5},{8,10},{9,11},{10,... | collective-permute-start | bytes 405512 | tf_op jit(solution)/shard_map/ppermute | solution.py:280
  32.4 0.5 collective-permute-start.10
  33.0 0.0 collective-permute-start.9
  33.0 3.0 %collective-permute-done.11.refs_1_ = f32[264,128]{1,0:T(8,128)S(1)} collective-permute-done((f32[264,128]{1,0:T(8,128)S(1)}, f32[264,128]{1,0:T(8,128)S(1)}, u32[]{:S(2)}, u32[]{:S(2)}) %collective-permute-start.11) | collective-permute-done | bytes 135200 | tf_op jit(solution)/shard_map/ppermute | solution.py:280
  35.9 0.0 collective-permute-start.13
  35.9 1.5 %collective-permute-done.10.refs_0_ = f32[264,128]{1,0:T(8,128)S(1)} collective-permute-done((f32[264,128]{1,0:T(8,128)S(1)}, f32[264,128]{1,0:T(8,128)S(1)}, u32[]{:S(2)}, u32[]{:S(2)}) %collective-permute-start.10) | collective-permute-done | bytes 135200 | tf_op jit(solution)/shard_map/ppermute | solution.py:280
  37.4 0.0 collective-permute-start.12
  37.4 0.0 collective-permute-done.9.other_ref
  37.4 0.0 collective-permute-done.13.refs_3_
  37.5 1.3 %collective-permute-done.12.refs_2_ = f32[264,128]{1,0:T(8,128)S(1)} collective-permute-done((f32[264,128]{1,0:T(8,128)S(1)}, f32[264,128]{1,0:T(8,128)S(1)}, u32[]{:S(2)}, u32[]{:S(2)}) %collective-permute-start.12) | collective-permute-done | bytes 135200 | tf_op jit(solution)/shard_map/ppermute | solution.py:280
  38.8 4.7 %shard_map.45 = (f32[256,512]{1,0:T(8,128)S(1)}, f32[264,128]{1,0:T(8,128)S(1)}, f32[264,128]{1,0:T(8,128)S(1)}) custom-call(s32[6,8]{1,0:T(8,128)S(1)} %copy-done.2, f32[264,128]{1,0:T(8,128)S(1)} %add_add_fusion.1.mine_ref, f32[264,128]{1,0:T(8,128)S(1)} %collective-permute-done.9.other_ref, f32[256,512]{1,0:T(8,128)S(1)} %get-tuple-element.39.local_ref, ...), custom_call_target="tpu_custom_call" | custom-call | tf_op jit(solution)/shard_map/pallas_call | solution.py:303
  43.5 0.2 collective-permute-start.14
  43.7 1.2 %collective-permute-done.14 = f32[264,128]{1,0:T(8,128)S(1)} collective-permute-done((f32[264,128]{1,0:T(8,128)S(1)}, f32[264,128]{1,0:T(8,128)S(1)}, u32[]{:S(2)}, u32[]{:S(2)}) %collective-permute-start.14) | collective-permute-done | bytes 135200 | tf_op jit(solution)/shard_map/ppermute | solution.py:280
  45.0 2.5 %collective-permute-start.17 = (f32[264,128]{1,0:T(8,128)S(1)}, f32[264,128]{1,0:T(8,128)S(1)}, u32[]{:S(2)}, u32[]{:S(2)}) collective-permute-start(f32[264,128]{1,0:T(8,128)S(1)} %add.46), channel_id=1, source_target_pairs={{0,24},{4,28},{8,16},{12,20},{16,8},{20,12},{24,0},{28,4},{1,25},{... | collective-permute-start | bytes 405512 | tf_op jit(solution)/shard_map/ppermute | solution.py:280
  47.5 0.0 collective-permute-start.16
  47.5 1.9 %collective-permute-start.15 = (f32[264,128]{1,0:T(8,128)S(1)}, f32[264,128]{1,0:T(8,128)S(1)}, u32[]{:S(2)}, u32[]{:S(2)}) collective-permute-start(f32[264,128]{1,0:T(8,128)S(1)} %add.46), channel_id=1, source_target_pairs={{0,8},{4,12},{8,0},{12,4},{16,24},{20,28},{24,16},{28,20},{1,9},{5... | collective-permute-start | bytes 405512 | tf_op jit(solution)/shard_map/ppermute | solution.py:280
  49.4 4.0 %collective-permute-done.17 = f32[264,128]{1,0:T(8,128)S(1)} collective-permute-done((f32[264,128]{1,0:T(8,128)S(1)}, f32[264,128]{1,0:T(8,128)S(1)}, u32[]{:S(2)}, u32[]{:S(2)}) %collective-permute-start.17) | collective-permute-done | bytes 135200 | tf_op jit(solution)/shard_map/ppermute | solution.py:280
  53.4 5.2 %collective-permute-done.16 = f32[264,128]{1,0:T(8,128)S(1)} collective-permute-done((f32[264,128]{1,0:T(8,128)S(1)}, f32[264,128]{1,0:T(8,128)S(1)}, u32[]{:S(2)}, u32[]{:S(2)}) %collective-permute-start.16) | collective-permute-done | bytes 135200 | tf_op jit(solution)/shard_map/ppermute | solution.py:280
  58.6 0.0 collective-permute-done.15
  58.6 0.1 collective-permute-start.18
  58.7 1.3 %collective-permute-done.18.other_ref = f32[264,128]{1,0:T(8,128)S(1)} collective-permute-done((f32[264,128]{1,0:T(8,128)S(1)}, f32[264,128]{1,0:T(8,128)S(1)}, u32[]{:S(2)}, u32[]{:S(2)}) %collective-permute-start.18) | collective-permute-done | bytes 135200 | tf_op jit(solution)/shard_map/ppermute | solution.py:280
  60.0 4.0 %shard_map.46 = (f32[64,512]{1,0:T(8,128)S(1)}, f32[64,512]{1,0:T(8,128)S(1)}, f32[64,512]{1,0:T(8,128)S(1)}, f32[64,512]{1,0:T(8,128)S(1)}, f32[16,128]{1,0:T(8,128)S(1)}) custom-call(s32[6,8]{1,0:T(8,128)S(1)} %copy-done.2, f32[264,128]{1,0:T(8,128)S(1)} %add_add_fusion.mine_ref, f32[264,128]{1,0:T(8,128)S(1)} %collective-permute-done.18.other_ref, ...), custom_call_target="tpu_custom_call" | custom-call | tf_op jit(solution)/shard_map/pallas_call | solution.py:303
  64.1 0.2 collective-permute-start.19
  64.3 1.0 %collective-permute-done.19 = f32[16,128]{1,0:T(8,128)S(1)} collective-permute-done((f32[16,128]{1,0:T(8,128)S(1)}, f32[16,128]{1,0:T(8,128)S(1)}, u32[]{:S(2)}, u32[]{:S(2)}) %collective-permute-start.19) | collective-permute-done | bytes 8224 | tf_op jit(solution)/shard_map/ppermute | solution.py:280
  65.3 2.2 %collective-permute-start.22 = (f32[16,128]{1,0:T(8,128)S(1)}, f32[16,128]{1,0:T(8,128)S(1)}, u32[]{:S(2)}, u32[]{:S(2)}) collective-permute-start(f32[16,128]{1,0:T(8,128)S(1)} %add.50), channel_id=1, source_target_pairs={{0,24},{4,28},{8,16},{12,20},{16,8},{20,12},{24,0},{28,4},{1,25},{... | collective-permute-start | bytes 24584 | tf_op jit(solution)/shard_map/ppermute | solution.py:280
  67.5 2.2 %collective-permute-start.20 = (f32[16,128]{1,0:T(8,128)S(1)}, f32[16,128]{1,0:T(8,128)S(1)}, u32[]{:S(2)}, u32[]{:S(2)}) collective-permute-start(f32[16,128]{1,0:T(8,128)S(1)} %add.50), channel_id=1, source_target_pairs={{0,8},{4,12},{8,0},{12,4},{16,24},{20,28},{24,16},{28,20},{1,9},{5... | collective-permute-start | bytes 24584 | tf_op jit(solution)/shard_map/ppermute | solution.py:280
  69.7 0.5 collective-permute-start.24
  70.2 1.2 %collective-permute-start.25 = (f32[64,512]{1,0:T(8,128)S(1)}, f32[64,512]{1,0:T(8,128)S(1)}, u32[]{:S(2)}, u32[]{:S(2)}) collective-permute-start(f32[64,512]{1,0:T(8,128)S(1)} %get-tuple-element.55), channel_id=1, source_target_pairs={{0,2},{1,3},{2,0},{3,1},{4,6},{5,7},{6,4},{7,5},{8,10},{9,11},{10,... | collective-permute-start | bytes 393224 | tf_op jit(solution)/shard_map/ppermute | solution.py:280
  71.4 1.8 %collective-permute-start.26 = (f32[64,512]{1,0:T(8,128)S(1)}, f32[64,512]{1,0:T(8,128)S(1)}, u32[]{:S(2)}, u32[]{:S(2)}) collective-permute-start(f32[64,512]{1,0:T(8,128)S(1)} %get-tuple-element.56), channel_id=1, source_target_pairs={{0,3},{1,2},{2,1},{3,0},{4,7},{5,6},{6,5},{7,4},{8,11},{9,10},{10,... | collective-permute-start | bytes 393224 | tf_op jit(solution)/shard_map/ppermute | solution.py:280
  73.2 0.0 collective-permute-done.21
  73.2 0.0 collective-permute-done.20
  73.2 0.6 collective-permute-start.23
  73.8 3.6 %collective-permute-done.23 = f32[16,128]{1,0:T(8,128)S(1)} collective-permute-done((f32[16,128]{1,0:T(8,128)S(1)}, f32[16,128]{1,0:T(8,128)S(1)}, u32[]{:S(2)}, u32[]{:S(2)}) %collective-permute-start.23) | collective-permute-done | bytes 8224 | tf_op jit(solution)/shard_map/ppermute | solution.py:280
  77.4 0.5 collective-permute-done.25.refs_2_
  77.9 0.0 collective-permute-done.26.refs_3_
  77.9 0.9 %collective-permute-start.27 = (f32[16,128]{1,0:T(8,128)S(1)}, f32[16,128]{1,0:T(8,128)S(1)}, u32[]{:S(2)}, u32[]{:S(2)}) collective-permute-start(f32[16,128]{1,0:T(8,128)S(1)} %add.54), channel_id=1, source_target_pairs={{0,2},{1,3},{2,0},{3,1},{4,6},{5,7},{6,4},{7,5},{8,10},{9,11},{10,... | collective-permute-start | bytes 24584 | tf_op jit(solution)/shard_map/ppermute | solution.py:280
  78.9 1.4 %shard_map.47 = f32[64,2048]{1,0:T(8,128)} custom-call(s32[6,8]{1,0:T(8,128)S(1)} %copy-done.2, f32[64,512]{1,0:T(8,128)S(1)} %get-tuple-element.57.refs_0_, f32[64,512]{1,0:T(8,128)S(1)} %collective-permute-done.24.refs_1_, f32[64,512]{1,0:T(8,128)S(1)} %collective-permute-done.25.refs_2_, f32[64,512]{1,0:T(8,128)S(1)} %collective-permute-done.26.refs_3_), custom_call_target="tpu_custom_call" | custom-call | bytes 1048576 | tf_op jit(solution)/shard_map/pallas_call | solution.py:303
  80.3 1.3 %collective-permute-done.27 = f32[16,128]{1,0:T(8,128)S(1)} collective-permute-done((f32[16,128]{1,0:T(8,128)S(1)}, f32[16,128]{1,0:T(8,128)S(1)}, u32[]{:S(2)}, u32[]{:S(2)}) %collective-permute-start.27) | collective-permute-done | bytes 8224 | tf_op jit(solution)/shard_map/ppermute | solution.py:280
  81.6 0.6 sqrt_bitcast_fusion
  (13 shorter events, 0.1 us)
Async XLA Ops:
  2.5 11.5 %copy-start = (f32[64,2048]{1,0:T(8,128)S(1)}, f32[64,2048]{1,0:T(8,128)}, u32[]{:S(2)}) copy-start(f32[64,2048]{1,0:T(8,128)} %slab_ref.1) | copy-start | bytes 1572868
  2.5 7.2 %collective-permute-start = (f32[64,512]{1,0:T(8,128)}, f32[64,512]{1,0:T(8,128)S(1)}, u32[]{:S(2)}, u32[]{:S(2)}) collective-permute-start(f32[64,512]{1,0:T(8,128)} %get-tuple-element.34), channel_id=1, source_target_pairs={{0,1},{1,0},{2,3},{3,2},{4,5},{5,4},{6,7},{7,6},{8,9},{9,8},{10,11... | collective-permute-start | bytes 393224 | tf_op jit(solution)/shard_map/ppermute | solution.py:280
  5.5 8.0 %collective-permute-start.1 = (f32[64,512]{1,0:T(8,128)}, f32[64,512]{1,0:T(8,128)S(1)}, u32[]{:S(2)}, u32[]{:S(2)}) collective-permute-start(f32[64,512]{1,0:T(8,128)} %get-tuple-element.35), channel_id=1, source_target_pairs={{0,2},{1,3},{2,0},{3,1},{4,6},{5,7},{6,4},{7,5},{8,10},{9,11},{10,... | collective-permute-start | bytes 393224 | tf_op jit(solution)/shard_map/ppermute | solution.py:280
  7.1 6.5 %collective-permute-start.2 = (f32[64,512]{1,0:T(8,128)}, f32[64,512]{1,0:T(8,128)S(1)}, u32[]{:S(2)}, u32[]{:S(2)}) collective-permute-start(f32[64,512]{1,0:T(8,128)} %get-tuple-element.36), channel_id=1, source_target_pairs={{0,3},{1,2},{2,1},{3,0},{4,7},{5,6},{6,5},{7,4},{8,11},{9,10},{10,... | collective-permute-start | bytes 393224 | tf_op jit(solution)/shard_map/ppermute | solution.py:280
  7.1 0.9 %copy-start.1 = (f32[64,512]{1,0:T(8,128)S(1)}, f32[64,512]{1,0:T(8,128)}, u32[]{:S(2)}) copy-start(f32[64,512]{1,0:T(8,128)} %get-tuple-element.33.in_ref) | copy-start | bytes 393220
  13.9 0.7 copy-start.2
  13.9 1.4 %collective-permute-start.3 = (f32[264,128]{1,0:T(8,128)S(1)}, f32[264,128]{1,0:T(8,128)S(1)}, u32[]{:S(2)}, u32[]{:S(2)}) collective-permute-start(f32[264,128]{1,0:T(8,128)S(1)} %get-tuple-element.38), channel_id=1, source_target_pairs={{0,4},{4,0},{8,12},{12,8},{16,20},{20,16},{24,28},{28,24},{1,5},{5... | collective-permute-start | bytes 405512 | tf_op jit(solution)/shard_map/ppermute | solution.py:280
  15.4 8.4 %collective-permute-start.6 = (f32[264,128]{1,0:T(8,128)S(1)}, f32[264,128]{1,0:T(8,128)S(1)}, u32[]{:S(2)}, u32[]{:S(2)}) collective-permute-start(f32[264,128]{1,0:T(8,128)S(1)} %add.42), channel_id=1, source_target_pairs={{0,24},{4,28},{8,16},{12,20},{16,8},{20,12},{24,0},{28,4},{1,25},{... | collective-permute-start | bytes 405512 | tf_op jit(solution)/shard_map/ppermute | solution.py:280
  19.1 11.7 %collective-permute-start.5 = (f32[264,128]{1,0:T(8,128)S(1)}, f32[264,128]{1,0:T(8,128)S(1)}, u32[]{:S(2)}, u32[]{:S(2)}) collective-permute-start(f32[264,128]{1,0:T(8,128)S(1)} %add.42), channel_id=1, source_target_pairs={{0,16},{4,20},{8,24},{12,28},{16,0},{20,4},{24,8},{28,12},{1,17},{... | collective-permute-start | bytes 405512 | tf_op jit(solution)/shard_map/ppermute | solution.py:280
  19.1 11.7 %collective-permute-start.4 = (f32[264,128]{1,0:T(8,128)S(1)}, f32[264,128]{1,0:T(8,128)S(1)}, u32[]{:S(2)}, u32[]{:S(2)}) collective-permute-start(f32[264,128]{1,0:T(8,128)S(1)} %add.42), channel_id=1, source_target_pairs={{0,8},{4,12},{8,0},{12,4},{16,24},{20,28},{24,16},{28,20},{1,9},{5... | collective-permute-start | bytes 405512 | tf_op jit(solution)/shard_map/ppermute | solution.py:280
  19.8 11.0 %collective-permute-start.7 = (f32[128,512]{1,0:T(8,128)S(1)}, f32[128,512]{1,0:T(8,128)S(1)}, u32[]{:S(2)}, u32[]{:S(2)}) collective-permute-start(f32[128,512]{1,0:T(8,128)S(1)} %get-tuple-element.43), channel_id=1, source_target_pairs={{0,1},{1,0},{2,3},{3,2},{4,5},{5,4},{6,7},{7,6},{8,9},{9,8},{10,11... | collective-permute-start | bytes 786440 | tf_op jit(solution)/shard_map/ppermute | solution.py:280
  21.1 9.8 %collective-permute-start.8 = (f32[128,512]{1,0:T(8,128)S(1)}, f32[128,512]{1,0:T(8,128)S(1)}, u32[]{:S(2)}, u32[]{:S(2)}) collective-permute-start(f32[128,512]{1,0:T(8,128)S(1)} %get-tuple-element.44), channel_id=1, source_target_pairs={{0,2},{1,3},{2,0},{3,1},{4,6},{5,7},{6,4},{7,5},{8,10},{9,11},{10,... | collective-permute-start | bytes 786440 | tf_op jit(solution)/shard_map/ppermute | solution.py:280
  30.8 5.1 %collective-permute-start.11 = (f32[264,128]{1,0:T(8,128)S(1)}, f32[264,128]{1,0:T(8,128)S(1)}, u32[]{:S(2)}, u32[]{:S(2)}) collective-permute-start(f32[264,128]{1,0:T(8,128)S(1)} %add_add_fusion.1.mine_ref), channel_id=1, source_target_pairs={{0,2},{1,3},{2,0},{3,1},{4,6},{5,7},{6,4},{7,5},{8,10},{9,11},{10,... | collective-permute-start | bytes 405512 | tf_op jit(solution)/shard_map/ppermute | solution.py:280
  32.4 5.0 %collective-permute-start.10 = (f32[264,128]{1,0:T(8,128)S(1)}, f32[264,128]{1,0:T(8,128)S(1)}, u32[]{:S(2)}, u32[]{:S(2)}) collective-permute-start(f32[264,128]{1,0:T(8,128)S(1)} %add_add_fusion.1.mine_ref), channel_id=1, source_target_pairs={{0,1},{1,0},{2,3},{3,2},{4,5},{5,4},{6,7},{7,6},{8,9},{9,8},{10,11... | collective-permute-start | bytes 405512 | tf_op jit(solution)/shard_map/ppermute | solution.py:280
  33.0 4.5 %collective-permute-start.9 = (f32[264,128]{1,0:T(8,128)S(1)}, f32[264,128]{1,0:T(8,128)S(1)}, u32[]{:S(2)}, u32[]{:S(2)}) collective-permute-start(f32[264,128]{1,0:T(8,128)S(1)} %add_add_fusion.1.mine_ref), channel_id=1, source_target_pairs={{0,4},{4,0},{8,12},{12,8},{16,20},{20,16},{24,28},{28,24},{1,5},{5... | collective-permute-start | bytes 405512 | tf_op jit(solution)/shard_map/ppermute | solution.py:280
  35.9 1.5 %collective-permute-start.13 = (f32[264,128]{1,0:T(8,128)S(1)}, f32[264,128]{1,0:T(8,128)S(1)}, u32[]{:S(2)}, u32[]{:S(2)}) collective-permute-start(f32[264,128]{1,0:T(8,128)S(1)} %collective-permute-done.11.refs_1_), channel_id=1, source_target_pairs={{0,4},{4,0},{8,12},{12,8},{16,20},{20,16},{24,28},{28,24},{1,5},{5... | collective-permute-start | bytes 405512 | tf_op jit(solution)/shard_map/ppermute | solution.py:280
  37.4 1.4 %collective-permute-start.12 = (f32[264,128]{1,0:T(8,128)S(1)}, f32[264,128]{1,0:T(8,128)S(1)}, u32[]{:S(2)}, u32[]{:S(2)}) collective-permute-start(f32[264,128]{1,0:T(8,128)S(1)} %collective-permute-done.10.refs_0_), channel_id=1, source_target_pairs={{0,4},{4,0},{8,12},{12,8},{16,20},{20,16},{24,28},{28,24},{1,5},{5... | collective-permute-start | bytes 405512 | tf_op jit(solution)/shard_map/ppermute | solution.py:280
  43.5 1.4 %collective-permute-start.14 = (f32[264,128]{1,0:T(8,128)S(1)}, f32[264,128]{1,0:T(8,128)S(1)}, u32[]{:S(2)}, u32[]{:S(2)}) collective-permute-start(f32[264,128]{1,0:T(8,128)S(1)} %get-tuple-element.50), channel_id=1, source_target_pairs={{0,4},{4,0},{8,12},{12,8},{16,20},{20,16},{24,28},{28,24},{1,5},{5... | collective-permute-start | bytes 405512 | tf_op jit(solution)/shard_map/ppermute | solution.py:280
  45.0 8.4 %collective-permute-start.17 = (f32[264,128]{1,0:T(8,128)S(1)}, f32[264,128]{1,0:T(8,128)S(1)}, u32[]{:S(2)}, u32[]{:S(2)}) collective-permute-start(f32[264,128]{1,0:T(8,128)S(1)} %add.46), channel_id=1, source_target_pairs={{0,24},{4,28},{8,16},{12,20},{16,8},{20,12},{24,0},{28,4},{1,25},{... | collective-permute-start | bytes 405512 | tf_op jit(solution)/shard_map/ppermute | solution.py:280
  47.5 11.1 %collective-permute-start.16 = (f32[264,128]{1,0:T(8,128)S(1)}, f32[264,128]{1,0:T(8,128)S(1)}, u32[]{:S(2)}, u32[]{:S(2)}) collective-permute-start(f32[264,128]{1,0:T(8,128)S(1)} %add.46), channel_id=1, source_target_pairs={{0,16},{4,20},{8,24},{12,28},{16,0},{20,4},{24,8},{28,12},{1,17},{... | collective-permute-start | bytes 405512 | tf_op jit(solution)/shard_map/ppermute | solution.py:280
  47.5 11.1 %collective-permute-start.15 = (f32[264,128]{1,0:T(8,128)S(1)}, f32[264,128]{1,0:T(8,128)S(1)}, u32[]{:S(2)}, u32[]{:S(2)}) collective-permute-start(f32[264,128]{1,0:T(8,128)S(1)} %add.46), channel_id=1, source_target_pairs={{0,8},{4,12},{8,0},{12,4},{16,24},{20,28},{24,16},{28,20},{1,9},{5... | collective-permute-start | bytes 405512 | tf_op jit(solution)/shard_map/ppermute | solution.py:280
  58.6 1.4 %collective-permute-start.18 = (f32[264,128]{1,0:T(8,128)S(1)}, f32[264,128]{1,0:T(8,128)S(1)}, u32[]{:S(2)}, u32[]{:S(2)}) collective-permute-start(f32[264,128]{1,0:T(8,128)S(1)} %add_add_fusion.mine_ref), channel_id=1, source_target_pairs={{0,4},{4,0},{8,12},{12,8},{16,20},{20,16},{24,28},{28,24},{1,5},{5... | collective-permute-start | bytes 405512 | tf_op jit(solution)/shard_map/ppermute | solution.py:280
  64.1 1.2 %collective-permute-start.19 = (f32[16,128]{1,0:T(8,128)S(1)}, f32[16,128]{1,0:T(8,128)S(1)}, u32[]{:S(2)}, u32[]{:S(2)}) collective-permute-start(f32[16,128]{1,0:T(8,128)S(1)} %get-tuple-element.52), channel_id=1, source_target_pairs={{0,4},{4,0},{8,12},{12,8},{16,20},{20,16},{24,28},{28,24},{1,5},{5... | collective-permute-start | bytes 24584 | tf_op jit(solution)/shard_map/ppermute | solution.py:280
  65.3 6.1 %collective-permute-start.22 = (f32[16,128]{1,0:T(8,128)S(1)}, f32[16,128]{1,0:T(8,128)S(1)}, u32[]{:S(2)}, u32[]{:S(2)}) collective-permute-start(f32[16,128]{1,0:T(8,128)S(1)} %add.50), channel_id=1, source_target_pairs={{0,24},{4,28},{8,16},{12,20},{16,8},{20,12},{24,0},{28,4},{1,25},{... | collective-permute-start | bytes 24584 | tf_op jit(solution)/shard_map/ppermute | solution.py:280
  67.5 5.7 %collective-permute-start.21 = (f32[16,128]{1,0:T(8,128)S(1)}, f32[16,128]{1,0:T(8,128)S(1)}, u32[]{:S(2)}, u32[]{:S(2)}) collective-permute-start(f32[16,128]{1,0:T(8,128)S(1)} %add.50), channel_id=1, source_target_pairs={{0,16},{4,20},{8,24},{12,28},{16,0},{20,4},{24,8},{28,12},{1,17},{... | collective-permute-start | bytes 24584 | tf_op jit(solution)/shard_map/ppermute | solution.py:280
  67.5 5.7 %collective-permute-start.20 = (f32[16,128]{1,0:T(8,128)S(1)}, f32[16,128]{1,0:T(8,128)S(1)}, u32[]{:S(2)}, u32[]{:S(2)}) collective-permute-start(f32[16,128]{1,0:T(8,128)S(1)} %add.50), channel_id=1, source_target_pairs={{0,8},{4,12},{8,0},{12,4},{16,24},{20,28},{24,16},{28,20},{1,9},{5... | collective-permute-start | bytes 24584 | tf_op jit(solution)/shard_map/ppermute | solution.py:280
  69.7 7.7 %collective-permute-start.24 = (f32[64,512]{1,0:T(8,128)S(1)}, f32[64,512]{1,0:T(8,128)S(1)}, u32[]{:S(2)}, u32[]{:S(2)}) collective-permute-start(f32[64,512]{1,0:T(8,128)S(1)} %get-tuple-element.54), channel_id=1, source_target_pairs={{0,1},{1,0},{2,3},{3,2},{4,5},{5,4},{6,7},{7,6},{8,9},{9,8},{10,11... | collective-permute-start | bytes 393224 | tf_op jit(solution)/shard_map/ppermute | solution.py:280
  70.2 7.7 %collective-permute-start.25 = (f32[64,512]{1,0:T(8,128)S(1)}, f32[64,512]{1,0:T(8,128)S(1)}, u32[]{:S(2)}, u32[]{:S(2)}) collective-permute-start(f32[64,512]{1,0:T(8,128)S(1)} %get-tuple-element.55), channel_id=1, source_target_pairs={{0,2},{1,3},{2,0},{3,1},{4,6},{5,7},{6,4},{7,5},{8,10},{9,11},{10,... | collective-permute-start | bytes 393224 | tf_op jit(solution)/shard_map/ppermute | solution.py:280
  71.4 6.5 %collective-permute-start.26 = (f32[64,512]{1,0:T(8,128)S(1)}, f32[64,512]{1,0:T(8,128)S(1)}, u32[]{:S(2)}, u32[]{:S(2)}) collective-permute-start(f32[64,512]{1,0:T(8,128)S(1)} %get-tuple-element.56), channel_id=1, source_target_pairs={{0,3},{1,2},{2,1},{3,0},{4,7},{5,6},{6,5},{7,4},{8,11},{9,10},{10,... | collective-permute-start | bytes 393224 | tf_op jit(solution)/shard_map/ppermute | solution.py:280
  73.2 4.2 %collective-permute-start.23 = (f32[16,128]{1,0:T(8,128)S(1)}, f32[16,128]{1,0:T(8,128)S(1)}, u32[]{:S(2)}, u32[]{:S(2)}) collective-permute-start(f32[16,128]{1,0:T(8,128)S(1)} %add_add_fusion.2), channel_id=1, source_target_pairs={{0,1},{1,0},{2,3},{3,2},{4,5},{5,4},{6,7},{7,6},{8,9},{9,8},{10,11... | collective-permute-start | bytes 24584 | tf_op jit(solution)/shard_map/ppermute | solution.py:280
  77.9 3.7 %collective-permute-start.27 = (f32[16,128]{1,0:T(8,128)S(1)}, f32[16,128]{1,0:T(8,128)S(1)}, u32[]{:S(2)}, u32[]{:S(2)}) collective-permute-start(f32[16,128]{1,0:T(8,128)S(1)} %add.54), channel_id=1, source_target_pairs={{0,2},{1,3},{2,0},{3,1},{4,6},{5,7},{6,4},{7,5},{8,10},{9,11},{10,... | collective-permute-start | bytes 24584 | tf_op jit(solution)/shard_map/ppermute | solution.py:280

commit v5 on v4

--- a/solution.py
+++ b/solution.py
@@ -168,14 +168,12 @@
             half = -0.5 * square
             moves.append(split(jnp.where(ident, half + 1.5, half)))
         if step < NS_STEPS - 1:
-            products = [
-                mul(split(jnp.concatenate([square, block], axis=0)), move)
-                for square, block, move in zip(squares, blocks, moves)
-            ]
-            squares = [mul(split(product[:width]), move) for product, move in zip(products, moves)]
-            blocks = [product[width:] for product in products]
-        else:
-            blocks = [mul(split(block), move) for block, move in zip(blocks, moves)]
+            upper = [mul(split(square[: width // 2]), move) for square, move in zip(squares, moves)]
+            lower = [mul(split(square[width // 2 :]), move) for square, move in zip(squares, moves)]
+            upper = [mul(split(square), move) for square, move in zip(upper, moves)]
+            lower = [mul(split(square), move) for square, move in zip(lower, moves)]
+            squares = [jnp.concatenate(halves, axis=0) for halves in zip(upper, lower)]
+        blocks = [mul(split(block), move) for block, move in zip(blocks, moves)]
     return [block * scale for block, scale in zip(blocks, scales)]
 
 
@@ -196,8 +194,8 @@
                 out[(index + 1) * rows : (index + 2) * rows, :] = local_ref[pl.ds(start, rows), :]
 
 
-def one_side(mine, other, ref, half):
-    k, kt = coupling_of(mine, other, ref.shape[1] // 2)
+def one_side(pair_coupling, ref, half):
+    k, kt = pair_coupling
     is_first = half == 0
     return (
         jnp.where(is_first, k, kt),
@@ -208,12 +206,21 @@
     )
 
 
-def turn_kernel(table_ref, mine_ref, other_ref, local_ref, own_ref, *refs, rnd, masks, rest):
+def turn_kernel(get_table, mine_ref, other_ref, local_ref, own_ref, *refs, rnd, masks, rest):
     *refs, next_ref, keep_ref, send_ref, scratch, raw_ref = refs
     came_refs, came_other_refs, raw_refs = (refs[i * len(masks) : (i + 1) * len(masks)] for i in range(3))
     me = lax.axis_index("pair")
+    rows, width = own_ref.shape[0], own_ref.shape[1] // 2
+
+    def put(other, piece):
+        raw_ref[pl.ds(pl.multiple_of((me ^ other) * rows, rows), rows), :] = piece
+
+    put(0, own_ref[...])
+    for mask, ref in zip(masks, raw_refs):
+        put(mask, ref[:rows, :])
+    coupling = coupling_of(mine_ref[...], other_ref[...], width)
+    table_ref = get_table()
     source = sender(table_ref, me)
-    rows = own_ref.shape[0]
 
     def pick(parts):
         picked = parts[0]
@@ -221,37 +228,32 @@
             picked = jnp.where(source == (me ^ mask), part, picked)
         return picked
 
-    def put(other, piece):
-        raw_ref[pl.ds(pl.multiple_of((me ^ other) * rows, rows), rows), :] = piece
-
-    put(0, own_ref[...])
-    for mask, ref in zip(masks, raw_refs):
-        put(mask, ref[:rows, :])
     for index, other in enumerate(rest):
         put(other, pick([ref[(index + 1) * rows : (index + 2) * rows, :] for ref in raw_refs]))
-    half = 1 - note(table_ref, KEEPS, source)
-    came_pair = pick([ref[...] for ref in came_refs]), pick([ref[...] for ref in came_other_refs])
+    came_coupling = coupling_of(
+        pick([ref[...] for ref in came_refs]), pick([ref[...] for ref in came_other_refs]), width
+    )
     kept, came = turned(
         [
-            one_side(mine_ref[...], other_ref[...], local_ref, note(table_ref, KEEPS, me)),
-            one_side(*came_pair, raw_ref, half),
+            one_side(coupling, local_ref, note(table_ref, KEEPS, me)),
+            one_side(came_coupling, raw_ref, 1 - note(table_ref, KEEPS, source)),
         ]
     )
     kept_block = table_ref[rnd, 2 * note(table_ref, PAIR, me) + note(table_ref, KEEPS, me)]
     kept_first = kept_block == table_ref[rnd + 1, 2 * note(table_ref, NEXT, me)]
     first, second = jnp.where(kept_first, kept, came), jnp.where(kept_first, came, kept)
-    width = first.shape[1]
     next_ref[:, :width] = first
     next_ref[:, width:] = second
     cross_of(first, second, keep_ref, send_ref, scratch)
 
 
-def last_turn_kernel(table_ref, mine_ref, other_ref, local_ref, *refs, rnd):
+def last_turn_kernel(get_table, mine_ref, other_ref, local_ref, *refs, rnd):
     *outs, squares_ref, scratch = refs
     width = local_ref.shape[1] // 2
     first, second = local_ref[:, :width], local_ref[:, width:]
     k, kt = coupling_of(mine_ref[...], other_ref[...], width)
     new = turned([(k, kt, first, -1.0, second), (kt, k, second, 1.0, first)])
+    table_ref = get_table()
     me = lax.axis_index("pair")
     squares_ref[...] = jnp.zeros_like(squares_ref)
     for half in range(2):
@@ -290,22 +292,46 @@
     return parts[0]
 
 
+def shares(x, axis, step):
+    return [x] + [swap(x, axis, mask) for mask in range(step, lax.axis_size(axis), step)]
+
+
 def over_chips(x):
-    return tree_sum([x] + [swap(x, "row", mask) for mask in range(2, lax.axis_size("row"), 2)])
+    return tree_sum(shares(x, "row", 2))
 
 
 def powers(size):
     return [1 << bit for bit in range(size.bit_length() - 1)]
 
 
-def call(kernel, ins, outs, scratch=(), table=None, cost=None):
+def with_late_table(kernel):
+    def run(table_vmem, *refs):
+        *refs, table_ref, sem = refs
+        copy = pltpu.make_async_copy(table_vmem, table_ref, sem)
+        copy.start()
+
+        def arrived():
+            copy.wait()
+            return table_ref
+
+        kernel(arrived, *refs)
+
+    return run
+
+
+def call(kernel, ins, outs, scratch=(), table=None, late=False, cost=None):
     ins = ([] if table is None else [table]) + ins
+    scratch = [pltpu.VMEM(shape, jnp.float32) for shape in scratch]
+    if late:
+        kernel = with_late_table(kernel)
+        scratch += [pltpu.SMEM(table.shape, jnp.int32), pltpu.SemaphoreType.DMA]
+    in_smem = table is not None and not late
     return pl.pallas_call(
         kernel,
         out_shape=[jax.ShapeDtypeStruct(shape, jnp.float32) for shape in outs],
-        in_specs=[SMEM] * (table is not None) + [VMEM] * (len(ins) - (table is not None)),
+        in_specs=[SMEM] * in_smem + [VMEM] * (len(ins) - in_smem),
         out_specs=[VMEM] * len(outs),
-        scratch_shapes=[pltpu.VMEM(shape, jnp.float32) for shape in scratch],
+        scratch_shapes=scratch,
         compiler_params=pltpu.CompilerParams(vmem_limit_bytes=24 * 2**20),
         cost_estimate=cost,
     )(*ins)
@@ -364,6 +390,7 @@
         crossed,
         [square, (group_rows, both)],
         table,
+        late=True,
     )
     mine = over_chips(keep + swap(send, "row", 1))
     *sent, squares = call(
@@ -372,14 +399,15 @@
         [(piece_rows, both)] * pair_count + [(ncols // LANES, LANES)],
         [(group_rows, both)],
         table,
-    )
-    back = spread(sent)
-    squares = over_chips(squares + swap(squares, "row", 1))
-    hops = powers(pair_count)
-    for mask in hops[:-1]:
-        squares = squares + swap(squares, "pair", mask)
-    squares, back = lax.optimization_barrier((squares, back))
-    squares = squares + swap(squares, "pair", hops[-1])
+        late=True,
+    )
+    squares, first_sent = lax.optimization_barrier((squares, sent[1]))
+    back = [sent[0], swap(first_sent, "pair", 1)]
+    squares = squares + swap(squares, "row", 1)
+    squares, sent = lax.optimization_barrier((squares, sent))
+    back += [swap(sent[mask], "pair", mask) for mask in range(2, pair_count)]
+    parts, back[1] = lax.optimization_barrier((shares(squares, "row", 2), back[1]))
+    squares = tree_sum(shares(tree_sum(parts), "pair", 1))
     (rotated,) = call(
         functools.partial(place_kernel, rnd=1),
         back,

time: 82.4 us -> 79.5 us (0.965)
  waiting for transfers between devices: 38.5 us -> 34.7 us
  starting transfers between devices: 27.6 us -> 29.5 us
  Pallas kernels: 13.2 us -> 12.1 us
    ppermute x28 -> x29, waiting for transfers between devices: 38.5 us -> 34.7 us  [swap(): lax.ppermute(x, axis, [(i, i ^ mask) for i in range(lax.axis_size(axis))])]
    ppermute x28 -> x29, starting transfers between devices: 27.6 us -> 29.5 us  [swap(): lax.ppermute(x, axis, [(i, i ^ mask) for i in range(lax.axis_size(axis))])]
    pallas_call x6, Pallas kernels: 11.3 us -> 10.2 us  [call(): pl.pallas_call(kernel, out_shape=[jax.ShapeDtypeStruct(shape, jnp.float32...]
  transfers between devices with their start and end apart: 28 -> 29, of which waited for: 16 -> 14; matrix products, arithmetic and copies ran while one was open for 0% -> 0% of each run, Pallas kernels for 3% -> 3%
where the time goes in v5:
time: 79.5 us; the launch traced here: 79.3 us
  waiting for transfers between devices  34.7 us (44%)
  starting transfers between devices  29.5 us (37%)
  Pallas kernels  12.1 us (15%)
  local copies, waits for them, and re-layouts  1.5 us (2%)
    ppermute x29, waiting for transfers between devices, swap(): lax.ppermute(x, axis, [(i, i ^ mask) for i in range(lax.axis_size(axis))])  34.7 us
    ppermute x29, starting transfers between devices, swap(): lax.ppermute(x, axis, [(i, i ^ mask) for i in range(lax.axis_size(axis))])  29.5 us
    pallas_call x6, Pallas kernels, call(): pl.pallas_call(kernel, out_shape=[jax.ShapeDtypeStruct(shape, jnp.float32...  10.2 us
    pallas_call x1, Pallas kernels, deal(): pl.pallas_call(functools.partial(deal_kernel, rnd=rnd), out_shape=[jax.Sh...  1.88 us
  transfers between devices with their start and end apart: 29, of which 14 were waited for; matrix products, arithmetic and copies ran while one was open for 0% of the time, Pallas kernels for 3%

profile of v5, /device:TPU:0, one launch (start us, length us, event | category | flops | bytes accessed | tf_op | source)
XLA Modules:
  0.0 79.3 jit_solution(14643352288159533976)
XLA Ops:
  0.6 1.9 %shard_map.41 = (s32[6,8]{1,0:T(8,128)}, f32[64,512]{1,0:T(8,128)}, f32[64,512]{1,0:T(8,128)}, f32[64,512]{1,0:T(8,128)}, f32[64,512]{1,0:T(8,128)}) custom-call(s32[2,8]{1,0:T(2,128)} %plan_hbm.1, f32[64,2048]{1,0:T(8,128)} %slab_ref.1), custom_call_target="tpu_custom_call" | custom-call | tf_op jit(solution)/shard_map/pallas_call | solution.py:344
  2.5 0.0 copy-start
  2.5 3.0 %collective-permute-start = (f32[64,512]{1,0:T(8,128)}, f32[64,512]{1,0:T(8,128)S(1)}, u32[]{:S(2)}, u32[]{:S(2)}) collective-permute-start(f32[64,512]{1,0:T(8,128)} %get-tuple-element.39), channel_id=1, source_target_pairs={{0,1},{1,0},{2,3},{3,2},{4,5},{5,4},{6,7},{7,6},{8,9},{9,8},{10,11... | collective-permute-start | bytes 393224 | tf_op jit(solution)/shard_map/ppermute | solution.py:282
  5.5 1.5 %collective-permute-start.1 = (f32[64,512]{1,0:T(8,128)}, f32[64,512]{1,0:T(8,128)S(1)}, u32[]{:S(2)}, u32[]{:S(2)}) collective-permute-start(f32[64,512]{1,0:T(8,128)} %get-tuple-element.40), channel_id=1, source_target_pairs={{0,2},{1,3},{2,0},{3,1},{4,6},{5,7},{6,4},{7,5},{8,10},{9,11},{10,... | collective-permute-start | bytes 393224 | tf_op jit(solution)/shard_map/ppermute | solution.py:282
  7.1 0.0 collective-permute-start.2
  7.1 0.9 %copy-done.1 = f32[64,512]{1,0:T(8,128)S(1)} copy-done((f32[64,512]{1,0:T(8,128)S(1)}, f32[64,512]{1,0:T(8,128)}, u32[]{:S(2)}) %copy-start.1) | copy-done | bytes 131096
  8.0 1.8 %collective-permute-done.refs_1_ = f32[64,512]{1,0:T(8,128)S(1)} collective-permute-done((f32[64,512]{1,0:T(8,128)}, f32[64,512]{1,0:T(8,128)S(1)}, u32[]{:S(2)}, u32[]{:S(2)}) %collective-permute-start) | collective-permute-done | bytes 131104 | tf_op jit(solution)/shard_map/ppermute | solution.py:282
  9.8 3.8 %collective-permute-done.1.refs_2_ = f32[64,512]{1,0:T(8,128)S(1)} collective-permute-done((f32[64,512]{1,0:T(8,128)}, f32[64,512]{1,0:T(8,128)S(1)}, u32[]{:S(2)}, u32[]{:S(2)}) %collective-permute-start.1) | collective-permute-done | bytes 131104 | tf_op jit(solution)/shard_map/ppermute | solution.py:282
  13.5 0.0 collective-permute-done.2.refs_3_
  13.5 0.4 shard_map.43
  13.9 0.0 copy-start.2
  14.0 0.1 collective-permute-start.3
  14.0 0.6 copy-done.2
  14.6 0.7 shard_map.44
  15.3 0.1 collective-permute-done.3
  15.4 3.7 %collective-permute-start.6 = (f32[264,128]{1,0:T(8,128)S(1)}, f32[264,128]{1,0:T(8,128)S(1)}, u32[]{:S(2)}, u32[]{:S(2)}) collective-permute-start(f32[264,128]{1,0:T(8,128)S(1)} %add.45), channel_id=1, source_target_pairs={{0,24},{4,28},{8,16},{12,20},{16,8},{20,12},{24,0},{28,4},{1,25},{... | collective-permute-start | bytes 405512 | tf_op jit(solution)/shard_map/ppermute | solution.py:282
  19.1 0.0 collective-permute-start.5
  19.1 0.8 collective-permute-start.4
  19.8 1.2 %collective-permute-start.7 = (f32[128,512]{1,0:T(8,128)S(1)}, f32[128,512]{1,0:T(8,128)S(1)}, u32[]{:S(2)}, u32[]{:S(2)}) collective-permute-start(f32[128,512]{1,0:T(8,128)S(1)} %get-tuple-element.48), channel_id=1, source_target_pairs={{0,1},{1,0},{2,3},{3,2},{4,5},{5,4},{6,7},{7,6},{8,9},{9,8},{10,11... | collective-permute-start | bytes 786440 | tf_op jit(solution)/shard_map/ppermute | solution.py:282
  21.1 0.8 %collective-permute-start.8 = (f32[128,512]{1,0:T(8,128)S(1)}, f32[128,512]{1,0:T(8,128)S(1)}, u32[]{:S(2)}, u32[]{:S(2)}) collective-permute-start(f32[128,512]{1,0:T(8,128)S(1)} %get-tuple-element.49), channel_id=1, source_target_pairs={{0,2},{1,3},{2,0},{3,1},{4,6},{5,7},{6,4},{7,5},{8,10},{9,11},{10,... | collective-permute-start | bytes 786440 | tf_op jit(solution)/shard_map/ppermute | solution.py:282
  21.9 1.9 %collective-permute-done.6 = f32[264,128]{1,0:T(8,128)S(1)} collective-permute-done((f32[264,128]{1,0:T(8,128)S(1)}, f32[264,128]{1,0:T(8,128)S(1)}, u32[]{:S(2)}, u32[]{:S(2)}) %collective-permute-start.6) | collective-permute-done | bytes 135200 | tf_op jit(solution)/shard_map/ppermute | solution.py:282
  23.8 7.0 %collective-permute-done.5 = f32[264,128]{1,0:T(8,128)S(1)} collective-permute-done((f32[264,128]{1,0:T(8,128)S(1)}, f32[264,128]{1,0:T(8,128)S(1)}, u32[]{:S(2)}, u32[]{:S(2)}) %collective-permute-start.5) | collective-permute-done | bytes 135200 | tf_op jit(solution)/shard_map/ppermute | solution.py:282
  30.8 0.0 collective-permute-done.4
  30.8 0.0 collective-permute-done.7.refs_8_
  30.8 0.0 collective-permute-done.8.refs_9_
  30.9 1.6 %collective-permute-start.11 = (f32[264,128]{1,0:T(8,128)S(1)}, f32[264,128]{1,0:T(8,128)S(1)}, u32[]{:S(2)}, u32[]{:S(2)}) collective-permute-start(f32[264,128]{1,0:T(8,128)S(1)} %add_add_fusion.1.refs_0_), channel_id=1, source_target_pairs={{0,2},{1,3},{2,0},{3,1},{4,6},{5,7},{6,4},{7,5},{8,10},{9,11},{10,... | collective-permute-start | bytes 405512 | tf_op jit(solution)/shard_map/ppermute | solution.py:282
  32.4 0.5 collective-permute-start.10
  33.0 0.0 collective-permute-start.9
  33.0 3.0 %collective-permute-done.11.refs_5_ = f32[264,128]{1,0:T(8,128)S(1)} collective-permute-done((f32[264,128]{1,0:T(8,128)S(1)}, f32[264,128]{1,0:T(8,128)S(1)}, u32[]{:S(2)}, u32[]{:S(2)}) %collective-permute-start.11) | collective-permute-done | bytes 135200 | tf_op jit(solution)/shard_map/ppermute | solution.py:282
  35.9 0.0 collective-permute-start.13
  35.9 1.5 %collective-permute-done.10.refs_4_ = f32[264,128]{1,0:T(8,128)S(1)} collective-permute-done((f32[264,128]{1,0:T(8,128)S(1)}, f32[264,128]{1,0:T(8,128)S(1)}, u32[]{:S(2)}, u32[]{:S(2)}) %collective-permute-start.10) | collective-permute-done | bytes 135200 | tf_op jit(solution)/shard_map/ppermute | solution.py:282
  37.4 0.0 collective-permute-start.12
  37.4 0.0 collective-permute-done.9.refs_1_
  37.4 0.0 collective-permute-done.13.refs_7_
  37.5 1.3 %collective-permute-done.12.refs_6_ = f32[264,128]{1,0:T(8,128)S(1)} collective-permute-done((f32[264,128]{1,0:T(8,128)S(1)}, f32[264,128]{1,0:T(8,128)S(1)}, u32[]{:S(2)}, u32[]{:S(2)}) %collective-permute-start.12) | collective-permute-done | bytes 135200 | tf_op jit(solution)/shard_map/ppermute | solution.py:282
  38.8 4.5 %shard_map.45 = (f32[256,512]{1,0:T(8,128)S(1)}, f32[264,128]{1,0:T(8,128)S(1)}, f32[264,128]{1,0:T(8,128)S(1)}) custom-call(s32[6,8]{1,0:T(8,128)S(1)} %copy-done.2, f32[264,128]{1,0:T(8,128)S(1)} %add_add_fusion.1.refs_0_, f32[264,128]{1,0:T(8,128)S(1)} %collective-permute-done.9.refs_1_, f32[256,512]{1,0:T(8,128)S(1)} %get-tuple-element.44.local_ref.refs_2_, ...), custom_call_target="tpu_custom_call" | custom-call | tf_op jit(solution)/shard_map/pallas_call | solution.py:329
  43.3 0.2 collective-permute-start.14
  43.5 1.2 %collective-permute-done.14 = f32[264,128]{1,0:T(8,128)S(1)} collective-permute-done((f32[264,128]{1,0:T(8,128)S(1)}, f32[264,128]{1,0:T(8,128)S(1)}, u32[]{:S(2)}, u32[]{:S(2)}) %collective-permute-start.14) | collective-permute-done | bytes 135200 | tf_op jit(solution)/shard_map/ppermute | solution.py:282
  44.7 2.5 %collective-permute-start.17 = (f32[264,128]{1,0:T(8,128)S(1)}, f32[264,128]{1,0:T(8,128)S(1)}, u32[]{:S(2)}, u32[]{:S(2)}) collective-permute-start(f32[264,128]{1,0:T(8,128)S(1)} %add.49), channel_id=1, source_target_pairs={{0,24},{4,28},{8,16},{12,20},{16,8},{20,12},{24,0},{28,4},{1,25},{... | collective-permute-start | bytes 405512 | tf_op jit(solution)/shard_map/ppermute | solution.py:282
  47.3 1.9 %collective-permute-start.15 = (f32[264,128]{1,0:T(8,128)S(1)}, f32[264,128]{1,0:T(8,128)S(1)}, u32[]{:S(2)}, u32[]{:S(2)}) collective-permute-start(f32[264,128]{1,0:T(8,128)S(1)} %add.49), channel_id=1, source_target_pairs={{0,8},{4,12},{8,0},{12,4},{16,24},{20,28},{24,16},{28,20},{1,9},{5... | collective-permute-start | bytes 405512 | tf_op jit(solution)/shard_map/ppermute | solution.py:282
  49.2 4.0 %collective-permute-done.17 = f32[264,128]{1,0:T(8,128)S(1)} collective-permute-done((f32[264,128]{1,0:T(8,128)S(1)}, f32[264,128]{1,0:T(8,128)S(1)}, u32[]{:S(2)}, u32[]{:S(2)}) %collective-permute-start.17) | collective-permute-done | bytes 135200 | tf_op jit(solution)/shard_map/ppermute | solution.py:282
  53.1 5.2 %collective-permute-done.16 = f32[264,128]{1,0:T(8,128)S(1)} collective-permute-done((f32[264,128]{1,0:T(8,128)S(1)}, f32[264,128]{1,0:T(8,128)S(1)}, u32[]{:S(2)}, u32[]{:S(2)}) %collective-permute-start.16) | collective-permute-done | bytes 135200 | tf_op jit(solution)/shard_map/ppermute | solution.py:282
  58.4 0.1 collective-permute-start.18
  58.4 1.3 %collective-permute-done.18.refs_1_ = f32[264,128]{1,0:T(8,128)S(1)} collective-permute-done((f32[264,128]{1,0:T(8,128)S(1)}, f32[264,128]{1,0:T(8,128)S(1)}, u32[]{:S(2)}, u32[]{:S(2)}) %collective-permute-start.18) | collective-permute-done | bytes 135200 | tf_op jit(solution)/shard_map/ppermute | solution.py:282
  59.8 3.3 %shard_map.46 = (f32[64,512]{1,0:T(8,128)S(1)}, f32[64,512]{1,0:T(8,128)S(1)}, f32[64,512]{1,0:T(8,128)S(1)}, f32[64,512]{1,0:T(8,128)S(1)}, f32[16,128]{1,0:T(8,128)S(1)}) custom-call(s32[6,8]{1,0:T(8,128)S(1)} %copy-done.2, f32[264,128]{1,0:T(8,128)S(1)} %add_add_fusion.refs_0_, f32[264,128]{1,0:T(8,128)S(1)} %collective-permute-done.18.refs_1_, ...), custom_call_target="tpu_custom_call" | custom-call | tf_op jit(solution)/shard_map/pallas_call | solution.py:329
  63.1 0.6 collective-permute-start.23
  63.7 1.2 %collective-permute-done.19 = f32[16,128]{1,0:T(8,128)S(1)} collective-permute-done((f32[16,128]{1,0:T(8,128)S(1)}, f32[16,128]{1,0:T(8,128)S(1)}, u32[]{:S(2)}, u32[]{:S(2)}) %collective-permute-start.19) | collective-permute-done | bytes 8224 | tf_op jit(solution)/shard_map/ppermute | solution.py:282
  64.8 2.2 %collective-permute-start.22 = (f32[16,128]{1,0:T(8,128)S(1)}, f32[16,128]{1,0:T(8,128)S(1)}, u32[]{:S(2)}, u32[]{:S(2)}) collective-permute-start(f32[16,128]{1,0:T(8,128)S(1)} %add.53), channel_id=1, source_target_pairs={{0,24},{4,28},{8,16},{12,20},{16,8},{20,12},{24,0},{28,4},{1,25},{... | collective-permute-start | bytes 24584 | tf_op jit(solution)/shard_map/ppermute | solution.py:282
  67.1 0.0 collective-permute-start.21
  67.1 2.2 %collective-permute-start.20 = (f32[16,128]{1,0:T(8,128)S(1)}, f32[16,128]{1,0:T(8,128)S(1)}, u32[]{:S(2)}, u32[]{:S(2)}) collective-permute-start(f32[16,128]{1,0:T(8,128)S(1)} %add.53), channel_id=1, source_target_pairs={{0,8},{4,12},{8,0},{12,4},{16,24},{20,28},{24,16},{28,20},{1,9},{5... | collective-permute-start | bytes 24584 | tf_op jit(solution)/shard_map/ppermute | solution.py:282
  69.2 1.2 %collective-permute-start.24 = (f32[64,512]{1,0:T(8,128)S(1)}, f32[64,512]{1,0:T(8,128)S(1)}, u32[]{:S(2)}, u32[]{:S(2)}) collective-permute-start(f32[64,512]{1,0:T(8,128)S(1)} %get-tuple-element.66), channel_id=1, source_target_pairs={{0,2},{1,3},{2,0},{3,1},{4,6},{5,7},{6,4},{7,5},{8,10},{9,11},{10,... | collective-permute-start | bytes 393224 | tf_op jit(solution)/shard_map/ppermute | solution.py:282
  70.4 0.0 collective-permute-done.22
  70.4 1.8 %collective-permute-start.25 = (f32[64,512]{1,0:T(8,128)S(1)}, f32[64,512]{1,0:T(8,128)S(1)}, u32[]{:S(2)}, u32[]{:S(2)}) collective-permute-start(f32[64,512]{1,0:T(8,128)S(1)} %get-tuple-element.67), channel_id=1, source_target_pairs={{0,3},{1,2},{2,1},{3,0},{4,7},{5,6},{6,5},{7,4},{8,11},{9,10},{10,... | collective-permute-start | bytes 393224 | tf_op jit(solution)/shard_map/ppermute | solution.py:282
  72.2 0.0 collective-permute-done.21
  72.2 0.0 collective-permute-done.20
  72.2 0.0 collective-permute-done.23.refs_1_
  72.2 1.2 %collective-permute-start.28 = (f32[16,128]{1,0:T(8,128)S(1)}, f32[16,128]{1,0:T(8,128)S(1)}, u32[]{:S(2)}, u32[]{:S(2)}) collective-permute-start(f32[16,128]{1,0:T(8,128)S(1)} %add_add_fusion.2), channel_id=1, source_target_pairs={{0,3},{1,2},{2,1},{3,0},{4,7},{5,6},{6,5},{7,4},{8,11},{9,10},{10,... | collective-permute-start | bytes 24584 | tf_op jit(solution)/shard_map/ppermute | solution.py:282
  73.4 1.2 %collective-permute-start.27 = (f32[16,128]{1,0:T(8,128)S(1)}, f32[16,128]{1,0:T(8,128)S(1)}, u32[]{:S(2)}, u32[]{:S(2)}) collective-permute-start(f32[16,128]{1,0:T(8,128)S(1)} %add_add_fusion.2), channel_id=1, source_target_pairs={{0,2},{1,3},{2,0},{3,1},{4,6},{5,7},{6,4},{7,5},{8,10},{9,11},{10,... | collective-permute-start | bytes 24584 | tf_op jit(solution)/shard_map/ppermute | solution.py:282
  74.6 1.1 %collective-permute-start.26 = (f32[16,128]{1,0:T(8,128)S(1)}, f32[16,128]{1,0:T(8,128)S(1)}, u32[]{:S(2)}, u32[]{:S(2)}) collective-permute-start(f32[16,128]{1,0:T(8,128)S(1)} %add_add_fusion.2), channel_id=1, source_target_pairs={{0,1},{1,0},{2,3},{3,2},{4,5},{5,4},{6,7},{7,6},{8,9},{9,8},{10,11... | collective-permute-start | bytes 24584 | tf_op jit(solution)/shard_map/ppermute | solution.py:282
  75.8 1.5 %collective-permute-done.24.refs_2_ = f32[64,512]{1,0:T(8,128)S(1)} collective-permute-done((f32[64,512]{1,0:T(8,128)S(1)}, f32[64,512]{1,0:T(8,128)S(1)}, u32[]{:S(2)}, u32[]{:S(2)}) %collective-permute-start.24) | collective-permute-done | bytes 131104 | tf_op jit(solution)/shard_map/ppermute | solution.py:282
  77.3 0.0 collective-permute-done.25.refs_3_
  77.3 1.4 %shard_map.47 = f32[64,2048]{1,0:T(8,128)} custom-call(s32[6,8]{1,0:T(8,128)S(1)} %copy-done.2, f32[64,512]{1,0:T(8,128)S(1)} %get-tuple-element.57.refs_0_, f32[64,512]{1,0:T(8,128)S(1)} %collective-permute-done.23.refs_1_, f32[64,512]{1,0:T(8,128)S(1)} %collective-permute-done.24.refs_2_, f32[64,512]{1,0:T(8,128)S(1)} %collective-permute-done.25.refs_3_), custom_call_target="tpu_custom_call" | custom-call | bytes 1048576 | tf_op jit(solution)/shard_map/pallas_call | solution.py:329
  78.7 0.0 collective-permute-done.26
  78.7 0.6 sqrt_bitcast_fusion
  (14 shorter events, 0.1 us)
Async XLA Ops:
  2.5 11.5 %copy-start = (f32[64,2048]{1,0:T(8,128)S(1)}, f32[64,2048]{1,0:T(8,128)}, u32[]{:S(2)}) copy-start(f32[64,2048]{1,0:T(8,128)} %slab_ref.1) | copy-start | bytes 1572868
  2.5 7.2 %collective-permute-start = (f32[64,512]{1,0:T(8,128)}, f32[64,512]{1,0:T(8,128)S(1)}, u32[]{:S(2)}, u32[]{:S(2)}) collective-permute-start(f32[64,512]{1,0:T(8,128)} %get-tuple-element.39), channel_id=1, source_target_pairs={{0,1},{1,0},{2,3},{3,2},{4,5},{5,4},{6,7},{7,6},{8,9},{9,8},{10,11... | collective-permute-start | bytes 393224 | tf_op jit(solution)/shard_map/ppermute | solution.py:282
  5.5 8.0 %collective-permute-start.1 = (f32[64,512]{1,0:T(8,128)}, f32[64,512]{1,0:T(8,128)S(1)}, u32[]{:S(2)}, u32[]{:S(2)}) collective-permute-start(f32[64,512]{1,0:T(8,128)} %get-tuple-element.40), channel_id=1, source_target_pairs={{0,2},{1,3},{2,0},{3,1},{4,6},{5,7},{6,4},{7,5},{8,10},{9,11},{10,... | collective-permute-start | bytes 393224 | tf_op jit(solution)/shard_map/ppermute | solution.py:282
  7.1 6.5 %collective-permute-start.2 = (f32[64,512]{1,0:T(8,128)}, f32[64,512]{1,0:T(8,128)S(1)}, u32[]{:S(2)}, u32[]{:S(2)}) collective-permute-start(f32[64,512]{1,0:T(8,128)} %get-tuple-element.41), channel_id=1, source_target_pairs={{0,3},{1,2},{2,1},{3,0},{4,7},{5,6},{6,5},{7,4},{8,11},{9,10},{10,... | collective-permute-start | bytes 393224 | tf_op jit(solution)/shard_map/ppermute | solution.py:282
  7.1 0.9 %copy-start.1 = (f32[64,512]{1,0:T(8,128)S(1)}, f32[64,512]{1,0:T(8,128)}, u32[]{:S(2)}) copy-start(f32[64,512]{1,0:T(8,128)} %get-tuple-element.38.in_ref) | copy-start | bytes 393220
  13.9 0.7 copy-start.2
  14.0 1.4 %collective-permute-start.3 = (f32[264,128]{1,0:T(8,128)S(1)}, f32[264,128]{1,0:T(8,128)S(1)}, u32[]{:S(2)}, u32[]{:S(2)}) collective-permute-start(f32[264,128]{1,0:T(8,128)S(1)} %get-tuple-element.43), channel_id=1, source_target_pairs={{0,4},{4,0},{8,12},{12,8},{16,20},{20,16},{24,28},{28,24},{1,5},{5... | collective-permute-start | bytes 405512 | tf_op jit(solution)/shard_map/ppermute | solution.py:282
  15.4 8.4 %collective-permute-start.6 = (f32[264,128]{1,0:T(8,128)S(1)}, f32[264,128]{1,0:T(8,128)S(1)}, u32[]{:S(2)}, u32[]{:S(2)}) collective-permute-start(f32[264,128]{1,0:T(8,128)S(1)} %add.45), channel_id=1, source_target_pairs={{0,24},{4,28},{8,16},{12,20},{16,8},{20,12},{24,0},{28,4},{1,25},{... | collective-permute-start | bytes 405512 | tf_op jit(solution)/shard_map/ppermute | solution.py:282
  19.1 11.7 %collective-permute-start.5 = (f32[264,128]{1,0:T(8,128)S(1)}, f32[264,128]{1,0:T(8,128)S(1)}, u32[]{:S(2)}, u32[]{:S(2)}) collective-permute-start(f32[264,128]{1,0:T(8,128)S(1)} %add.45), channel_id=1, source_target_pairs={{0,16},{4,20},{8,24},{12,28},{16,0},{20,4},{24,8},{28,12},{1,17},{... | collective-permute-start | bytes 405512 | tf_op jit(solution)/shard_map/ppermute | solution.py:282
  19.1 11.7 %collective-permute-start.4 = (f32[264,128]{1,0:T(8,128)S(1)}, f32[264,128]{1,0:T(8,128)S(1)}, u32[]{:S(2)}, u32[]{:S(2)}) collective-permute-start(f32[264,128]{1,0:T(8,128)S(1)} %add.45), channel_id=1, source_target_pairs={{0,8},{4,12},{8,0},{12,4},{16,24},{20,28},{24,16},{28,20},{1,9},{5... | collective-permute-start | bytes 405512 | tf_op jit(solution)/shard_map/ppermute | solution.py:282
  19.8 11.0 %collective-permute-start.7 = (f32[128,512]{1,0:T(8,128)S(1)}, f32[128,512]{1,0:T(8,128)S(1)}, u32[]{:S(2)}, u32[]{:S(2)}) collective-permute-start(f32[128,512]{1,0:T(8,128)S(1)} %get-tuple-element.48), channel_id=1, source_target_pairs={{0,1},{1,0},{2,3},{3,2},{4,5},{5,4},{6,7},{7,6},{8,9},{9,8},{10,11... | collective-permute-start | bytes 786440 | tf_op jit(solution)/shard_map/ppermute | solution.py:282
  21.1 9.8 %collective-permute-start.8 = (f32[128,512]{1,0:T(8,128)S(1)}, f32[128,512]{1,0:T(8,128)S(1)}, u32[]{:S(2)}, u32[]{:S(2)}) collective-permute-start(f32[128,512]{1,0:T(8,128)S(1)} %get-tuple-element.49), channel_id=1, source_target_pairs={{0,2},{1,3},{2,0},{3,1},{4,6},{5,7},{6,4},{7,5},{8,10},{9,11},{10,... | collective-permute-start | bytes 786440 | tf_op jit(solution)/shard_map/ppermute | solution.py:282
  30.9 5.1 %collective-permute-start.11 = (f32[264,128]{1,0:T(8,128)S(1)}, f32[264,128]{1,0:T(8,128)S(1)}, u32[]{:S(2)}, u32[]{:S(2)}) collective-permute-start(f32[264,128]{1,0:T(8,128)S(1)} %add_add_fusion.1.refs_0_), channel_id=1, source_target_pairs={{0,2},{1,3},{2,0},{3,1},{4,6},{5,7},{6,4},{7,5},{8,10},{9,11},{10,... | collective-permute-start | bytes 405512 | tf_op jit(solution)/shard_map/ppermute | solution.py:282
  32.4 5.0 %collective-permute-start.10 = (f32[264,128]{1,0:T(8,128)S(1)}, f32[264,128]{1,0:T(8,128)S(1)}, u32[]{:S(2)}, u32[]{:S(2)}) collective-permute-start(f32[264,128]{1,0:T(8,128)S(1)} %add_add_fusion.1.refs_0_), channel_id=1, source_target_pairs={{0,1},{1,0},{2,3},{3,2},{4,5},{5,4},{6,7},{7,6},{8,9},{9,8},{10,11... | collective-permute-start | bytes 405512 | tf_op jit(solution)/shard_map/ppermute | solution.py:282
  33.0 4.5 %collective-permute-start.9 = (f32[264,128]{1,0:T(8,128)S(1)}, f32[264,128]{1,0:T(8,128)S(1)}, u32[]{:S(2)}, u32[]{:S(2)}) collective-permute-start(f32[264,128]{1,0:T(8,128)S(1)} %add_add_fusion.1.refs_0_), channel_id=1, source_target_pairs={{0,4},{4,0},{8,12},{12,8},{16,20},{20,16},{24,28},{28,24},{1,5},{5... | collective-permute-start | bytes 405512 | tf_op jit(solution)/shard_map/ppermute | solution.py:282
  35.9 1.5 %collective-permute-start.13 = (f32[264,128]{1,0:T(8,128)S(1)}, f32[264,128]{1,0:T(8,128)S(1)}, u32[]{:S(2)}, u32[]{:S(2)}) collective-permute-start(f32[264,128]{1,0:T(8,128)S(1)} %collective-permute-done.11.refs_5_), channel_id=1, source_target_pairs={{0,4},{4,0},{8,12},{12,8},{16,20},{20,16},{24,28},{28,24},{1,5},{5... | collective-permute-start | bytes 405512 | tf_op jit(solution)/shard_map/ppermute | solution.py:282
  37.4 1.4 %collective-permute-start.12 = (f32[264,128]{1,0:T(8,128)S(1)}, f32[264,128]{1,0:T(8,128)S(1)}, u32[]{:S(2)}, u32[]{:S(2)}) collective-permute-start(f32[264,128]{1,0:T(8,128)S(1)} %collective-permute-done.10.refs_4_), channel_id=1, source_target_pairs={{0,4},{4,0},{8,12},{12,8},{16,20},{20,16},{24,28},{28,24},{1,5},{5... | collective-permute-start | bytes 405512 | tf_op jit(solution)/shard_map/ppermute | solution.py:282
  43.3 1.4 %collective-permute-start.14 = (f32[264,128]{1,0:T(8,128)S(1)}, f32[264,128]{1,0:T(8,128)S(1)}, u32[]{:S(2)}, u32[]{:S(2)}) collective-permute-start(f32[264,128]{1,0:T(8,128)S(1)} %get-tuple-element.55), channel_id=1, source_target_pairs={{0,4},{4,0},{8,12},{12,8},{16,20},{20,16},{24,28},{28,24},{1,5},{5... | collective-permute-start | bytes 405512 | tf_op jit(solution)/shard_map/ppermute | solution.py:282
  44.7 8.4 %collective-permute-start.17 = (f32[264,128]{1,0:T(8,128)S(1)}, f32[264,128]{1,0:T(8,128)S(1)}, u32[]{:S(2)}, u32[]{:S(2)}) collective-permute-start(f32[264,128]{1,0:T(8,128)S(1)} %add.49), channel_id=1, source_target_pairs={{0,24},{4,28},{8,16},{12,20},{16,8},{20,12},{24,0},{28,4},{1,25},{... | collective-permute-start | bytes 405512 | tf_op jit(solution)/shard_map/ppermute | solution.py:282
  47.3 11.1 %collective-permute-start.16 = (f32[264,128]{1,0:T(8,128)S(1)}, f32[264,128]{1,0:T(8,128)S(1)}, u32[]{:S(2)}, u32[]{:S(2)}) collective-permute-start(f32[264,128]{1,0:T(8,128)S(1)} %add.49), channel_id=1, source_target_pairs={{0,16},{4,20},{8,24},{12,28},{16,0},{20,4},{24,8},{28,12},{1,17},{... | collective-permute-start | bytes 405512 | tf_op jit(solution)/shard_map/ppermute | solution.py:282
  47.3 11.1 %collective-permute-start.15 = (f32[264,128]{1,0:T(8,128)S(1)}, f32[264,128]{1,0:T(8,128)S(1)}, u32[]{:S(2)}, u32[]{:S(2)}) collective-permute-start(f32[264,128]{1,0:T(8,128)S(1)} %add.49), channel_id=1, source_target_pairs={{0,8},{4,12},{8,0},{12,4},{16,24},{20,28},{24,16},{28,20},{1,9},{5... | collective-permute-start | bytes 405512 | tf_op jit(solution)/shard_map/ppermute | solution.py:282
  58.4 1.4 %collective-permute-start.18 = (f32[264,128]{1,0:T(8,128)S(1)}, f32[264,128]{1,0:T(8,128)S(1)}, u32[]{:S(2)}, u32[]{:S(2)}) collective-permute-start(f32[264,128]{1,0:T(8,128)S(1)} %add_add_fusion.refs_0_), channel_id=1, source_target_pairs={{0,4},{4,0},{8,12},{12,8},{16,20},{20,16},{24,28},{28,24},{1,5},{5... | collective-permute-start | bytes 405512 | tf_op jit(solution)/shard_map/ppermute | solution.py:282
  63.1 9.1 %collective-permute-start.23 = (f32[64,512]{1,0:T(8,128)S(1)}, f32[64,512]{1,0:T(8,128)S(1)}, u32[]{:S(2)}, u32[]{:S(2)}) collective-permute-start(f32[64,512]{1,0:T(8,128)S(1)} %get-tuple-element.64), channel_id=1, source_target_pairs={{0,1},{1,0},{2,3},{3,2},{4,5},{5,4},{6,7},{7,6},{8,9},{9,8},{10,11... | collective-permute-start | bytes 393224 | tf_op jit(solution)/shard_map/ppermute | solution.py:282
  63.7 1.2 %collective-permute-start.19 = (f32[16,128]{1,0:T(8,128)S(1)}, f32[16,128]{1,0:T(8,128)S(1)}, u32[]{:S(2)}, u32[]{:S(2)}) collective-permute-start(f32[16,128]{1,0:T(8,128)S(1)} %get-tuple-element.60), channel_id=1, source_target_pairs={{0,4},{4,0},{8,12},{12,8},{16,20},{20,16},{24,28},{28,24},{1,5},{5... | collective-permute-start | bytes 24584 | tf_op jit(solution)/shard_map/ppermute | solution.py:282
  64.8 5.6 %collective-permute-start.22 = (f32[16,128]{1,0:T(8,128)S(1)}, f32[16,128]{1,0:T(8,128)S(1)}, u32[]{:S(2)}, u32[]{:S(2)}) collective-permute-start(f32[16,128]{1,0:T(8,128)S(1)} %add.53), channel_id=1, source_target_pairs={{0,24},{4,28},{8,16},{12,20},{16,8},{20,12},{24,0},{28,4},{1,25},{... | collective-permute-start | bytes 24584 | tf_op jit(solution)/shard_map/ppermute | solution.py:282
  67.1 5.1 %collective-permute-start.21 = (f32[16,128]{1,0:T(8,128)S(1)}, f32[16,128]{1,0:T(8,128)S(1)}, u32[]{:S(2)}, u32[]{:S(2)}) collective-permute-start(f32[16,128]{1,0:T(8,128)S(1)} %add.53), channel_id=1, source_target_pairs={{0,16},{4,20},{8,24},{12,28},{16,0},{20,4},{24,8},{28,12},{1,17},{... | collective-permute-start | bytes 24584 | tf_op jit(solution)/shard_map/ppermute | solution.py:282
  67.1 5.1 %collective-permute-start.20 = (f32[16,128]{1,0:T(8,128)S(1)}, f32[16,128]{1,0:T(8,128)S(1)}, u32[]{:S(2)}, u32[]{:S(2)}) collective-permute-start(f32[16,128]{1,0:T(8,128)S(1)} %add.53), channel_id=1, source_target_pairs={{0,8},{4,12},{8,0},{12,4},{16,24},{20,28},{24,16},{28,20},{1,9},{5... | collective-permute-start | bytes 24584 | tf_op jit(solution)/shard_map/ppermute | solution.py:282
  69.2 8.0 %collective-permute-start.24 = (f32[64,512]{1,0:T(8,128)S(1)}, f32[64,512]{1,0:T(8,128)S(1)}, u32[]{:S(2)}, u32[]{:S(2)}) collective-permute-start(f32[64,512]{1,0:T(8,128)S(1)} %get-tuple-element.66), channel_id=1, source_target_pairs={{0,2},{1,3},{2,0},{3,1},{4,6},{5,7},{6,4},{7,5},{8,10},{9,11},{10,... | collective-permute-start | bytes 393224 | tf_op jit(solution)/shard_map/ppermute | solution.py:282
  70.4 6.8 %collective-permute-start.25 = (f32[64,512]{1,0:T(8,128)S(1)}, f32[64,512]{1,0:T(8,128)S(1)}, u32[]{:S(2)}, u32[]{:S(2)}) collective-permute-start(f32[64,512]{1,0:T(8,128)S(1)} %get-tuple-element.67), channel_id=1, source_target_pairs={{0,3},{1,2},{2,1},{3,0},{4,7},{5,6},{6,5},{7,4},{8,11},{9,10},{10,... | collective-permute-start | bytes 393224 | tf_op jit(solution)/shard_map/ppermute | solution.py:282
  72.2 6.5 %collective-permute-start.28 = (f32[16,128]{1,0:T(8,128)S(1)}, f32[16,128]{1,0:T(8,128)S(1)}, u32[]{:S(2)}, u32[]{:S(2)}) collective-permute-start(f32[16,128]{1,0:T(8,128)S(1)} %add_add_fusion.2), channel_id=1, source_target_pairs={{0,3},{1,2},{2,1},{3,0},{4,7},{5,6},{6,5},{7,4},{8,11},{9,10},{10,... | collective-permute-start | bytes 24584 | tf_op jit(solution)/shard_map/ppermute | solution.py:282
  73.4 5.3 %collective-permute-start.27 = (f32[16,128]{1,0:T(8,128)S(1)}, f32[16,128]{1,0:T(8,128)S(1)}, u32[]{:S(2)}, u32[]{:S(2)}) collective-permute-start(f32[16,128]{1,0:T(8,128)S(1)} %add_add_fusion.2), channel_id=1, source_target_pairs={{0,2},{1,3},{2,0},{3,1},{4,6},{5,7},{6,4},{7,5},{8,10},{9,11},{10,... | collective-permute-start | bytes 24584 | tf_op jit(solution)/shard_map/ppermute | solution.py:282
  74.6 4.1 %collective-permute-start.26 = (f32[16,128]{1,0:T(8,128)S(1)}, f32[16,128]{1,0:T(8,128)S(1)}, u32[]{:S(2)}, u32[]{:S(2)}) collective-permute-start(f32[16,128]{1,0:T(8,128)S(1)} %add_add_fusion.2), channel_id=1, source_target_pairs={{0,1},{1,0},{2,3},{3,2},{4,5},{5,4},{6,7},{7,6},{8,9},{9,8},{10,11... | collective-permute-start | bytes 24584 | tf_op jit(solution)/shard_map/ppermute | solution.py:282
